TPU v7x, 256 devices: a whole 4x4x8 slice. The times are simulated.
256 devices in a mesh: wide: 32 (over x, y, z_hi), narrow: 8 (over z_lo, core).
Axes of the slice: x: 4, y: 4, z: 8 (z_hi: 2, z_lo: 4; z = z_hi * 4 + z_lo), core: 2. Of those that a mesh axis runs over, the one named last changes fastest.
Arguments:
- tokens: bfloat16 [2, 256, 9216], P(None, None, 'narrow'), may hold values from -6 to 6
- gate_weight: bfloat16 [36864, 9216], P(('wide', 'narrow')), may hold values from -0.0625 to 0.0625
- up_weight: bfloat16 [36864, 9216], P(('wide', 'narrow')), may hold values from -0.0625 to 0.0625
- down_weight: bfloat16 [36864, 9216], P('wide', 'narrow'), may hold values from -0.03125 to 0.03125
Outputs:
- mixed: bfloat16 [2, 256, 9216], P(None, 'wide', 'narrow')
All inputs are finite; a program needn't handle non-finite values.
Results may differ from a plain program's by a relative error of at most 0.0049.
Values may be sent and summed in bfloat16 or wider, within the bound.
No kernel may reach another device: no remote copies, remote signals or barrier semaphores. Data moves between devices by JAX's collectives and lax.ppermute only.
A program may use at most 64 MiB of HBM per device.

v0:
```python
import jax
import jax.numpy as jnp
from jax import lax
from jax.sharding import PartitionSpec as P


def local(tokens, gate_weight, up_weight, down_weight):
    units = gate_weight.shape[0]
    batches, count_rows = (tokens.shape[0], tokens.shape[1])
    piece = lax.all_gather(tokens, "narrow", axis=2, tiled=True)
    width = piece.shape[-1]
    flat_rows = piece.reshape(-1, width)
    gate_part = jnp.einsum("bk,fk->bf", flat_rows, gate_weight, preferred_element_type=jnp.float32)
    up_part = jnp.einsum("bk,fk->bf", flat_rows, up_weight, preferred_element_type=jnp.float32)
    hidden = (
        (jax.nn.silu(gate_part) * up_part).astype(jnp.bfloat16).reshape(batches, count_rows, units)
    )
    hidden_all = lax.all_gather(hidden, "narrow", axis=2, tiled=True)
    summed = lax.psum_scatter(
        jnp.einsum("brf,fd->rbd", hidden_all, down_weight, preferred_element_type=jnp.float32),
        "wide",
        scatter_dimension=0,
        tiled=True,
    )
    return jnp.transpose(summed, (1, 0, 2)).astype(jnp.bfloat16)


def solution(mesh):
    return jax.shard_map(
        local,
        mesh=mesh,
        in_specs=(
            P(None, None, "narrow"),
            P(("wide", "narrow"), None),
            P(("wide", "narrow"), None),
            P("wide", "narrow"),
        ),
        out_specs=P(None, "wide", "narrow"),
        check_vma=False,
    )
```

profile of v0, /device:TPU:1, one launch (start us, length us, event | category | flops | bytes accessed | tf_op | source)
XLA Modules:
  0.0 433.6 jit_solution(9380924694865850173)
XLA Ops:
  6.5 0.0 copy-start
  6.5 0.0 all-gather.3.cloned.1.call-start
  6.5 0.7 all-gather.3.cloned.1.call-update
  7.3 0.0 all-gather.5.cloned.1.call-start
  7.3 107.2 %all-gather.3.cloned.1.call-done = bf16[2,256,9216]{2,1,0:T(8,128)(2,1)} async-done(((bf16[2,256,1152]{2,1,0:T(8,128)(2,1)}), bf16[2,256,9216]{2,1,0:T(8,128)(2,1)}) %all-gather.3.cloned.1.call-update) | async-done | bytes 9437200 | tf_op jit(solution)/shard_map/all_gather | solution.py:10
  114.5 0.0 copy-start.1
  114.5 0.0 copy-start.2
  114.5 7.9 %fusion.2 = f32[512,144]{0,1:T(8,128)S(1)} fusion(bf16[512,9216]{1,0:T(8,128)(2,1)} %bitcast.19, bf16[144,9216]{1,0:T(8,128)(2,1)} %param.5), kind=kOutput, calls=%fused_computation.6 | convolution fusion | flops 1358954496 | bytes 12386304 | tf_op jit(solution)/shard_map/bk,fk->bf/dot_general | solution.py:13
  122.3 0.0 copy-done.1
  122.4 0.0 copy-done.2
  122.4 3.3 fusion.1
  125.7 0.7 copy.8
  126.3 0.0 all-gather.5.cloned.1.call-update
  126.3 0.0 reduce-scatter.2.cloned.1.call-start
  126.4 35.9 %all-gather.5.cloned.1.call-done = bf16[2,256,1152]{1,2,0:T(8,128)(2,1)} async-done(((bf16[2,256,144]{1,2,0:T(8,128)(2,1)}), bf16[2,256,1152]{1,2,0:T(8,128)(2,1)}) %all-gather.5.cloned.1.call-update) | async-done | bytes 1179664 | tf_op jit(solution)/shard_map/all_gather | solution.py:18
  162.3 0.0 copy-done
  162.3 4.5 %convolution_bitcast_fusion = f32[256,2,1152]{2,0,1:T(8,128)} fusion(bf16[2,256,1152]{1,2,0:T(8,128)(2,1)} %all-gather.5.cloned.1.call-done, bf16[1152,1152]{1,0:T(8,128)(2,1)S(1)} %copy-done), kind=kOutput, calls=%fused_computation | convolution fusion | flops 1358954496 | bytes 6193152 | tf_op jit(solution)/shard_map/brf,fd->rbd/dot_general | solution.py:20
  166.8 0.0 reduce-scatter.2.cloned.1.call-update
  166.8 258.7 %reduce-scatter.2.cloned.1.call-done = f32[8,2,1152]{2,0,1:T(8,128)} async-done(((f32[256,2,1152]{2,0,1:T(8,128)}), f32[8,2,1152]{2,0,1:T(8,128)}) %reduce-scatter.2.cloned.1.call-update) | async-done | bytes 73744 | tf_op jit(solution)/shard_map/reduce_scatter | solution.py:19
  425.6 1.5 convert_bitcast_fusion
Async XLA Ops:
  6.5 155.7 %copy-start = (bf16[1152,1152]{1,0:T(8,128)(2,1)S(1)}, bf16[1152,1152]{1,0:T(8,128)(2,1)}, u32[]{:S(2)}) copy-start(bf16[1152,1152]{1,0:T(8,128)(2,1)} %param.7) | copy-start | bytes 7962628
  6.5 107.9 %all-gather.3.cloned.1.call-start = ((), (), s32[]{:S(2)}) async-start(), calls=%async_computation.1 | async-start | bytes 10616832 | tf_op jit(solution)/shard_map/all_gather | solution.py:10
  7.3 155.0 %all-gather.5.cloned.1.call-start = ((), (), s32[]{:S(2)}) async-start(), calls=%async_computation.2 | async-start | bytes 1327104 | tf_op jit(solution)/shard_map/all_gather | solution.py:18
  114.5 7.9 %copy-start.1 = (bf16[2,256,9216]{2,1,0:T(8,128)(2,1)S(1)}, bf16[2,256,9216]{2,1,0:T(8,128)(2,1)}, u32[]{:S(2)}) copy-start(bf16[2,256,9216]{2,1,0:T(8,128)(2,1)} %all-gather.3.cloned.1.call-done) | copy-start | bytes 28311556
  114.5 7.9 %copy-start.2 = (bf16[144,9216]{1,0:T(8,128)(2,1)S(1)}, bf16[144,9216]{1,0:T(8,128)(2,1)}, u32[]{:S(2)}) copy-start(bf16[144,9216]{1,0:T(8,128)(2,1)} %param.6) | copy-start | bytes 7962628
  126.3 299.2 %reduce-scatter.2.cloned.1.call-start = ((), (), s32[]{:S(2)}) async-start(), calls=%async_computation.3 | async-start | bytes 2433024 | tf_op jit(solution)/shard_map/reduce_scatter | solution.py:19
Sparse Core Ops, SparseCore 0:
  9.2 105.2 all-gather.2
  126.5 35.7 all-gather.4
  167.6 257.9 reduce-scatter.1
where the time goes:
time: 434 us
  waiting for transfers between devices  403 us (93%)
  matrix products  15.7 us (4%)
  between operations  13.1 us (3%)
    reduce_scatter x1, waiting for transfers between devices, local(): lax.psum_scatter(jnp.einsum('brf,fd->rbd', hidden_all, down_weight, prefe...  259 us
    all_gather x1, waiting for transfers between devices, local(): piece = lax.all_gather(tokens, 'narrow', axis=2, tiled=True)  107 us
    all_gather x1, waiting for transfers between devices, local(): hidden_all = lax.all_gather(hidden, 'narrow', axis=2, tiled=True)  35.9 us
  transfers between devices with their start and end apart: 3, of which 3 were waited for; matrix products, arithmetic and copies ran while one was open for 0% of the time, Pallas kernels for 0%

commit v1 on v0

v1 whole, which is shorter than its diff:
```python
import jax
import jax.numpy as jnp
import numpy as np
from jax import lax
from jax.sharding import Mesh, PartitionSpec as P

AXES = ("x", "y", "h", "l", "c")
SIZES = (4, 4, 2, 4, 2)
F32 = jnp.float32
BF16 = jnp.bfloat16


def _perm(move):
    pairs = []
    for source in range(256):
        x, y, h, l, c = (int(i) for i in np.unravel_index(source, SIZES))
        X, Y, Z, C = move(x, y, h * 4 + l, c)
        Z %= 8
        pairs.append((source, int(np.ravel_multi_index((X % 4, Y % 4, Z // 4, Z % 4, C % 2), SIZES))))
    return pairs


def _permute(a, move):
    return lax.ppermute(a, AXES, _perm(move))


def _first(k):
    return lambda x, y, z, c: (x + k, y, z, c) if c == 0 else (x, y + k, z, c)


def _second(k):
    return lambda x, y, z, c: (x, y + k, z, c) if c == 0 else (x + k, y, z, c)


def _swap(x, y, z, c):
    return (x, y, z, 1 - c)


def _z(k):
    return lambda x, y, z, c: (x, y, z + k, c)


def _z_two(x, y, z, c):
    return (x, y, z + 2 if c == 0 else z - 2, c)


def _lo(k):
    return lambda x, y, z, c: (x, y, (z // 4) * 4 + (z % 4 + k) % 4, c)


def local(tokens, gate_weight, up_weight, down_weight):
    x, y, h, l, c = (lax.axis_index(a) for a in AXES)
    core0 = c == 0
    width = tokens.shape[-1]
    units = gate_weight.shape[0]

    gate_other = _permute(gate_weight, _swap)
    up_other = _permute(up_weight, _swap)

    t0 = tokens[0]
    t1 = tokens[1].reshape(4, 4, 16, width).transpose(1, 0, 2, 3).reshape(256, width)
    mine = jnp.where(core0, t0, t1)
    theirs = jnp.where(core0, t1, t0)
    other = _permute(theirs, _swap)
    own = jnp.concatenate([jnp.where(core0, mine, other), jnp.where(core0, other, mine)], axis=1)

    q = jnp.where(core0, x + 2 * y, 2 * x + y) % 4
    own2 = jnp.concatenate([own, own], axis=0)
    own = lax.dynamic_slice_in_dim(own2, q * 64, 256, axis=0)
    quarter = own[:64]

    from_up = _permute(quarter, _z(-1))
    from_down = _permute(quarter, _z(1))
    from_two = _permute(quarter, _z_two)
    down_other = _permute(down_weight, _swap)

    bundle = jnp.concatenate([from_up, from_two, from_down], axis=1)
    next1 = _permute(bundle, _first(-1))
    next3 = _permute(bundle, _first(1))
    next2a = _permute(bundle[:32], _second(-1))
    next2b = _permute(bundle[32:], _second(1))
    rest = jnp.concatenate([bundle, next1, next2a, next2b, next3], axis=0)

    w = jnp.concatenate(
        [
            jnp.where(core0, gate_weight, gate_other),
            jnp.where(core0, gate_other, gate_weight),
            jnp.where(core0, up_weight, up_other),
            jnp.where(core0, up_other, up_weight),
        ],
        axis=0,
    )
    block = 2 * width
    w2 = jnp.concatenate([w, w], axis=1)
    w = lax.dynamic_slice_in_dim(w2, l * block, 4 * block, axis=1)

    both = jnp.einsum("bk,fk->bf", own, w[:, :block], preferred_element_type=F32)
    both = both + jnp.einsum("bk,fk->bf", rest, w[:, block:], preferred_element_type=F32)
    gate, up = both[:, : 2 * units], both[:, 2 * units :]
    hidden = (jax.nn.silu(gate) * up).astype(BF16)

    hs = [hidden] + [_permute(hidden, _lo(-k)) for k in (1, 2, 3)]
    dw = jnp.concatenate([down_weight, down_other], axis=1)
    dw = lax.dynamic_slice_in_dim(jnp.concatenate([dw, dw], axis=0), l * 2 * units, 8 * units, axis=0)
    part = jnp.einsum("bf,fd->bd", jnp.concatenate(hs, axis=1), dw, preferred_element_type=F32)

    p = jnp.where(core0, y, x) % 2
    part = part.reshape(4, 64, 2 * width)

    def to(k):
        return lax.dynamic_index_in_dim(part, (k + 2 * p) % 4, 0, keepdims=False)

    stage = to(0)
    got = [_permute(to(k).astype(BF16), _first(k)) for k in (1, 3, 2)]
    for g in got:
        stage = stage + g.astype(F32)
    stage = stage.reshape(4, 16, 2 * width)
    s2 = jnp.where(core0, y, x)

    def to2(k):
        return lax.dynamic_index_in_dim(stage, (s2 + k) % 4, 0, keepdims=False)

    last = to2(0)
    got = [_permute(to2(k).astype(BF16), _second(k)) for k in (1, 3, 2)]
    for g in got:
        last = last + g.astype(F32)
    last = last.reshape(2, 8, 2 * width)
    here = lax.dynamic_index_in_dim(last, h, 0, keepdims=False)
    there = lax.dynamic_index_in_dim(last, 1 - h, 0, keepdims=False)
    a = _permute(there[:, :width], _z(4))
    b = _permute(here[:, width:], _swap)
    d = _permute(there[:, width:], lambda x, y, z, c: (x, y, z + 4, 1 - c))
    same = (here[:, :width] + a).astype(BF16)
    cross = (b + d).astype(BF16)
    return jnp.stack([jnp.where(core0, same, cross), jnp.where(core0, cross, same)])


def solution(mesh):
    fine = Mesh(mesh.devices.reshape(SIZES), AXES)
    wide, narrow = ("x", "y", "h"), ("l", "c")
    return jax.shard_map(
        local,
        mesh=fine,
        in_specs=(
            P(None, None, narrow),
            P(wide + narrow, None),
            P(wide + narrow, None),
            P(wide, narrow),
        ),
        out_specs=P(None, wide, narrow),
        check_vma=False,
    )
```

time: 434 us -> 180 us (0.41)
  waiting for transfers between devices: 403 us -> 59.4 us
  other arithmetic: 1.5 us -> 57.6 us
  starting transfers between devices: 0.08 us -> 46 us
  between operations: 13.1 us -> 0.26 us
    reduce_scatter x1 -> x0, waiting for transfers between devices: 259 us -> none  [local(): lax.psum_scatter(jnp.einsum('brf,fd->rbd', hidden_all, down_weight, prefe...]
    all_gather x2 -> x0, waiting for transfers between devices: 143 us -> none  [the longest x1 107 us: local(): piece = lax.all_gather(tokens, 'narrow', axis=2, tiled=True)]
    ppermute x0 -> x23, waiting for transfers between devices: none -> 59.4 us  [_permute(): return lax.ppermute(a, AXES, _perm(move))]
    concatenate x0 -> x2, other arithmetic: none -> 47.2 us  [the longest x1 42.4 us: local(): w2 = jnp.concatenate([w, w], axis=1)]
    ppermute x0 -> x23, starting transfers between devices: none -> 46 us  [_permute(): return lax.ppermute(a, AXES, _perm(move))]
    select_n x0 -> x4, other arithmetic: none -> 8.52 us  [the longest x1 2.9 us: local(): jnp.where(core0, up_other, up_weight)]
  transfers between devices with their start and end apart: 3 -> 23, of which waited for: 3 -> 14; matrix products, arithmetic and copies ran while one was open for 0% -> 29% of each run, Pallas kernels for 0% -> 0%
where the time goes in v1:
time: 180 us; the launch traced here: 178 us
  waiting for transfers between devices  59.4 us (33%)
  other arithmetic  57.6 us (32%)
  starting transfers between devices  46 us (26%)
  matrix products  11.8 us (7%)
  local copies, waits for them, and re-layouts  3.48 us (2%)
    ppermute x23, waiting for transfers between devices, _permute(): return lax.ppermute(a, AXES, _perm(move))  59.4 us
    ppermute x23, starting transfers between devices, _permute(): return lax.ppermute(a, AXES, _perm(move))  46 us
    concatenate x1, other arithmetic, local(): w2 = jnp.concatenate([w, w], axis=1)  42.4 us
    dot_general x1, matrix products, local(): jnp.einsum('bf,fd->bd', jnp.concatenate(hs, axis=1), dw, preferred_elemen...  8.62 us
    concatenate x1, other arithmetic, local(): own2 = jnp.concatenate([own, own], axis=0)  4.81 us
  transfers between devices with their start and end apart: 23, of which 14 were waited for; matrix products, arithmetic and copies ran while one was open for 29% of the time, Pallas kernels for 0%

profile of v1, /device:TPU:1, one launch (start us, length us, event | category | flops | bytes accessed | tf_op | source)
XLA Modules:
  0.0 178.5 jit_solution(125584151378221130)
XLA Ops:
  0.0 1.1 slice.40
  1.2 0.0 copy-start
  1.2 2.1 %bitcast_select_fusion = bf16[256,1152]{1,0:T(8,128)(2,1)} fusion(bf16[4,4,16,1152]{3,2,1,0:T(8,128)(2,1)S(1)} %copy.5, pred[]{:T(512)S(6)} %eq.14, bf16[2,256,1152]{2,1,0:T(8,128)(2,1)} %param.4), kind=kLoop, calls=%fused_computation.49 | loop fusion | flops 294912 | bytes 1769473 | tf_op jit(solution)/shard_map/jit(_where)/select_n | solution.py:63
  3.3 3.2 %collective-permute-start = (bf16[256,1152]{1,0:T(8,128)(2,1)}, bf16[256,1152]{1,0:T(8,128)(2,1)}, u32[]{:S(2)}, u32[]{:S(2)}) collective-permute-start(bf16[256,1152]{1,0:T(8,128)(2,1)} %bitcast_select_fusion), channel_id=1, source_target_pairs={{0,1},{1,0},{2,3},{3,2},{4,5},{5,4},{6,7},{7,6},{8,9},{9,8},{10,11... | collective-permute-start | bytes 1769480 | tf_op jit(solution)/shard_map/ppermute | solution.py:24
  6.6 2.0 %collective-permute-done = bf16[256,1152]{1,0:T(8,128)(2,1)} collective-permute-done((bf16[256,1152]{1,0:T(8,128)(2,1)}, bf16[256,1152]{1,0:T(8,128)(2,1)}, u32[]{:S(2)}, u32[]{:S(2)}) %collective-permute-start) | collective-permute-done | bytes 589856 | tf_op jit(solution)/shard_map/ppermute | solution.py:24
  8.5 1.4 broadcast_select_fusion.4
  9.9 4.8 %fusion.20 = bf16[256,2304]{1,0:T(8,128)(2,1)S(1)} fusion(s32[]{:T(128)S(6)} %select_n.152, bf16[256,1152]{1,0:T(8,128)(2,1)S(1)} %get-tuple-element.16, bf16[256,1152]{1,0:T(8,128)(2,1)S(1)} %get-tuple-element.15), kind=kLoop, calls=%fused_computation.37 | loop fusion | flops 4718592 | bytes 2359300 | tf_op jit(solution)/shard_map/concatenate | solution.py:68
  14.8 1.1 copy-done.1
  15.8 3.8 %collective-permute-start.3 = (bf16[64,2304]{1,0:T(8,128)(2,1)S(1)}, bf16[64,2304]{1,0:T(8,128)(2,1)S(1)}, u32[]{:S(2)}, u32[]{:S(2)}) collective-permute-start(bf16[64,2304]{1,0:T(8,128)(2,1)S(1)} %slice.53), channel_id=1, source_target_pairs={{0,14},{1,15},{2,0},{3,1},{4,2},{5,3},{6,4},{7,5},{8,6},{9,7},{10,... | collective-permute-start | bytes 884744 | tf_op jit(solution)/shard_map/ppermute | solution.py:24
  19.7 0.7 collective-permute-start.1
  20.3 0.0 collective-permute-start.2
  20.3 0.5 collective-permute-start.13
  20.8 0.0 collective-permute-start.5
  20.9 4.9 %collective-permute-done.3 = bf16[64,2304]{1,0:T(8,128)(2,1)S(1)} collective-permute-done((bf16[64,2304]{1,0:T(8,128)(2,1)S(1)}, bf16[64,2304]{1,0:T(8,128)(2,1)S(1)}, u32[]{:S(2)}, u32[]{:S(2)}) %collective-permute-start.3) | collective-permute-done | bytes 294944 | tf_op jit(solution)/shard_map/ppermute | solution.py:24
  25.7 2.6 %collective-permute-start.4 = (bf16[64,2304]{1,0:T(8,128)(2,1)S(1)}, bf16[64,2304]{1,0:T(8,128)(2,1)S(1)}, u32[]{:S(2)}, u32[]{:S(2)}) collective-permute-start(bf16[64,2304]{1,0:T(8,128)(2,1)S(1)} %slice.53), channel_id=1, source_target_pairs={{0,4},{1,13},{2,6},{3,15},{4,8},{5,1},{6,10},{7,3},{8,12},{9,5},{1... | collective-permute-start | bytes 884744 | tf_op jit(solution)/shard_map/ppermute | solution.py:24
  28.4 6.9 %collective-permute-done.4 = bf16[64,2304]{1,0:T(8,128)(2,1)S(1)} collective-permute-done((bf16[64,2304]{1,0:T(8,128)(2,1)S(1)}, bf16[64,2304]{1,0:T(8,128)(2,1)S(1)}, u32[]{:S(2)}, u32[]{:S(2)}) %collective-permute-start.4) | collective-permute-done | bytes 294944 | tf_op jit(solution)/shard_map/ppermute | solution.py:24
  35.3 0.0 collective-permute-done.5
  35.4 1.4 collective-permute-start.9
  36.8 1.5 collective-permute-start.6
  38.3 0.1 fusion.45
  38.4 10.6 %collective-permute-done.6 = bf16[64,6912]{1,0:T(8,128)(2,1)S(1)} collective-permute-done((bf16[64,6912]{1,0:T(8,128)(2,1)S(1)}, bf16[64,6912]{1,0:T(8,128)(2,1)S(1)}, u32[]{:S(2)}, u32[]{:S(2)}) %collective-permute-start.6) | collective-permute-done | bytes 884768 | tf_op jit(solution)/shard_map/ppermute | solution.py:24
  49.0 2.5 %collective-permute-start.7 = (bf16[32,6912]{1,0:T(8,128)(2,1)S(1)}, bf16[32,6912]{1,0:T(8,128)(2,1)S(1)}, u32[]{:S(2)}, u32[]{:S(2)}) collective-permute-start(bf16[32,6912]{1,0:T(8,128)(2,1)S(1)} %get-tuple-element.18), channel_id=1, source_target_pairs={{0,48},{1,193},{2,50},{3,195},{4,52},{5,197},{6,54},{7,199},{8,56}... | collective-permute-start | bytes 1327112 | tf_op jit(solution)/shard_map/ppermute | solution.py:24
  51.4 0.1 constant_dynamic-update-slice_fusion.6
  51.5 5.2 %collective-permute-done.7 = bf16[32,6912]{1,0:T(8,128)(2,1)S(1)} collective-permute-done((bf16[32,6912]{1,0:T(8,128)(2,1)S(1)}, bf16[32,6912]{1,0:T(8,128)(2,1)S(1)}, u32[]{:S(2)}, u32[]{:S(2)}) %collective-permute-start.7) | collective-permute-done | bytes 442400 | tf_op jit(solution)/shard_map/ppermute | solution.py:24
  56.7 0.9 collective-permute-start.8
  57.7 8.1 %collective-permute-done.8 = bf16[32,6912]{1,0:T(8,128)(2,1)S(1)} collective-permute-done((bf16[32,6912]{1,0:T(8,128)(2,1)S(1)}, bf16[32,6912]{1,0:T(8,128)(2,1)S(1)}, u32[]{:S(2)}, u32[]{:S(2)}) %collective-permute-start.8) | collective-permute-done | bytes 442400 | tf_op jit(solution)/shard_map/ppermute | solution.py:24
  65.8 0.0 collective-permute-done.9
  65.8 0.1 constant_dynamic-update-slice_fusion.3
  65.9 0.0 collective-permute-done.1
  65.9 2.1 %broadcast_select_fusion.2 = (bf16[144,9216]{1,0:T(8,128)(2,1)S(1)}, bf16[144,9216]{1,0:T(8,128)(2,1)S(1)}) fusion(bf16[144,9216]{1,0:T(8,128)(2,1)} %collective-permute-done.1, bf16[144,9216]{1,0:T(8,128)(2,1)S(1)} %copy-done, pred[]{:T(512)S(6)} %eq.14), kind=kLoop, calls=%fused_computation.29 | loop fusion | flops 2654208 | bytes 10616833 | tf_op jit(solution)/shard_map/jit(_where)/select_n | solution.py:87
  68.0 0.0 collective-permute-done.2
  68.0 2.9 %broadcast_select_fusion = (bf16[144,9216]{1,0:T(8,128)(2,1)S(1)}, bf16[144,9216]{1,0:T(8,128)(2,1)S(1)}) fusion(bf16[144,9216]{1,0:T(8,128)(2,1)} %collective-permute-done.2, bf16[144,9216]{1,0:T(8,128)(2,1)} %param.6, pred[]{:T(512)S(6)} %eq.14), kind=kLoop, calls=%fused_computation.27 | loop fusion | flops 2654208 | bytes 10616833 | tf_op jit(solution)/shard_map/jit(_where)/select_n | solution.py:89
  70.9 42.4 %fusion.3 = bf16[576,9216]{1,0:T(8,128)(2,1)S(1)} fusion(s32[]{:T(128)S(6)} %select_n.158, bf16[144,9216]{1,0:T(8,128)(2,1)S(1)} %get-tuple-element.11, bf16[144,9216]{1,0:T(8,128)(2,1)S(1)} %get-tuple-element.10, bf16[144,9216]{1,0:T(8,128)(2,1)S(1)} %get-tuple-element.9, bf16[144,9216]{1,0:T(8,128)(2,1)S(1)} %get-tuple-element.8), kind=kLoop, calls=%fused_computation.11 | loop fusion | flops 84934656 | bytes 21233668 | tf_op jit(solution)/shard_map/concatenate | solution.py:94
  113.3 2.2 %fusion.7 = f32[256,576]{0,1:T(8,128)S(1)} fusion(bf16[256,6912]{1,0:T(8,128)(2,1)S(1)} %constant_dynamic-update-slice_fusion.3, bf16[576,9216]{1,0:T(8,128)(2,1)S(1)} %fusion.3), kind=kOutput, calls=%fused_computation.19 | convolution fusion | flops 2038431744 | bytes 12091392 | tf_op jit(solution)/shard_map/bk,fk->bf/dot_general | solution.py:98
  115.6 0.9 fusion.16
  116.5 0.1 fusion.34
  116.6 1.1 collective-permute-start.12
  117.7 2.9 %collective-permute-start.11 = (bf16[256,288]{0,1:T(8,128)(2,1)S(1)}, bf16[256,288]{0,1:T(8,128)(2,1)S(1)}, u32[]{:S(2)}, u32[]{:S(2)}) collective-permute-start(bf16[256,288]{0,1:T(8,128)(2,1)S(1)} %fusion.34), channel_id=1, source_target_pairs={{0,4},{1,5},{2,6},{3,7},{4,0},{5,1},{6,2},{7,3},{8,12},{9,13},{10,... | collective-permute-start | bytes 442376 | tf_op jit(solution)/shard_map/ppermute | solution.py:24
  120.6 0.1 collective-permute-start.10
  120.7 0.0 collective-permute-done.13
  120.7 2.2 %collective-permute-done.12 = bf16[256,288]{0,1:T(8,128)(2,1)S(1)} collective-permute-done((bf16[256,288]{0,1:T(8,128)(2,1)S(1)}, bf16[256,288]{0,1:T(8,128)(2,1)S(1)}, u32[]{:S(2)}, u32[]{:S(2)}) %collective-permute-start.12) | collective-permute-done | bytes 147488 | tf_op jit(solution)/shard_map/ppermute | solution.py:24
  122.9 3.8 %collective-permute-done.11 = bf16[256,288]{0,1:T(8,128)(2,1)S(1)} collective-permute-done((bf16[256,288]{0,1:T(8,128)(2,1)S(1)}, bf16[256,288]{0,1:T(8,128)(2,1)S(1)}, u32[]{:S(2)}, u32[]{:S(2)}) %collective-permute-start.11) | collective-permute-done | bytes 147488 | tf_op jit(solution)/shard_map/ppermute | solution.py:24
  126.7 0.0 collective-permute-done.10
  126.7 8.6 %fusion.12 = f32[256,2304]{1,0:T(8,128)S(1)} fusion(s32[]{:T(128)S(6)} %select_n.159, bf16[1152,1152]{1,0:T(8,128)(2,1)} %param.7, bf16[1152,1152]{1,0:T(8,128)(2,1)} %collective-permute-done.13, bf16[256,288]{0,1:T(8,128)(2,1)S(1)} %collective-permute-done.12, bf16[256,288]{0,1:T(8,128)(2,1)S(1)} %collective-permute-done.11, ...), kind=kOutput, calls=%fused_computation.24 | convolution fusion | flops 1382547456 | bytes 8257540 | tf_op jit(solution)/shard_map/bf,fd->bd/dot_general | solution.py:105
  135.4 0.8 fusion.31
  136.2 3.9 %collective-permute-start.14 = (bf16[64,2304]{1,0:T(8,128)(2,1)}, bf16[64,2304]{1,0:T(8,128)(2,1)S(1)}, u32[]{:S(2)}, u32[]{:S(2)}) collective-permute-start(bf16[64,2304]{1,0:T(8,128)(2,1)} %get-tuple-element.12), channel_id=1, source_target_pairs={{0,64},{1,17},{2,66},{3,19},{4,68},{5,21},{6,70},{7,23},{8,72},{9,... | collective-permute-start | bytes 884744 | tf_op jit(solution)/shard_map/ppermute | solution.py:24
  140.1 1.0 collective-permute-start.16
  141.1 1.4 collective-permute-start.15
  142.5 1.8 collective-permute-done.14
  144.2 4.3 %collective-permute-done.16 = bf16[64,2304]{1,0:T(8,128)(2,1)S(1)} collective-permute-done((bf16[64,2304]{1,0:T(8,128)(2,1)S(1)}, bf16[64,2304]{1,0:T(8,128)(2,1)S(1)}, u32[]{:S(2)}, u32[]{:S(2)}) %collective-permute-start.16) | collective-permute-done | bytes 294944 | tf_op jit(solution)/shard_map/ppermute | solution.py:24
  148.6 0.0 collective-permute-done.15
  148.6 1.1 fusion.30
  149.7 0.1 collective-permute-start.17
  149.8 2.0 %collective-permute-start.19 = (bf16[16,2304]{1,0:T(8,128)(2,1)S(1)}, bf16[16,2304]{1,0:T(8,128)(2,1)S(1)}, u32[]{:S(2)}, u32[]{:S(2)}) collective-permute-start(bf16[16,2304]{1,0:T(8,128)(2,1)S(1)} %get-tuple-element.20), channel_id=1, source_target_pairs={{0,32},{1,129},{2,34},{3,131},{4,36},{5,133},{6,38},{7,135},{8,40}... | collective-permute-start | bytes 221192 | tf_op jit(solution)/shard_map/ppermute | solution.py:24
  151.8 0.7 collective-permute-start.18
  152.4 2.5 %collective-permute-done.17 = bf16[16,2304]{1,0:T(8,128)(2,1)S(1)} collective-permute-done((bf16[16,2304]{1,0:T(8,128)(2,1)S(1)}, bf16[16,2304]{1,0:T(8,128)(2,1)S(1)}, u32[]{:S(2)}, u32[]{:S(2)}) %collective-permute-start.17) | collective-permute-done | bytes 73760 | tf_op jit(solution)/shard_map/ppermute | solution.py:24
  155.0 0.0 collective-permute-done.19
  155.0 0.6 collective-permute-done.18
  155.6 10.3 %collective-permute-start.21 = (f32[8,1152]{1,0:T(8,128)S(1)}, f32[8,1152]{1,0:T(8,128)S(1)}, u32[]{:S(2)}, u32[]{:S(2)}) collective-permute-start(f32[8,1152]{1,0:T(8,128)S(1)} %slice.61), channel_id=1, source_target_pairs={{0,1},{1,0},{2,3},{3,2},{4,5},{5,4},{6,7},{7,6},{8,9},{9,8},{10,11... | collective-permute-start | bytes 110600 | tf_op jit(solution)/shard_map/ppermute | solution.py:24
  165.9 5.1 %collective-permute-start.22 = (f32[8,1152]{1,0:T(8,128)S(1)}, f32[8,1152]{1,0:T(8,128)S(1)}, u32[]{:S(2)}, u32[]{:S(2)}) collective-permute-start(f32[8,1152]{1,0:T(8,128)S(1)} %get-tuple-element.30), channel_id=1, source_target_pairs={{0,9},{1,8},{2,11},{3,10},{4,13},{5,12},{6,15},{7,14},{8,1},{9,0},... | collective-permute-start | bytes 110600 | tf_op jit(solution)/shard_map/ppermute | solution.py:24
  171.0 0.3 collective-permute-start.20
  171.3 1.9 %collective-permute-done.22 = f32[8,1152]{1,0:T(8,128)S(1)} collective-permute-done((f32[8,1152]{1,0:T(8,128)S(1)}, f32[8,1152]{1,0:T(8,128)S(1)}, u32[]{:S(2)}, u32[]{:S(2)}) %collective-permute-start.22) | collective-permute-done | bytes 36896 | tf_op jit(solution)/shard_map/ppermute | solution.py:24
  173.2 4.6 %collective-permute-done.20 = f32[8,1152]{1,0:T(8,128)S(1)} collective-permute-done((f32[8,1152]{1,0:T(8,128)S(1)}, f32[8,1152]{1,0:T(8,128)S(1)}, u32[]{:S(2)}, u32[]{:S(2)}) %collective-permute-start.20) | collective-permute-done | bytes 36896 | tf_op jit(solution)/shard_map/ppermute | solution.py:24
  177.9 0.6 pad_maximum_fusion
  (19 shorter events, 0.4 us)
Async XLA Ops:
  1.2 18.5 %copy-start = (bf16[144,9216]{1,0:T(8,128)(2,1)S(1)}, bf16[144,9216]{1,0:T(8,128)(2,1)}, u32[]{:S(2)}) copy-start(bf16[144,9216]{1,0:T(8,128)(2,1)} %param.5) | copy-start | bytes 7962628
  3.3 5.2 %collective-permute-start = (bf16[256,1152]{1,0:T(8,128)(2,1)}, bf16[256,1152]{1,0:T(8,128)(2,1)}, u32[]{:S(2)}, u32[]{:S(2)}) collective-permute-start(bf16[256,1152]{1,0:T(8,128)(2,1)} %bitcast_select_fusion), channel_id=1, source_target_pairs={{0,1},{1,0},{2,3},{3,2},{4,5},{5,4},{6,7},{7,6},{8,9},{9,8},{10,11... | collective-permute-start | bytes 1769480 | tf_op jit(solution)/shard_map/ppermute | solution.py:24
  14.7 1.1 copy-start.1
  15.8 9.9 %collective-permute-start.3 = (bf16[64,2304]{1,0:T(8,128)(2,1)S(1)}, bf16[64,2304]{1,0:T(8,128)(2,1)S(1)}, u32[]{:S(2)}, u32[]{:S(2)}) collective-permute-start(bf16[64,2304]{1,0:T(8,128)(2,1)S(1)} %slice.53), channel_id=1, source_target_pairs={{0,14},{1,15},{2,0},{3,1},{4,2},{5,3},{6,4},{7,5},{8,6},{9,7},{10,... | collective-permute-start | bytes 884744 | tf_op jit(solution)/shard_map/ppermute | solution.py:24
  19.7 46.2 %collective-permute-start.1 = (bf16[144,9216]{1,0:T(8,128)(2,1)S(1)}, bf16[144,9216]{1,0:T(8,128)(2,1)}, u32[]{:S(2)}, u32[]{:S(2)}) collective-permute-start(bf16[144,9216]{1,0:T(8,128)(2,1)S(1)} %copy-done), channel_id=1, source_target_pairs={{0,1},{1,0},{2,3},{3,2},{4,5},{5,4},{6,7},{7,6},{8,9},{9,8},{10,11... | collective-permute-start | bytes 7962632 | tf_op jit(solution)/shard_map/ppermute | solution.py:24
  20.3 47.7 %collective-permute-start.2 = (bf16[144,9216]{1,0:T(8,128)(2,1)}, bf16[144,9216]{1,0:T(8,128)(2,1)}, u32[]{:S(2)}, u32[]{:S(2)}) collective-permute-start(bf16[144,9216]{1,0:T(8,128)(2,1)} %param.6), channel_id=1, source_target_pairs={{0,1},{1,0},{2,3},{3,2},{4,5},{5,4},{6,7},{7,6},{8,9},{9,8},{10,11... | collective-permute-start | bytes 7962632 | tf_op jit(solution)/shard_map/ppermute | solution.py:24
  20.3 100.4 %collective-permute-start.13 = (bf16[1152,1152]{1,0:T(8,128)(2,1)}, bf16[1152,1152]{1,0:T(8,128)(2,1)}, u32[]{:S(2)}, u32[]{:S(2)}) collective-permute-start(bf16[1152,1152]{1,0:T(8,128)(2,1)} %param.7), channel_id=1, source_target_pairs={{0,1},{1,0},{2,3},{3,2},{4,5},{5,4},{6,7},{7,6},{8,9},{9,8},{10,11... | collective-permute-start | bytes 7962632 | tf_op jit(solution)/shard_map/ppermute | solution.py:24
  20.8 14.5 %collective-permute-start.5 = (bf16[64,2304]{1,0:T(8,128)(2,1)S(1)}, bf16[64,2304]{1,0:T(8,128)(2,1)S(1)}, u32[]{:S(2)}, u32[]{:S(2)}) collective-permute-start(bf16[64,2304]{1,0:T(8,128)(2,1)S(1)} %slice.53), channel_id=1, source_target_pairs={{0,2},{1,3},{2,4},{3,5},{4,6},{5,7},{6,8},{7,9},{8,10},{9,11},{10,... | collective-permute-start | bytes 884744 | tf_op jit(solution)/shard_map/ppermute | solution.py:24
  25.7 9.6 %collective-permute-start.4 = (bf16[64,2304]{1,0:T(8,128)(2,1)S(1)}, bf16[64,2304]{1,0:T(8,128)(2,1)S(1)}, u32[]{:S(2)}, u32[]{:S(2)}) collective-permute-start(bf16[64,2304]{1,0:T(8,128)(2,1)S(1)} %slice.53), channel_id=1, source_target_pairs={{0,4},{1,13},{2,6},{3,15},{4,8},{5,1},{6,10},{7,3},{8,12},{9,5},{1... | collective-permute-start | bytes 884744 | tf_op jit(solution)/shard_map/ppermute | solution.py:24
  35.4 30.4 %collective-permute-start.9 = (bf16[64,6912]{1,0:T(8,128)(2,1)S(1)}, bf16[64,6912]{1,0:T(8,128)(2,1)S(1)}, u32[]{:S(2)}, u32[]{:S(2)}) collective-permute-start(bf16[64,6912]{1,0:T(8,128)(2,1)S(1)} %get-tuple-element.22), channel_id=1, source_target_pairs={{0,64},{1,17},{2,66},{3,19},{4,68},{5,21},{6,70},{7,23},{8,72},{9,... | collective-permute-start | bytes 2654216 | tf_op jit(solution)/shard_map/ppermute | solution.py:24
  36.8 12.2 %collective-permute-start.6 = (bf16[64,6912]{1,0:T(8,128)(2,1)S(1)}, bf16[64,6912]{1,0:T(8,128)(2,1)S(1)}, u32[]{:S(2)}, u32[]{:S(2)}) collective-permute-start(bf16[64,6912]{1,0:T(8,128)(2,1)S(1)} %get-tuple-element.22), channel_id=1, source_target_pairs={{0,192},{1,49},{2,194},{3,51},{4,196},{5,53},{6,198},{7,55},{8,200... | collective-permute-start | bytes 2654216 | tf_op jit(solution)/shard_map/ppermute | solution.py:24
  49.0 7.7 %collective-permute-start.7 = (bf16[32,6912]{1,0:T(8,128)(2,1)S(1)}, bf16[32,6912]{1,0:T(8,128)(2,1)S(1)}, u32[]{:S(2)}, u32[]{:S(2)}) collective-permute-start(bf16[32,6912]{1,0:T(8,128)(2,1)S(1)} %get-tuple-element.18), channel_id=1, source_target_pairs={{0,48},{1,193},{2,50},{3,195},{4,52},{5,197},{6,54},{7,199},{8,56}... | collective-permute-start | bytes 1327112 | tf_op jit(solution)/shard_map/ppermute | solution.py:24
  56.7 9.1 %collective-permute-start.8 = (bf16[32,6912]{1,0:T(8,128)(2,1)S(1)}, bf16[32,6912]{1,0:T(8,128)(2,1)S(1)}, u32[]{:S(2)}, u32[]{:S(2)}) collective-permute-start(bf16[32,6912]{1,0:T(8,128)(2,1)S(1)} %get-tuple-element.17), channel_id=1, source_target_pairs={{0,16},{1,65},{2,18},{3,67},{4,20},{5,69},{6,22},{7,71},{8,24},{9,... | collective-permute-start | bytes 1327112 | tf_op jit(solution)/shard_map/ppermute | solution.py:24
  113.3 2.3 %copy-start.2 = (bf16[256,2304]{1,0:T(8,128)(2,1)S(1)}, bf16[256,2304]{1,0:T(8,128)(2,1)}, u32[]{:S(2)}) copy-start(bf16[256,2304]{1,0:T(8,128)(2,1)} %copy-done.1) | copy-start | bytes 3538948
  116.6 6.3 %collective-permute-start.12 = (bf16[256,288]{0,1:T(8,128)(2,1)S(1)}, bf16[256,288]{0,1:T(8,128)(2,1)S(1)}, u32[]{:S(2)}, u32[]{:S(2)}) collective-permute-start(bf16[256,288]{0,1:T(8,128)(2,1)S(1)} %fusion.34), channel_id=1, source_target_pairs={{0,2},{1,3},{2,4},{3,5},{4,6},{5,7},{6,0},{7,1},{8,10},{9,11},{10,... | collective-permute-start | bytes 442376 | tf_op jit(solution)/shard_map/ppermute | solution.py:24
  117.7 9.1 %collective-permute-start.11 = (bf16[256,288]{0,1:T(8,128)(2,1)S(1)}, bf16[256,288]{0,1:T(8,128)(2,1)S(1)}, u32[]{:S(2)}, u32[]{:S(2)}) collective-permute-start(bf16[256,288]{0,1:T(8,128)(2,1)S(1)} %fusion.34), channel_id=1, source_target_pairs={{0,4},{1,5},{2,6},{3,7},{4,0},{5,1},{6,2},{7,3},{8,12},{9,13},{10,... | collective-permute-start | bytes 442376 | tf_op jit(solution)/shard_map/ppermute | solution.py:24
  120.6 6.1 %collective-permute-start.10 = (bf16[256,288]{0,1:T(8,128)(2,1)S(1)}, bf16[256,288]{0,1:T(8,128)(2,1)S(1)}, u32[]{:S(2)}, u32[]{:S(2)}) collective-permute-start(bf16[256,288]{0,1:T(8,128)(2,1)S(1)} %fusion.34), channel_id=1, source_target_pairs={{0,6},{1,7},{2,0},{3,1},{4,2},{5,3},{6,4},{7,5},{8,14},{9,15},{10,... | collective-permute-start | bytes 442376 | tf_op jit(solution)/shard_map/ppermute | solution.py:24
  136.2 8.0 %collective-permute-start.14 = (bf16[64,2304]{1,0:T(8,128)(2,1)}, bf16[64,2304]{1,0:T(8,128)(2,1)S(1)}, u32[]{:S(2)}, u32[]{:S(2)}) collective-permute-start(bf16[64,2304]{1,0:T(8,128)(2,1)} %get-tuple-element.12), channel_id=1, source_target_pairs={{0,64},{1,17},{2,66},{3,19},{4,68},{5,21},{6,70},{7,23},{8,72},{9,... | collective-permute-start | bytes 884744 | tf_op jit(solution)/shard_map/ppermute | solution.py:24
  140.1 8.5 %collective-permute-start.16 = (bf16[64,2304]{1,0:T(8,128)(2,1)S(1)}, bf16[64,2304]{1,0:T(8,128)(2,1)S(1)}, u32[]{:S(2)}, u32[]{:S(2)}) collective-permute-start(bf16[64,2304]{1,0:T(8,128)(2,1)S(1)} %get-tuple-element.13), channel_id=1, source_target_pairs={{0,128},{1,33},{2,130},{3,35},{4,132},{5,37},{6,134},{7,39},{8,136... | collective-permute-start | bytes 884744 | tf_op jit(solution)/shard_map/ppermute | solution.py:24
  141.1 7.5 %collective-permute-start.15 = (bf16[64,2304]{1,0:T(8,128)(2,1)S(1)}, bf16[64,2304]{1,0:T(8,128)(2,1)}, u32[]{:S(2)}, u32[]{:S(2)}) collective-permute-start(bf16[64,2304]{1,0:T(8,128)(2,1)S(1)} %get-tuple-element.14), channel_id=1, source_target_pairs={{0,192},{1,49},{2,194},{3,51},{4,196},{5,53},{6,198},{7,55},{8,200... | collective-permute-start | bytes 884744 | tf_op jit(solution)/shard_map/ppermute | solution.py:24
  149.7 5.3 %collective-permute-start.17 = (bf16[16,2304]{1,0:T(8,128)(2,1)S(1)}, bf16[16,2304]{1,0:T(8,128)(2,1)S(1)}, u32[]{:S(2)}, u32[]{:S(2)}) collective-permute-start(bf16[16,2304]{1,0:T(8,128)(2,1)S(1)} %get-tuple-element.19), channel_id=1, source_target_pairs={{0,16},{1,65},{2,18},{3,67},{4,20},{5,69},{6,22},{7,71},{8,24},{9,... | collective-permute-start | bytes 221192 | tf_op jit(solution)/shard_map/ppermute | solution.py:24
  149.8 5.2 %collective-permute-start.19 = (bf16[16,2304]{1,0:T(8,128)(2,1)S(1)}, bf16[16,2304]{1,0:T(8,128)(2,1)S(1)}, u32[]{:S(2)}, u32[]{:S(2)}) collective-permute-start(bf16[16,2304]{1,0:T(8,128)(2,1)S(1)} %get-tuple-element.20), channel_id=1, source_target_pairs={{0,32},{1,129},{2,34},{3,131},{4,36},{5,133},{6,38},{7,135},{8,40}... | collective-permute-start | bytes 221192 | tf_op jit(solution)/shard_map/ppermute | solution.py:24
  151.8 3.8 %collective-permute-start.18 = (bf16[16,2304]{1,0:T(8,128)(2,1)S(1)}, bf16[16,2304]{1,0:T(8,128)(2,1)S(1)}, u32[]{:S(2)}, u32[]{:S(2)}) collective-permute-start(bf16[16,2304]{1,0:T(8,128)(2,1)S(1)} %get-tuple-element.21), channel_id=1, source_target_pairs={{0,48},{1,193},{2,50},{3,195},{4,52},{5,197},{6,54},{7,199},{8,56}... | collective-permute-start | bytes 221192 | tf_op jit(solution)/shard_map/ppermute | solution.py:24
  155.6 15.7 %collective-permute-start.21 = (f32[8,1152]{1,0:T(8,128)S(1)}, f32[8,1152]{1,0:T(8,128)S(1)}, u32[]{:S(2)}, u32[]{:S(2)}) collective-permute-start(f32[8,1152]{1,0:T(8,128)S(1)} %slice.61), channel_id=1, source_target_pairs={{0,1},{1,0},{2,3},{3,2},{4,5},{5,4},{6,7},{7,6},{8,9},{9,8},{10,11... | collective-permute-start | bytes 110600 | tf_op jit(solution)/shard_map/ppermute | solution.py:24
  165.9 7.3 %collective-permute-start.22 = (f32[8,1152]{1,0:T(8,128)S(1)}, f32[8,1152]{1,0:T(8,128)S(1)}, u32[]{:S(2)}, u32[]{:S(2)}) collective-permute-start(f32[8,1152]{1,0:T(8,128)S(1)} %get-tuple-element.30), channel_id=1, source_target_pairs={{0,9},{1,8},{2,11},{3,10},{4,13},{5,12},{6,15},{7,14},{8,1},{9,0},... | collective-permute-start | bytes 110600 | tf_op jit(solution)/shard_map/ppermute | solution.py:24
  171.0 6.8 %collective-permute-start.20 = (f32[8,1152]{1,0:T(8,128)S(1)}, f32[8,1152]{1,0:T(8,128)S(1)}, u32[]{:S(2)}, u32[]{:S(2)}) collective-permute-start(f32[8,1152]{1,0:T(8,128)S(1)} %get-tuple-element.31), channel_id=1, source_target_pairs={{0,8},{1,9},{2,10},{3,11},{4,12},{5,13},{6,14},{7,15},{8,0},{9,1},... | collective-permute-start | bytes 110600 | tf_op jit(solution)/shard_map/ppermute | solution.py:24

commit v2 on v1

v2 whole, which is shorter than its diff:
```python
import functools

import jax
import jax.numpy as jnp
import numpy as np
from jax import lax
from jax.experimental import pallas as pl
from jax.experimental.pallas import tpu as pltpu
from jax.sharding import Mesh, PartitionSpec as P

AXES = ("x", "y", "h", "l", "c")
SIZES = (4, 4, 2, 4, 2)
F32 = jnp.float32
BF16 = jnp.bfloat16
MIB = 1 << 20


def _perm(move):
    pairs = []
    for source in range(256):
        x, y, h, l, c = (int(i) for i in np.unravel_index(source, SIZES))
        X, Y, Z, C = move(x, y, h * 4 + l, c)
        Z %= 8
        pairs.append((source, int(np.ravel_multi_index((X % 4, Y % 4, Z // 4, Z % 4, C % 2), SIZES))))
    return pairs


def _permute(a, move):
    return lax.ppermute(a, AXES, _perm(move))


def _first(k):
    return lambda x, y, z, c: (x + k, y, z, c) if c == 0 else (x, y + k, z, c)


def _second(k):
    return lambda x, y, z, c: (x, y + k, z, c) if c == 0 else (x + k, y, z, c)


def _swap(x, y, z, c):
    return (x, y, z, 1 - c)


def _z(k):
    return lambda x, y, z, c: (x, y, z + k, c)


def _z_two(x, y, z, c):
    return (x, y, z + 2 if c == 0 else z - 2, c)


def _lo(k):
    return lambda x, y, z, c: (x, y, (z // 4) * 4 + (z % 4 + k) % 4, c)


VMEM = functools.partial(pl.BlockSpec, memory_space=pltpu.VMEM)
ANY = pl.BlockSpec(memory_space=pl.ANY)
SMEM = pl.BlockSpec(memory_space=pltpu.SMEM)


def _order_kernel(place, tokens, mine, theirs):
    for half, out in ((0, mine), (1, theirs)):
        batch = place[half]
        q = place[2 + half]
        for i in range(4):
            a = lax.rem(q + i, 4)
            for j in range(4):
                block = jnp.where(batch == 0, a * 4 + j, j * 4 + a)
                row = pl.multiple_of(block * 16, 16)
                out[pl.ds((i * 4 + j) * 16, 16), :] = tokens[batch, pl.ds(row, 16), :]


def _order(place, tokens):
    _, rows, width = tokens.shape
    shape = jax.ShapeDtypeStruct((rows, width), BF16)
    return pl.pallas_call(
        _order_kernel,
        in_specs=[SMEM, VMEM()],
        out_specs=[VMEM(), VMEM()],
        out_shape=[shape, shape],
        name="order_rows",
    )(place, tokens)


def _load_weights(offsets, weights, buffer, sems, blocks):
    units = weights[0].shape[0]
    width = buffer.shape[-1]
    copies = []
    for k in range(blocks):
        column = pl.multiple_of(offsets[k] * width, 128)
        copies.append(
            [
                pltpu.make_async_copy(
                    w.at[:, pl.ds(column, width)],
                    buffer.at[k, pl.ds(i * units, units), :],
                    sems.at[k, i],
                )
                for i, w in enumerate(weights)
            ]
        )
    for step in copies:
        for copy in step:
            copy.start()
    return copies


def _dot_t(w, t):
    return lax.dot_general(w, t, (((1,), (1,)), ((), ())), preferred_element_type=F32)


def _own_kernel(offsets, mine, other, g0, g1, u0, u1, out, buffer, sems):
    copies = _load_weights(offsets, (g0, g1, u0, u1), buffer, sems, 2)
    for k, t in enumerate((mine, other)):
        for copy in copies[k]:
            copy.wait()
        part = _dot_t(buffer[k], t[...])
        if k == 0:
            out[...] = part
        else:
            out[...] += part


def _own(offsets, mine, other, weights):
    units, (rows, width) = weights[0].shape[0], mine.shape
    return pl.pallas_call(
        _own_kernel,
        in_specs=[SMEM, VMEM(), VMEM()] + [ANY] * 4,
        out_specs=VMEM(),
        out_shape=jax.ShapeDtypeStruct((4 * units, rows), F32),
        scratch_shapes=[pltpu.VMEM((2, 4 * units, width), BF16), pltpu.SemaphoreType.DMA((2, 4))],
        compiler_params=pltpu.CompilerParams(vmem_limit_bytes=16 * MIB),
        cost_estimate=pl.CostEstimate(
            flops=2 * 8 * units * rows * width, bytes_accessed=20 * units * width, transcendentals=0
        ),
        name="own_features",
    )(offsets, mine, other, *weights)


def _hidden_kernel(offsets, tokens, start, g0, g1, u0, u1, out, acc, buffer, sems):
    copies = _load_weights(offsets, (g0, g1, u0, u1), buffer, sems, 6)
    units = g0.shape[0]
    for k in range(6):
        for copy in copies[k]:
            copy.wait()
        part = _dot_t(buffer[k], tokens[k])
        if k == 0:
            acc[...] = start[...] + part
        else:
            acc[...] += part
    gate = acc[pl.ds(0, 2 * units), :]
    up = acc[pl.ds(2 * units, 2 * units), :]
    hidden = (gate / (1 + jnp.exp(-gate)) * up).astype(BF16)
    half = hidden.shape[1] // 2
    odd = offsets[6] == 1
    a, b = hidden[:, :half], hidden[:, half:]
    out[:, :half] = jnp.where(odd, b, a)
    out[:, half:] = jnp.where(odd, a, b)


def _hidden(offsets, tokens, start, weights):
    units, (blocks, rows, width) = weights[0].shape[0], tokens.shape
    return pl.pallas_call(
        _hidden_kernel,
        in_specs=[SMEM, VMEM(), VMEM()] + [ANY] * 4,
        out_specs=VMEM(),
        out_shape=jax.ShapeDtypeStruct((2 * units, rows), BF16),
        scratch_shapes=[
            pltpu.VMEM((4 * units, rows), F32),
            pltpu.VMEM((blocks, 4 * units, width), BF16),
            pltpu.SemaphoreType.DMA((blocks, 4)),
        ],
        compiler_params=pltpu.CompilerParams(vmem_limit_bytes=24 * MIB),
        cost_estimate=pl.CostEstimate(
            flops=2 * 4 * blocks * units * rows * width,
            bytes_accessed=8 * blocks * units * width,
            transcendentals=2 * units * rows,
        ),
        name="gate_up_silu",
    )(offsets, tokens, start, *weights)


COLUMNS = 384


def _down_kernel(place, h0, h1, h2, h3, d0, d1, own, s1, s2, s3, ht, buffer, sems):
    width = d0.shape[1]
    tiles = width // COLUMNS
    units = h0.shape[0] // 2
    copies = []
    for i, d in enumerate((d0, d1)):
        for n in range(tiles):
            copies.append(
                pltpu.make_async_copy(
                    d.at[:, pl.ds(n * COLUMNS, COLUMNS)], buffer.at[i * tiles + n], sems.at[i * tiles + n]
                )
            )
    for copy in copies:
        copy.start()
    l, c = place[0], place[1]
    for k, part in enumerate((h0, h1, h2, h3)):
        base = lax.rem(l + k, 4) * (2 * units)
        for i, core in enumerate((c, 1 - c)):
            row = pl.multiple_of(base + core * units, 16)
            ht[pl.ds(row, units), :] = part[pl.ds(i * units, units), :]
    hidden = ht[...].T
    block = hidden.shape[0] // 4
    for i in range(2):
        for n in range(tiles):
            copies[i * tiles + n].wait()
            result = jnp.dot(hidden, buffer[i * tiles + n], preferred_element_type=F32)
            columns = pl.ds(n * COLUMNS, COLUMNS)
            own[i, :, columns] = result[:block]
            for k, out in enumerate((s1, s2, s3)):
                out[i, :, columns] = result[(k + 1) * block : (k + 2) * block].astype(BF16)


def _down(place, hs, d0, d1):
    units2, rows = hs[0].shape
    depth, width = d0.shape
    block = rows // 4
    tiles = 2 * width // COLUMNS
    send = jax.ShapeDtypeStruct((2, block, width), BF16)
    return pl.pallas_call(
        _down_kernel,
        in_specs=[SMEM] + [VMEM()] * 4 + [ANY] * 2,
        out_specs=[VMEM()] * 4,
        out_shape=[jax.ShapeDtypeStruct((2, block, width), F32), send, send, send],
        scratch_shapes=[
            pltpu.VMEM((depth, rows), BF16),
            pltpu.VMEM((tiles, depth, COLUMNS), BF16),
            pltpu.SemaphoreType.DMA((tiles,)),
        ],
        compiler_params=pltpu.CompilerParams(vmem_limit_bytes=24 * MIB),
        cost_estimate=pl.CostEstimate(
            flops=4 * rows * depth * width, bytes_accessed=4 * depth * width, transcendentals=0
        ),
        name="down",
    )(place, *hs, d0, d1)


def local(tokens, gate_weight, up_weight, down_weight):
    x, y, h, l, c = (lax.axis_index(a).astype(jnp.int32) for a in AXES)
    core0 = c == 0
    width = tokens.shape[-1]

    q0, q1 = (x + 2 * y) % 4, (2 * x + y) % 4
    place = jnp.stack([c, 1 - c, jnp.where(core0, q0, q1), jnp.where(core0, q1, q0)])
    s2 = jnp.where(core0, y, x)
    ahead = [((l + k) % 4) * 2 for k in range(4)]
    columns_own = jnp.stack([ahead[0] + c, ahead[0] + 1 - c])
    columns = jnp.stack([o for a in ahead[1:] for o in (a + c, a + 1 - c)] + [s2 % 2])

    mine, theirs = _order(place, tokens)
    other = _permute(theirs, _swap)
    gate_other = _permute(gate_weight, _swap)
    up_other = _permute(up_weight, _swap)

    quarter = jnp.stack([mine[:64], other[:64]])
    from_up = _permute(quarter, _z(-1))
    from_down = _permute(quarter, _z(1))
    from_two = _permute(quarter, _z_two)
    down_in, _ = lax.optimization_barrier((down_weight, from_up))
    down_other = _permute(down_in, _swap)

    bundle = jnp.concatenate([from_up, from_two, from_down], axis=0)
    bundle, gate_other, up_other = lax.optimization_barrier((bundle, gate_other, up_other))
    weights = (gate_weight, gate_other, up_weight, up_other)
    next1 = _permute(bundle, _first(-1))
    next3 = _permute(bundle, _first(1))
    next2a = _permute(bundle[:, :32], _second(-1))
    next2b = _permute(bundle[:, 32:], _second(1))
    start = _own(columns_own, mine, other, weights)
    rest = jnp.concatenate([bundle, next1, next2a, next2b, next3], axis=1)

    hidden = _hidden(columns, rest, start, weights)
    hs = [hidden] + [_permute(hidden, _lo(-k)) for k in (1, 2, 3)]

    own, *sends = _down(jnp.stack([l, c]), hs, down_weight, down_other)
    got = [_permute(s, _first(k)) for s, k in zip(sends, (1, 2, 3))]
    stage = own
    for g in got:
        stage = stage + g.astype(F32)
    stage = stage.reshape(2, 4, 16, width)

    def to2(k):
        return lax.dynamic_index_in_dim(stage, (s2 + k) % 4, 1, keepdims=False)

    last = to2(0)
    got = [_permute(to2(k).astype(BF16), _second(k)) for k in (1, 2, 3)]
    for g in got:
        last = last + g.astype(F32)

    cross = _permute(last[1], _swap)
    both = jnp.stack([jnp.where(core0, last[0], cross), jnp.where(core0, cross, last[0])])
    both = both.reshape(2, 2, 8, width)
    here = lax.dynamic_index_in_dim(both, h, 1, keepdims=False)
    there = lax.dynamic_index_in_dim(both, 1 - h, 1, keepdims=False)
    return (here + _permute(there, _z(4))).astype(BF16)


def solution(mesh):
    fine = Mesh(mesh.devices.reshape(SIZES), AXES)
    wide, narrow = ("x", "y", "h"), ("l", "c")
    return jax.shard_map(
        local,
        mesh=fine,
        in_specs=(
            P(None, None, narrow),
            P(wide + narrow, None),
            P(wide + narrow, None),
            P(wide, narrow),
        ),
        out_specs=P(None, wide, narrow),
        check_vma=False,
    )
```

time: 180 us -> 112 us (0.62)
  other arithmetic: 57.6 us -> 4.47 us
  Pallas kernels: 0 us -> 17 us
  waiting for transfers between devices: 59.4 us -> 43.1 us
  matrix products: 11.8 us -> 0 us
  starting transfers between devices: 46 us -> 39.8 us
  local copies, waits for them, and re-layouts: 3.48 us -> 6.3 us
    concatenate x2 -> x1, other arithmetic: 47.2 us -> 2.15 us  [local(): bundle = jnp.concatenate([from_up, from_two, from_down], axis=0)]
    pallas_call x0 -> x4, Pallas kernels: none -> 17 us  [the longest x1 7.06 us: _hidden(): pl.pallas_call(_hidden_kernel, in_specs=[SMEM, VMEM(), VMEM()] + [ANY] *...]
    ppermute x23 -> x22, waiting for transfers between devices: 59.4 us -> 43.1 us  [_permute(): return lax.ppermute(a, AXES, _perm(move))]
    dot_general x3 -> x0, matrix products: 11.8 us -> none  [the longest x1 8.62 us: local(): jnp.einsum('bf,fd->bd', jnp.concatenate(hs, axis=1), dw, preferred_elemen...]
    select_n x4 -> x0, other arithmetic: 8.52 us -> none  [the longest x1 2.9 us: local(): jnp.where(core0, up_other, up_weight)]
    ppermute x23 -> x22, starting transfers between devices: 46 us -> 39.8 us  [_permute(): return lax.ppermute(a, AXES, _perm(move))]
    unnamed x11 -> x16, local copies, waits for them, and re-layouts: 1.27 us -> 3.5 us
  transfers between devices with their start and end apart: 23 -> 22, of which waited for: 14 -> 14; matrix products, arithmetic and copies ran while one was open for 29% -> 8% of each run, Pallas kernels for 0% -> 12%
where the time goes in v2:
time: 112 us; the launch traced here: 111 us
  waiting for transfers between devices  43.1 us (38%)
  starting transfers between devices  39.8 us (36%)
  Pallas kernels  17 us (15%)
  local copies, waits for them, and re-layouts  6.3 us (6%)
  other arithmetic  4.47 us (4%)
    ppermute x22, waiting for transfers between devices, _permute(): return lax.ppermute(a, AXES, _perm(move))  43.1 us
    ppermute x22, starting transfers between devices, _permute(): return lax.ppermute(a, AXES, _perm(move))  39.8 us
    pallas_call x1, Pallas kernels, _hidden(): pl.pallas_call(_hidden_kernel, in_specs=[SMEM, VMEM(), VMEM()] + [ANY] *...  7.06 us
    pallas_call x1, Pallas kernels, _down(): pl.pallas_call(_down_kernel, in_specs=[SMEM] + [VMEM()] * 4 + [ANY] * 2,...  4.15 us
    unnamed x16, local copies, waits for them, and re-layouts  3.5 us
    pallas_call x1, Pallas kernels, _own(): pl.pallas_call(_own_kernel, in_specs=[SMEM, VMEM(), VMEM()] + [ANY] * 4,...  3.34 us
    pallas_call x1, Pallas kernels, _order(): pl.pallas_call(_order_kernel, in_specs=[SMEM, VMEM()], out_specs=[VMEM(),...  2.44 us
  transfers between devices with their start and end apart: 22, of which 14 were waited for; matrix products, arithmetic and copies ran while one was open for 8% of the time, Pallas kernels for 12%

profile of v2, /device:TPU:1, one launch (start us, length us, event | category | flops | bytes accessed | tf_op | source)
XLA Modules:
  0.0 110.9 jit_solution(14623709540704203188)
XLA Ops:
  0.0 3.2 %collective-permute-start.4 = (bf16[144,9216]{1,0:T(8,128)(2,1)}, bf16[144,9216]{1,0:T(8,128)(2,1)}, u32[]{:S(2)}, u32[]{:S(2)}) collective-permute-start(bf16[144,9216]{1,0:T(8,128)(2,1)} %g0.3), channel_id=1, source_target_pairs={{0,1},{1,0},{2,3},{3,2},{4,5},{5,4},{6,7},{7,6},{8,9},{9,8},{10,11... | collective-permute-start | bytes 7962632 | tf_op jit(solution)/shard_map/ppermute | solution.py:29
  3.2 0.0 collective-permute-start.5
  3.2 0.6 pad_add_fusion.1.place
  3.8 2.4 %order_rows.1 = (bf16[256,1152]{1,0:T(8,128)(2,1)}, bf16[256,1152]{1,0:T(8,128)(2,1)}) custom-call(s32[4]{0:T(128)} %pad_add_fusion.1.place, bf16[2,256,1152]{2,1,0:T(8,128)(2,1)} %tokens.1), custom_call_target="tpu_custom_call" | custom-call | tf_op jit(solution)/shard_map/order_rows/pallas_call | solution.py:76
  6.3 0.5 collective-permute-start
  6.8 1.2 %slice_bitcast_fusion.1 = bf16[1,64,1152]{2,1,0:T(8,128)(2,1)S(1)} fusion(bf16[256,1152]{1,0:T(8,128)(2,1)} %get-tuple-element.15.mine), kind=kLoop, calls=%fused_computation.14 | loop fusion | bytes 294912 | tf_op jit(solution)/shard_map/stack | solution.py:258
  8.0 1.8 %collective-permute-done.other = bf16[256,1152]{1,0:T(8,128)(2,1)S(1)} collective-permute-done((bf16[256,1152]{1,0:T(8,128)(2,1)}, bf16[256,1152]{1,0:T(8,128)(2,1)S(1)}, u32[]{:S(2)}, u32[]{:S(2)}) %collective-permute-start) | collective-permute-done | bytes 589856 | tf_op jit(solution)/shard_map/ppermute | solution.py:29
  9.7 0.8 copy-done.4
  10.6 0.8 pad_maximum_fusion.1
  11.3 3.8 %collective-permute-start.1 = (bf16[2,64,1152]{2,1,0:T(8,128)(2,1)}, bf16[2,64,1152]{2,1,0:T(8,128)(2,1)S(1)}, u32[]{:S(2)}, u32[]{:S(2)}) collective-permute-start(bf16[2,64,1152]{2,1,0:T(8,128)(2,1)} %pad_maximum_fusion.1), channel_id=1, source_target_pairs={{0,14},{1,15},{2,0},{3,1},{4,2},{5,3},{6,4},{7,5},{8,6},{9,7},{10,... | collective-permute-start | bytes 884744 | tf_op jit(solution)/shard_map/ppermute | solution.py:29
  15.2 1.2 %collective-permute-start.2 = (bf16[2,64,1152]{2,1,0:T(8,128)(2,1)}, bf16[2,64,1152]{2,1,0:T(8,128)(2,1)}, u32[]{:S(2)}, u32[]{:S(2)}) collective-permute-start(bf16[2,64,1152]{2,1,0:T(8,128)(2,1)} %pad_maximum_fusion.1), channel_id=1, source_target_pairs={{0,4},{1,13},{2,6},{3,15},{4,8},{5,1},{6,10},{7,3},{8,12},{9,5},{1... | collective-permute-start | bytes 884744 | tf_op jit(solution)/shard_map/ppermute | solution.py:29
  16.3 0.7 collective-permute-start.3
  17.1 5.1 %collective-permute-done.1 = bf16[2,64,1152]{2,1,0:T(8,128)(2,1)S(1)} collective-permute-done((bf16[2,64,1152]{2,1,0:T(8,128)(2,1)}, bf16[2,64,1152]{2,1,0:T(8,128)(2,1)S(1)}, u32[]{:S(2)}, u32[]{:S(2)}) %collective-permute-start.1) | collective-permute-done | bytes 294944 | tf_op jit(solution)/shard_map/ppermute | solution.py:29
  22.2 4.1 %collective-permute-start.13 = (bf16[1152,1152]{1,0:T(8,128)(2,1)}, bf16[1152,1152]{1,0:T(8,128)(2,1)}, u32[]{:S(2)}, u32[]{:S(2)}) collective-permute-start(bf16[1152,1152]{1,0:T(8,128)(2,1)} %d0.1), channel_id=1, source_target_pairs={{0,1},{1,0},{2,3},{3,2},{4,5},{5,4},{6,7},{7,6},{8,9},{9,8},{10,11... | collective-permute-start | bytes 7962632 | tf_op jit(solution)/shard_map/ppermute | solution.py:29
  26.3 2.3 %collective-permute-done.2 = bf16[2,64,1152]{2,1,0:T(8,128)(2,1)} collective-permute-done((bf16[2,64,1152]{2,1,0:T(8,128)(2,1)}, bf16[2,64,1152]{2,1,0:T(8,128)(2,1)}, u32[]{:S(2)}, u32[]{:S(2)}) %collective-permute-start.2) | collective-permute-done | bytes 294944 | tf_op jit(solution)/shard_map/ppermute | solution.py:29
  28.6 1.5 %collective-permute-done.3 = bf16[2,64,1152]{2,1,0:T(8,128)(2,1)} collective-permute-done((bf16[2,64,1152]{2,1,0:T(8,128)(2,1)}, bf16[2,64,1152]{2,1,0:T(8,128)(2,1)}, u32[]{:S(2)}, u32[]{:S(2)}) %collective-permute-start.3) | collective-permute-done | bytes 294944 | tf_op jit(solution)/shard_map/ppermute | solution.py:29
  30.1 2.2 %pad_maximum_fusion = bf16[6,64,1152]{2,1,0:T(8,128)(2,1)} fusion(bf16[2,64,1152]{2,1,0:T(8,128)(2,1)} %collective-permute-done.3, bf16[2,64,1152]{2,1,0:T(8,128)(2,1)} %collective-permute-done.2, bf16[2,64,1152]{2,1,0:T(8,128)(2,1)S(1)} %collective-permute-done.1), kind=kLoop, calls=%fused_computation | loop fusion | flops 884736 | bytes 1769472 | tf_op jit(solution)/shard_map/concatenate | solution.py:265
  32.3 0.0 collective-permute-done.4.g1
  32.3 0.0 collective-permute-done.5.u1
  32.3 2.7 %collective-permute-start.6 = (bf16[6,64,1152]{2,1,0:T(8,128)(2,1)}, bf16[6,64,1152]{2,1,0:T(8,128)(2,1)}, u32[]{:S(2)}, u32[]{:S(2)}) collective-permute-start(bf16[6,64,1152]{2,1,0:T(8,128)(2,1)} %pad_maximum_fusion), channel_id=1, source_target_pairs={{0,192},{1,49},{2,194},{3,51},{4,196},{5,53},{6,198},{7,55},{8,200... | collective-permute-start | bytes 2654216 | tf_op jit(solution)/shard_map/ppermute | solution.py:29
  35.0 0.1 pad_add_fusion.2.offsets
  35.1 0.1 stack.83.offsets
  35.2 0.1 collective-permute-start.9
  35.3 1.4 %fusion.11 = (bf16[6,32,1152]{2,1,0:T(8,128)(2,1)S(1)}, bf16[6,32,1152]{2,1,0:T(8,128)(2,1)S(1)}) fusion(bf16[6,64,1152]{2,1,0:T(8,128)(2,1)} %pad_maximum_fusion), kind=kLoop, calls=%fused_computation.36 | loop fusion | bytes 1769472 | tf_op jit(solution)/shard_map/slice | solution.py:271
  36.6 2.6 %collective-permute-start.7 = (bf16[6,32,1152]{2,1,0:T(8,128)(2,1)S(1)}, bf16[6,32,1152]{2,1,0:T(8,128)(2,1)S(1)}, u32[]{:S(2)}, u32[]{:S(2)}) collective-permute-start(bf16[6,32,1152]{2,1,0:T(8,128)(2,1)S(1)} %get-tuple-element.26), channel_id=1, source_target_pairs={{0,48},{1,193},{2,50},{3,195},{4,52},{5,197},{6,54},{7,199},{8,56}... | collective-permute-start | bytes 1327112 | tf_op jit(solution)/shard_map/ppermute | solution.py:29
  39.2 1.2 %constant_dynamic-update-slice_fusion.4 = bf16[6,256,1152]{2,1,0:T(8,128)(2,1)S(1)} fusion(bf16[6,64,1152]{2,1,0:T(8,128)(2,1)} %pad_maximum_fusion), kind=kLoop, calls=%fused_computation.32 | loop fusion | bytes 1769472
  40.5 0.1 collective-permute-start.8
  40.6 3.3 %own_features.1.start = f32[576,256]{1,0:T(8,128)S(1)} custom-call(s32[2]{0:T(128)S(1)} %pad_add_fusion.2.offsets, bf16[256,1152]{1,0:T(8,128)(2,1)S(1)} %copy-done.3, bf16[256,1152]{1,0:T(8,128)(2,1)S(1)} %copy-done.5, bf16[144,9216]{1,0:T(8,128)(2,1)S(1)} %copy-done, bf16[144,9216]{1,0:T(8,128)(2,1)} %collective-permute-done.4.g1, ...), custom_call_target="tpu_custom_call" | custom-call | flops 679477248 | bytes 3317760 | tf_op jit(solution)/shard_map/own_features/pallas_call | solution.py:125
  43.9 4.8 %collective-permute-done.6 = bf16[6,64,1152]{2,1,0:T(8,128)(2,1)} collective-permute-done((bf16[6,64,1152]{2,1,0:T(8,128)(2,1)}, bf16[6,64,1152]{2,1,0:T(8,128)(2,1)}, u32[]{:S(2)}, u32[]{:S(2)}) %collective-permute-start.6) | collective-permute-done | bytes 884768 | tf_op jit(solution)/shard_map/ppermute | solution.py:29
  48.7 1.3 %constant_dynamic-update-slice_fusion.3 = bf16[6,256,1152]{2,1,0:T(8,128)(2,1)S(1)} fusion(bf16[6,256,1152]{2,1,0:T(8,128)(2,1)S(1)} %constant_dynamic-update-slice_fusion.4, bf16[6,64,1152]{2,1,0:T(8,128)(2,1)} %collective-permute-done.6), kind=kLoop, calls=%fused_computation.31 | loop fusion | bytes 1769472
  50.0 0.0 collective-permute-done.7
  50.0 0.1 constant_dynamic-update-slice_fusion.2
  50.1 3.9 %collective-permute-done.8 = bf16[6,32,1152]{2,1,0:T(8,128)(2,1)S(1)} collective-permute-done((bf16[6,32,1152]{2,1,0:T(8,128)(2,1)S(1)}, bf16[6,32,1152]{2,1,0:T(8,128)(2,1)S(1)}, u32[]{:S(2)}, u32[]{:S(2)}) %collective-permute-start.8) | collective-permute-done | bytes 442400 | tf_op jit(solution)/shard_map/ppermute | solution.py:29
  54.0 0.1 constant_dynamic-update-slice_fusion.1
  54.1 0.0 collective-permute-done.9
  54.1 0.1 constant_dynamic-update-slice_fusion.tokens
  54.2 0.0 copy-start.2
  54.2 7.1 %gate_up_silu.1.h0 = bf16[288,256]{1,0:T(8,128)(2,1)S(1)} custom-call(s32[7]{0:T(128)S(1)} %stack.83.offsets, bf16[6,256,1152]{2,1,0:T(8,128)(2,1)S(1)} %constant_dynamic-update-slice_fusion.tokens, f32[576,256]{1,0:T(8,128)S(1)} %own_features.1.start, bf16[144,9216]{1,0:T(8,128)(2,1)S(1)} %copy-done, bf16[144,9216]{1,0:T(8,128)(2,1)} %collective-permute-done.4.g1, ...), custom_call_target="tpu_custom_call" | custom-call | flops 2038431744 | bytes 7962624 | tf_op jit(solution)/shard_map/gate_up_silu/pallas_call | solution.py:162
  61.3 0.3 collective-permute-start.10
  61.6 0.7 collective-permute-start.11
  62.2 1.4 %collective-permute-start.12 = (bf16[288,256]{1,0:T(8,128)(2,1)S(1)}, bf16[288,256]{1,0:T(8,128)(2,1)S(1)}, u32[]{:S(2)}, u32[]{:S(2)}) collective-permute-start(bf16[288,256]{1,0:T(8,128)(2,1)S(1)} %gate_up_silu.1.h0), channel_id=1, source_target_pairs={{0,2},{1,3},{2,4},{3,5},{4,6},{5,7},{6,0},{7,1},{8,10},{9,11},{10,... | collective-permute-start | bytes 442376 | tf_op jit(solution)/shard_map/ppermute | solution.py:29
  63.6 0.1 pad_add_fusion.place
  63.7 0.0 collective-permute-done.13.d1
  63.7 4.2 %collective-permute-done.10.h1 = bf16[288,256]{1,0:T(8,128)(2,1)S(1)} collective-permute-done((bf16[288,256]{1,0:T(8,128)(2,1)S(1)}, bf16[288,256]{1,0:T(8,128)(2,1)S(1)}, u32[]{:S(2)}, u32[]{:S(2)}) %collective-permute-start.10) | collective-permute-done | bytes 147488 | tf_op jit(solution)/shard_map/ppermute | solution.py:29
  67.8 0.0 collective-permute-done.11.h2
  67.8 5.1 %collective-permute-done.12.h3 = bf16[288,256]{1,0:T(8,128)(2,1)S(1)} collective-permute-done((bf16[288,256]{1,0:T(8,128)(2,1)S(1)}, bf16[288,256]{1,0:T(8,128)(2,1)S(1)}, u32[]{:S(2)}, u32[]{:S(2)}) %collective-permute-start.12) | collective-permute-done | bytes 147488 | tf_op jit(solution)/shard_map/ppermute | solution.py:29
  72.9 4.1 %down.1 = (f32[2,64,1152]{2,1,0:T(8,128)S(1)}, bf16[2,64,1152]{2,1,0:T(8,128)(2,1)S(1)}, bf16[2,64,1152]{2,1,0:T(8,128)(2,1)S(1)}, bf16[2,64,1152]{2,1,0:T(8,128)(2,1)S(1)}) custom-call(s32[2]{0:T(128)S(1)} %pad_add_fusion.place, bf16[288,256]{1,0:T(8,128)(2,1)S(1)} %gate_up_silu.1.h0, bf16[288,256]{1,0:T(8,128)(2,1)S(1)} %collective-permute-done.10.h1, ...), custom_call_target="tpu_custom_call" | custom-call | flops 1358954496 | bytes 5308416 | tf_op jit(solution)/shard_map/down/pallas_call | solution.py:223
  77.1 0.1 collective-permute-start.14
  77.2 3.4 %collective-permute-start.15 = (bf16[2,64,1152]{2,1,0:T(8,128)(2,1)S(1)}, bf16[2,64,1152]{2,1,0:T(8,128)(2,1)S(1)}, u32[]{:S(2)}, u32[]{:S(2)}) collective-permute-start(bf16[2,64,1152]{2,1,0:T(8,128)(2,1)S(1)} %get-tuple-element.23), channel_id=1, source_target_pairs={{0,128},{1,33},{2,130},{3,35},{4,132},{5,37},{6,134},{7,39},{8,136... | collective-permute-start | bytes 884744 | tf_op jit(solution)/shard_map/ppermute | solution.py:29
  80.6 3.3 %collective-permute-done.14 = bf16[2,64,1152]{2,1,0:T(8,128)(2,1)S(1)} collective-permute-done((bf16[2,64,1152]{2,1,0:T(8,128)(2,1)S(1)}, bf16[2,64,1152]{2,1,0:T(8,128)(2,1)S(1)}, u32[]{:S(2)}, u32[]{:S(2)}) %collective-permute-start.14) | collective-permute-done | bytes 294944 | tf_op jit(solution)/shard_map/ppermute | solution.py:29
  84.0 4.2 %collective-permute-done.15 = bf16[2,64,1152]{2,1,0:T(8,128)(2,1)S(1)} collective-permute-done((bf16[2,64,1152]{2,1,0:T(8,128)(2,1)S(1)}, bf16[2,64,1152]{2,1,0:T(8,128)(2,1)S(1)}, u32[]{:S(2)}, u32[]{:S(2)}) %collective-permute-start.15) | collective-permute-done | bytes 294944 | tf_op jit(solution)/shard_map/ppermute | solution.py:29
  88.2 0.0 collective-permute-done.16
  88.2 0.1 convert_add_fusion
  88.4 0.1 collective-permute-start.17
  88.4 1.4 %collective-permute-start.18 = (bf16[2,16,1152]{2,1,0:T(8,128)(2,1)S(1)}, bf16[2,16,1152]{2,1,0:T(8,128)(2,1)S(1)}, u32[]{:S(2)}, u32[]{:S(2)}) collective-permute-start(bf16[2,16,1152]{2,1,0:T(8,128)(2,1)S(1)} %get-tuple-element.29), channel_id=1, source_target_pairs={{0,32},{1,129},{2,34},{3,131},{4,36},{5,133},{6,38},{7,135},{8,40}... | collective-permute-start | bytes 221192 | tf_op jit(solution)/shard_map/ppermute | solution.py:29
  89.8 2.0 %collective-permute-start.19 = (bf16[2,16,1152]{2,1,0:T(8,128)(2,1)S(1)}, bf16[2,16,1152]{2,1,0:T(8,128)(2,1)S(1)}, u32[]{:S(2)}, u32[]{:S(2)}) collective-permute-start(bf16[2,16,1152]{2,1,0:T(8,128)(2,1)S(1)} %get-tuple-element.28), channel_id=1, source_target_pairs={{0,48},{1,193},{2,50},{3,195},{4,52},{5,197},{6,54},{7,199},{8,56}... | collective-permute-start | bytes 221192 | tf_op jit(solution)/shard_map/ppermute | solution.py:29
  91.8 1.8 %collective-permute-done.17 = bf16[2,16,1152]{2,1,0:T(8,128)(2,1)S(1)} collective-permute-done((bf16[2,16,1152]{2,1,0:T(8,128)(2,1)S(1)}, bf16[2,16,1152]{2,1,0:T(8,128)(2,1)S(1)}, u32[]{:S(2)}, u32[]{:S(2)}) %collective-permute-start.17) | collective-permute-done | bytes 73760 | tf_op jit(solution)/shard_map/ppermute | solution.py:29
  93.6 0.0 collective-permute-done.18
  93.6 0.6 collective-permute-done.19
  94.3 7.7 %collective-permute-start.20 = (f32[16,1152]{1,0:T(8,128)S(1)}, f32[16,1152]{1,0:T(8,128)S(1)}, u32[]{:S(2)}, u32[]{:S(2)}) collective-permute-start(f32[16,1152]{1,0:T(8,128)S(1)} %slice_bitcast_fusion.2), channel_id=1, source_target_pairs={{0,1},{1,0},{2,3},{3,2},{4,5},{5,4},{6,7},{7,6},{8,9},{9,8},{10,11... | collective-permute-start | bytes 221192 | tf_op jit(solution)/shard_map/ppermute | solution.py:29
  102.0 0.9 collective-permute-done.20
  102.9 3.8 %collective-permute-start.21 = (f32[2,8,1152]{2,1,0:T(8,128)S(1)}, f32[2,8,1152]{2,1,0:T(8,128)S(1)}, u32[]{:S(2)}, u32[]{:S(2)}) collective-permute-start(f32[2,8,1152]{2,1,0:T(8,128)S(1)} %fusion.6), channel_id=1, source_target_pairs={{0,8},{1,9},{2,10},{3,11},{4,12},{5,13},{6,14},{7,15},{8,0},{9,1},... | collective-permute-start | bytes 221192 | tf_op jit(solution)/shard_map/ppermute | solution.py:29
  106.7 3.5 %collective-permute-done.21 = f32[2,8,1152]{2,1,0:T(8,128)S(1)} collective-permute-done((f32[2,8,1152]{2,1,0:T(8,128)S(1)}, f32[2,8,1152]{2,1,0:T(8,128)S(1)}, u32[]{:S(2)}, u32[]{:S(2)}) %collective-permute-start.21) | collective-permute-done | bytes 73760 | tf_op jit(solution)/shard_map/ppermute | solution.py:29
  110.2 0.6 fusion.10
  (17 shorter events, 0.1 us)
Async XLA Ops:
  0.0 32.3 %collective-permute-start.4 = (bf16[144,9216]{1,0:T(8,128)(2,1)}, bf16[144,9216]{1,0:T(8,128)(2,1)}, u32[]{:S(2)}, u32[]{:S(2)}) collective-permute-start(bf16[144,9216]{1,0:T(8,128)(2,1)} %g0.3), channel_id=1, source_target_pairs={{0,1},{1,0},{2,3},{3,2},{4,5},{5,4},{6,7},{7,6},{8,9},{9,8},{10,11... | collective-permute-start | bytes 7962632 | tf_op jit(solution)/shard_map/ppermute | solution.py:29
  3.2 29.0 %collective-permute-start.5 = (bf16[144,9216]{1,0:T(8,128)(2,1)}, bf16[144,9216]{1,0:T(8,128)(2,1)}, u32[]{:S(2)}, u32[]{:S(2)}) collective-permute-start(bf16[144,9216]{1,0:T(8,128)(2,1)} %u0.3), channel_id=1, source_target_pairs={{0,1},{1,0},{2,3},{3,2},{4,5},{5,4},{6,7},{7,6},{8,9},{9,8},{10,11... | collective-permute-start | bytes 7962632 | tf_op jit(solution)/shard_map/ppermute | solution.py:29
  6.3 34.3 %copy-start = (bf16[144,9216]{1,0:T(8,128)(2,1)S(1)}, bf16[144,9216]{1,0:T(8,128)(2,1)}, u32[]{:S(2)}) copy-start(bf16[144,9216]{1,0:T(8,128)(2,1)} %g0.3) | copy-start | bytes 7962628
  6.3 34.3 %copy-start.3 = (bf16[256,1152]{1,0:T(8,128)(2,1)S(1)}, bf16[256,1152]{1,0:T(8,128)(2,1)}, u32[]{:S(2)}) copy-start(bf16[256,1152]{1,0:T(8,128)(2,1)} %get-tuple-element.15.mine) | copy-start | bytes 1769476
  6.3 3.4 %collective-permute-start = (bf16[256,1152]{1,0:T(8,128)(2,1)}, bf16[256,1152]{1,0:T(8,128)(2,1)S(1)}, u32[]{:S(2)}, u32[]{:S(2)}) collective-permute-start(bf16[256,1152]{1,0:T(8,128)(2,1)} %get-tuple-element.16), channel_id=1, source_target_pairs={{0,1},{1,0},{2,3},{3,2},{4,5},{5,4},{6,7},{7,6},{8,9},{9,8},{10,11... | collective-permute-start | bytes 1769480 | tf_op jit(solution)/shard_map/ppermute | solution.py:29
  9.7 0.8 copy-start.4
  11.3 10.8 %collective-permute-start.1 = (bf16[2,64,1152]{2,1,0:T(8,128)(2,1)}, bf16[2,64,1152]{2,1,0:T(8,128)(2,1)S(1)}, u32[]{:S(2)}, u32[]{:S(2)}) collective-permute-start(bf16[2,64,1152]{2,1,0:T(8,128)(2,1)} %pad_maximum_fusion.1), channel_id=1, source_target_pairs={{0,14},{1,15},{2,0},{3,1},{4,2},{5,3},{6,4},{7,5},{8,6},{9,7},{10,... | collective-permute-start | bytes 884744 | tf_op jit(solution)/shard_map/ppermute | solution.py:29
  15.2 13.5 %collective-permute-start.2 = (bf16[2,64,1152]{2,1,0:T(8,128)(2,1)}, bf16[2,64,1152]{2,1,0:T(8,128)(2,1)}, u32[]{:S(2)}, u32[]{:S(2)}) collective-permute-start(bf16[2,64,1152]{2,1,0:T(8,128)(2,1)} %pad_maximum_fusion.1), channel_id=1, source_target_pairs={{0,4},{1,13},{2,6},{3,15},{4,8},{5,1},{6,10},{7,3},{8,12},{9,5},{1... | collective-permute-start | bytes 884744 | tf_op jit(solution)/shard_map/ppermute | solution.py:29
  16.3 13.8 %collective-permute-start.3 = (bf16[2,64,1152]{2,1,0:T(8,128)(2,1)}, bf16[2,64,1152]{2,1,0:T(8,128)(2,1)}, u32[]{:S(2)}, u32[]{:S(2)}) collective-permute-start(bf16[2,64,1152]{2,1,0:T(8,128)(2,1)} %pad_maximum_fusion.1), channel_id=1, source_target_pairs={{0,2},{1,3},{2,4},{3,5},{4,6},{5,7},{6,8},{7,9},{8,10},{9,11},{10,... | collective-permute-start | bytes 884744 | tf_op jit(solution)/shard_map/ppermute | solution.py:29
  22.2 41.5 %collective-permute-start.13 = (bf16[1152,1152]{1,0:T(8,128)(2,1)}, bf16[1152,1152]{1,0:T(8,128)(2,1)}, u32[]{:S(2)}, u32[]{:S(2)}) collective-permute-start(bf16[1152,1152]{1,0:T(8,128)(2,1)} %d0.1), channel_id=1, source_target_pairs={{0,1},{1,0},{2,3},{3,2},{4,5},{5,4},{6,7},{7,6},{8,9},{9,8},{10,11... | collective-permute-start | bytes 7962632 | tf_op jit(solution)/shard_map/ppermute | solution.py:29
  32.3 16.5 %collective-permute-start.6 = (bf16[6,64,1152]{2,1,0:T(8,128)(2,1)}, bf16[6,64,1152]{2,1,0:T(8,128)(2,1)}, u32[]{:S(2)}, u32[]{:S(2)}) collective-permute-start(bf16[6,64,1152]{2,1,0:T(8,128)(2,1)} %pad_maximum_fusion), channel_id=1, source_target_pairs={{0,192},{1,49},{2,194},{3,51},{4,196},{5,53},{6,198},{7,55},{8,200... | collective-permute-start | bytes 2654216 | tf_op jit(solution)/shard_map/ppermute | solution.py:29
  35.2 5.4 %copy-start.1 = (bf16[144,9216]{1,0:T(8,128)(2,1)S(1)}, bf16[144,9216]{1,0:T(8,128)(2,1)}, u32[]{:S(2)}) copy-start(bf16[144,9216]{1,0:T(8,128)(2,1)} %u0.3) | copy-start | bytes 7962628
  35.2 5.4 %copy-start.5 = (bf16[256,1152]{1,0:T(8,128)(2,1)S(1)}, bf16[256,1152]{1,0:T(8,128)(2,1)}, u32[]{:S(2)}) copy-start(bf16[256,1152]{1,0:T(8,128)(2,1)} %copy-done.4) | copy-start | bytes 1769476
  35.2 18.9 %collective-permute-start.9 = (bf16[6,64,1152]{2,1,0:T(8,128)(2,1)}, bf16[6,64,1152]{2,1,0:T(8,128)(2,1)S(1)}, u32[]{:S(2)}, u32[]{:S(2)}) collective-permute-start(bf16[6,64,1152]{2,1,0:T(8,128)(2,1)} %pad_maximum_fusion), channel_id=1, source_target_pairs={{0,64},{1,17},{2,66},{3,19},{4,68},{5,21},{6,70},{7,23},{8,72},{9,... | collective-permute-start | bytes 2654216 | tf_op jit(solution)/shard_map/ppermute | solution.py:29
  36.6 13.4 %collective-permute-start.7 = (bf16[6,32,1152]{2,1,0:T(8,128)(2,1)S(1)}, bf16[6,32,1152]{2,1,0:T(8,128)(2,1)S(1)}, u32[]{:S(2)}, u32[]{:S(2)}) collective-permute-start(bf16[6,32,1152]{2,1,0:T(8,128)(2,1)S(1)} %get-tuple-element.26), channel_id=1, source_target_pairs={{0,48},{1,193},{2,50},{3,195},{4,52},{5,197},{6,54},{7,199},{8,56}... | collective-permute-start | bytes 1327112 | tf_op jit(solution)/shard_map/ppermute | solution.py:29
  40.5 13.5 %collective-permute-start.8 = (bf16[6,32,1152]{2,1,0:T(8,128)(2,1)S(1)}, bf16[6,32,1152]{2,1,0:T(8,128)(2,1)S(1)}, u32[]{:S(2)}, u32[]{:S(2)}) collective-permute-start(bf16[6,32,1152]{2,1,0:T(8,128)(2,1)S(1)} %get-tuple-element.25), channel_id=1, source_target_pairs={{0,16},{1,65},{2,18},{3,67},{4,20},{5,69},{6,22},{7,71},{8,24},{9,... | collective-permute-start | bytes 1327112 | tf_op jit(solution)/shard_map/ppermute | solution.py:29
  54.2 18.7 %copy-start.2 = (bf16[1152,1152]{1,0:T(8,128)(2,1)S(1)}, bf16[1152,1152]{1,0:T(8,128)(2,1)}, u32[]{:S(2)}) copy-start(bf16[1152,1152]{1,0:T(8,128)(2,1)} %d0.1) | copy-start | bytes 7962628
  61.3 6.5 %collective-permute-start.10 = (bf16[288,256]{1,0:T(8,128)(2,1)S(1)}, bf16[288,256]{1,0:T(8,128)(2,1)S(1)}, u32[]{:S(2)}, u32[]{:S(2)}) collective-permute-start(bf16[288,256]{1,0:T(8,128)(2,1)S(1)} %gate_up_silu.1.h0), channel_id=1, source_target_pairs={{0,6},{1,7},{2,0},{3,1},{4,2},{5,3},{6,4},{7,5},{8,14},{9,15},{10,... | collective-permute-start | bytes 442376 | tf_op jit(solution)/shard_map/ppermute | solution.py:29
  61.6 6.3 %collective-permute-start.11 = (bf16[288,256]{1,0:T(8,128)(2,1)S(1)}, bf16[288,256]{1,0:T(8,128)(2,1)S(1)}, u32[]{:S(2)}, u32[]{:S(2)}) collective-permute-start(bf16[288,256]{1,0:T(8,128)(2,1)S(1)} %gate_up_silu.1.h0), channel_id=1, source_target_pairs={{0,4},{1,5},{2,6},{3,7},{4,0},{5,1},{6,2},{7,3},{8,12},{9,13},{10,... | collective-permute-start | bytes 442376 | tf_op jit(solution)/shard_map/ppermute | solution.py:29
  62.2 10.7 %collective-permute-start.12 = (bf16[288,256]{1,0:T(8,128)(2,1)S(1)}, bf16[288,256]{1,0:T(8,128)(2,1)S(1)}, u32[]{:S(2)}, u32[]{:S(2)}) collective-permute-start(bf16[288,256]{1,0:T(8,128)(2,1)S(1)} %gate_up_silu.1.h0), channel_id=1, source_target_pairs={{0,2},{1,3},{2,4},{3,5},{4,6},{5,7},{6,0},{7,1},{8,10},{9,11},{10,... | collective-permute-start | bytes 442376 | tf_op jit(solution)/shard_map/ppermute | solution.py:29
  77.1 6.9 %collective-permute-start.14 = (bf16[2,64,1152]{2,1,0:T(8,128)(2,1)S(1)}, bf16[2,64,1152]{2,1,0:T(8,128)(2,1)S(1)}, u32[]{:S(2)}, u32[]{:S(2)}) collective-permute-start(bf16[2,64,1152]{2,1,0:T(8,128)(2,1)S(1)} %get-tuple-element.22), channel_id=1, source_target_pairs={{0,64},{1,17},{2,66},{3,19},{4,68},{5,21},{6,70},{7,23},{8,72},{9,... | collective-permute-start | bytes 884744 | tf_op jit(solution)/shard_map/ppermute | solution.py:29
  77.2 11.0 %collective-permute-start.15 = (bf16[2,64,1152]{2,1,0:T(8,128)(2,1)S(1)}, bf16[2,64,1152]{2,1,0:T(8,128)(2,1)S(1)}, u32[]{:S(2)}, u32[]{:S(2)}) collective-permute-start(bf16[2,64,1152]{2,1,0:T(8,128)(2,1)S(1)} %get-tuple-element.23), channel_id=1, source_target_pairs={{0,128},{1,33},{2,130},{3,35},{4,132},{5,37},{6,134},{7,39},{8,136... | collective-permute-start | bytes 884744 | tf_op jit(solution)/shard_map/ppermute | solution.py:29
  80.6 7.6 %collective-permute-start.16 = (bf16[2,64,1152]{2,1,0:T(8,128)(2,1)S(1)}, bf16[2,64,1152]{2,1,0:T(8,128)(2,1)S(1)}, u32[]{:S(2)}, u32[]{:S(2)}) collective-permute-start(bf16[2,64,1152]{2,1,0:T(8,128)(2,1)S(1)} %get-tuple-element.24), channel_id=1, source_target_pairs={{0,192},{1,49},{2,194},{3,51},{4,196},{5,53},{6,198},{7,55},{8,200... | collective-permute-start | bytes 884744 | tf_op jit(solution)/shard_map/ppermute | solution.py:29
  88.4 5.3 %collective-permute-start.17 = (bf16[2,16,1152]{2,1,0:T(8,128)(2,1)S(1)}, bf16[2,16,1152]{2,1,0:T(8,128)(2,1)S(1)}, u32[]{:S(2)}, u32[]{:S(2)}) collective-permute-start(bf16[2,16,1152]{2,1,0:T(8,128)(2,1)S(1)} %get-tuple-element.27), channel_id=1, source_target_pairs={{0,16},{1,65},{2,18},{3,67},{4,20},{5,69},{6,22},{7,71},{8,24},{9,... | collective-permute-start | bytes 221192 | tf_op jit(solution)/shard_map/ppermute | solution.py:29
  88.4 5.2 %collective-permute-start.18 = (bf16[2,16,1152]{2,1,0:T(8,128)(2,1)S(1)}, bf16[2,16,1152]{2,1,0:T(8,128)(2,1)S(1)}, u32[]{:S(2)}, u32[]{:S(2)}) collective-permute-start(bf16[2,16,1152]{2,1,0:T(8,128)(2,1)S(1)} %get-tuple-element.29), channel_id=1, source_target_pairs={{0,32},{1,129},{2,34},{3,131},{4,36},{5,133},{6,38},{7,135},{8,40}... | collective-permute-start | bytes 221192 | tf_op jit(solution)/shard_map/ppermute | solution.py:29
  89.8 4.4 %collective-permute-start.19 = (bf16[2,16,1152]{2,1,0:T(8,128)(2,1)S(1)}, bf16[2,16,1152]{2,1,0:T(8,128)(2,1)S(1)}, u32[]{:S(2)}, u32[]{:S(2)}) collective-permute-start(bf16[2,16,1152]{2,1,0:T(8,128)(2,1)S(1)} %get-tuple-element.28), channel_id=1, source_target_pairs={{0,48},{1,193},{2,50},{3,195},{4,52},{5,197},{6,54},{7,199},{8,56}... | collective-permute-start | bytes 221192 | tf_op jit(solution)/shard_map/ppermute | solution.py:29
  94.3 8.6 %collective-permute-start.20 = (f32[16,1152]{1,0:T(8,128)S(1)}, f32[16,1152]{1,0:T(8,128)S(1)}, u32[]{:S(2)}, u32[]{:S(2)}) collective-permute-start(f32[16,1152]{1,0:T(8,128)S(1)} %slice_bitcast_fusion.2), channel_id=1, source_target_pairs={{0,1},{1,0},{2,3},{3,2},{4,5},{5,4},{6,7},{7,6},{8,9},{9,8},{10,11... | collective-permute-start | bytes 221192 | tf_op jit(solution)/shard_map/ppermute | solution.py:29
  102.9 7.3 %collective-permute-start.21 = (f32[2,8,1152]{2,1,0:T(8,128)S(1)}, f32[2,8,1152]{2,1,0:T(8,128)S(1)}, u32[]{:S(2)}, u32[]{:S(2)}) collective-permute-start(f32[2,8,1152]{2,1,0:T(8,128)S(1)} %fusion.6), channel_id=1, source_target_pairs={{0,8},{1,9},{2,10},{3,11},{4,12},{5,13},{6,14},{7,15},{8,0},{9,1},... | collective-permute-start | bytes 221192 | tf_op jit(solution)/shard_map/ppermute | solution.py:29

commit v3 on v0

v3 whole, which is shorter than its diff:
```python
import jax
import jax.numpy as jnp
import numpy as np
from jax import lax
from jax.experimental import pallas as pl
from jax.experimental.pallas import tpu as pltpu
from jax.sharding import Mesh, PartitionSpec as P

AXES = ("x", "y", "h", "l", "c")
SIZES = (4, 4, 2, 4, 2)
F32 = jnp.float32
BF16 = jnp.bfloat16
MIB = 1 << 20


def _perm(move):
    pairs = []
    for source in range(256):
        x, y, h, l, c = (int(i) for i in np.unravel_index(source, SIZES))
        X, Y, Z, C = move(x, y, h * 4 + l, c)
        Z %= 8
        pairs.append((source, int(np.ravel_multi_index((X % 4, Y % 4, Z // 4, Z % 4, C % 2), SIZES))))
    return pairs


def _permute(a, move):
    return lax.ppermute(a, AXES, _perm(move))


def _first(k):
    return lambda x, y, z, c: (x + k, y, z, c) if c == 0 else (x, y + k, z, c)


def _second(k):
    return lambda x, y, z, c: (x, y + k, z, c) if c == 0 else (x + k, y, z, c)


def _swap(x, y, z, c):
    return (x, y, z, 1 - c)


def _z(k):
    return lambda x, y, z, c: (x, y, z + k, c)


def _z_two(x, y, z, c):
    return (x, y, z + 2 if z % 2 == 0 else z - 2, c)


def _lo(k):
    return lambda x, y, z, c: (x, y, (z // 4) * 4 + (z % 4 + k) % 4, c)


def _only(core, move):
    return [(s, d) for s, d in _perm(move) if s % 2 == core]


VMEM = pl.BlockSpec(memory_space=pltpu.VMEM)
NT = (((1,), (1,)), ((), ()))


def _place():
    return [lax.axis_index(a).astype(jnp.int32) for a in AXES]


def _along(core, x, y):
    return jnp.where(core == 0, x, y), jnp.where(core == 0, y, x)


def _order_kernel(tokens, mine, theirs):
    x, y, _, _, c = _place()
    for core, out in ((c, mine), (1 - c, theirs)):
        first, second = _along(core, x, y)
        for half, q in enumerate((first + 2 * second, 2 * first + second)):
            for i in range(4):
                a = lax.rem(q + i, 4)
                base = 64 + half * 96 + (i - 1) * 32 if i else half * 32
                for j in range(2):
                    b = 2 * half + j
                    block = jnp.where(core == 0, a * 4 + b, b * 4 + a)
                    row = pl.multiple_of(block * 16, 16)
                    out[pl.ds(base + j * 16, 16), :] = tokens[core, pl.ds(row, 16), :]


def _order(tokens):
    _, rows, width = tokens.shape
    shape = jax.ShapeDtypeStruct((rows, width), BF16)
    return pl.pallas_call(
        _order_kernel,
        in_specs=[VMEM],
        out_specs=[VMEM] * 2,
        out_shape=[shape, shape],
        compiler_params=pltpu.CompilerParams(vmem_limit_bytes=8 * MIB),
        name="order_rows",
    )(tokens)


def _weight_columns(weights, block, width):
    column = pl.multiple_of(block * width, 128)
    return jnp.concatenate([w[:, pl.ds(column, width)] for w in weights], axis=0)


def _own_kernel(mine, other, g0, g1, u0, u1, out):
    _, _, _, l, c = _place()
    width = mine.shape[1]
    for k, own in enumerate((mine, other)):
        w = _weight_columns((g0, g1, u0, u1), 2 * l + (c if k == 0 else 1 - c), width)
        t = jnp.concatenate([own[:32], own[64:160], own[32:64], own[160:]], axis=0)
        part = lax.dot_general(w, t, NT, preferred_element_type=F32)
        if k == 0:
            out[...] = part
        else:
            out[...] += part


def _own(mine, other, weights):
    units, (rows, width) = weights[0].shape[0], mine.shape
    return pl.pallas_call(
        _own_kernel,
        in_specs=[VMEM] * 6,
        out_specs=VMEM,
        out_shape=jax.ShapeDtypeStruct((4 * units, rows), F32),
        compiler_params=pltpu.CompilerParams(vmem_limit_bytes=16 * MIB),
        cost_estimate=pl.CostEstimate(
            flops=2 * 8 * units * rows * width, bytes_accessed=20 * units * width, transcendentals=0
        ),
        name="own_features",
    )(mine, other, *weights)


def _pack_kernel(p0, p1, p2, first_back, first_on, second_back, second_on):
    for i, piece in enumerate((p0, p1, p2)):
        for j in range(2):
            k = 2 * i + j
            a, b = piece[j, :32], piece[j, 32:]
            first_back[k] = jnp.concatenate([a, b[:16]], axis=0)
            first_on[k] = jnp.concatenate([a, b[16:]], axis=0)
            second_back[k] = jnp.concatenate([a[:16], b], axis=0)
            second_on[k] = jnp.concatenate([a[16:], b], axis=0)


def _pack(pieces):
    send = jax.ShapeDtypeStruct((6, 48, pieces[0].shape[-1]), BF16)
    return pl.pallas_call(
        _pack_kernel,
        in_specs=[VMEM] * 3,
        out_specs=[VMEM] * 4,
        out_shape=[send] * 4,
        compiler_params=pltpu.CompilerParams(vmem_limit_bytes=16 * MIB),
        name="pack_quarters",
    )(*pieces)


def _hidden_kernel(z0, z1, z2, p1, m1, p2, m2, start, g0, g1, u0, u1, out, acc):
    x, y, _, l, c = _place()
    first, second = _along(c, x, y)
    width = z0.shape[-1]
    units = g0.shape[0]
    for k in range(6):
        block = 2 * lax.rem(l + 1 + k // 2, 4) + (c if k % 2 == 0 else 1 - c)
        w = _weight_columns((g0, g1, u0, u1), block, width)
        kept = (z0, z1, z2)[k // 2][k % 2]
        t = jnp.concatenate(
            [
                kept[:32],
                p1[k, :32],
                p2[k, :16],
                m2[k, :16],
                m1[k, :32],
                kept[32:],
                p2[k, 16:],
                p1[k, 32:],
                m1[k, 32:],
                m2[k, 16:],
            ],
            axis=0,
        )
        part = lax.dot_general(w, t, NT, preferred_element_type=F32)
        if k == 0:
            acc[...] = start[...] + part
        else:
            acc[...] += part
    gate = acc[pl.ds(0, 2 * units), :]
    up = acc[pl.ds(2 * units, 2 * units), :]
    hidden = gate / (1 + jnp.exp(-gate)) * up
    half = hidden.shape[1] // 2
    group = half // 4
    turns = (2 * lax.rem(second, 2), lax.rem(first + second, 4))
    for i, turn in enumerate(turns):
        part = pltpu.roll(hidden[:, i * half : (i + 1) * half], turn * group, 1)
        out[:, i * half : (i + 1) * half] = part.astype(BF16)


def _hidden(kept, around, start, weights):
    units, width = weights[0].shape[0], kept[0].shape[-1]
    rows = start.shape[1]
    return pl.pallas_call(
        _hidden_kernel,
        in_specs=[VMEM] * 12,
        out_specs=VMEM,
        out_shape=jax.ShapeDtypeStruct((2 * units, rows), BF16),
        scratch_shapes=[pltpu.VMEM((4 * units, rows), F32)],
        compiler_params=pltpu.CompilerParams(vmem_limit_bytes=24 * MIB),
        cost_estimate=pl.CostEstimate(
            flops=2 * 24 * units * rows * width,
            bytes_accessed=48 * units * width,
            transcendentals=2 * units * rows,
        ),
        name="gate_up_silu",
    )(*kept, *around, start, *weights)


def _down_kernel(h0, h1, h2, h3, d0, d1, own, s1, s2, s3, ht):
    _, _, _, l, c = _place()
    units = h0.shape[0] // 2
    for k, part in enumerate((h0, h1, h2, h3)):
        base = lax.rem(l + k, 4) * (2 * units)
        for i, core in enumerate((c, 1 - c)):
            row = pl.multiple_of(base + core * units, 16)
            ht[pl.ds(row, units), :] = part[pl.ds(i * units, units), :]
    hidden = ht[...].T
    half = hidden.shape[0] // 2
    group = half // 4
    for i, d in enumerate((d0, d1)):
        result = jnp.dot(hidden, d[...], preferred_element_type=F32)
        for k, out in enumerate((own, s1, s2, s3)):
            for j in range(2):
                rows = result[j * half + k * group : j * half + (k + 1) * group]
                out[i, j * group : (j + 1) * group, :] = rows.astype(out.dtype)


def _down(hs, d0, d1):
    rows = hs[0].shape[1]
    depth, width = d0.shape
    block = rows // 4
    send = jax.ShapeDtypeStruct((2, block, width), BF16)
    return pl.pallas_call(
        _down_kernel,
        in_specs=[VMEM] * 6,
        out_specs=[VMEM] * 4,
        out_shape=[jax.ShapeDtypeStruct((2, block, width), F32), send, send, send],
        scratch_shapes=[pltpu.VMEM((depth, rows), BF16)],
        compiler_params=pltpu.CompilerParams(vmem_limit_bytes=24 * MIB),
        cost_estimate=pl.CostEstimate(
            flops=4 * rows * depth * width, bytes_accessed=4 * depth * width, transcendentals=0
        ),
        name="down",
    )(*hs, d0, d1)


def _sum_first_kernel(own, g1, g2, g3, kept, s1, s2, s3):
    x, y, _, _, c = _place()
    _, second = _along(c, x, y)
    for k, out in enumerate((kept, s1, s2, s3)):
        rows = pl.ds(pl.multiple_of(lax.rem(second + k, 4) * 16, 16), 16)
        total = own[:, rows, :]
        for g in (g1, g2, g3):
            total = total + g[:, rows, :].astype(F32)
        out[...] = total.astype(out.dtype)


def _sum_first(own, got):
    width = own.shape[-1]
    send = jax.ShapeDtypeStruct((2, 16, width), BF16)
    return pl.pallas_call(
        _sum_first_kernel,
        in_specs=[VMEM] * 4,
        out_specs=[VMEM] * 4,
        out_shape=[jax.ShapeDtypeStruct((2, 16, width), F32), send, send, send],
        compiler_params=pltpu.CompilerParams(vmem_limit_bytes=8 * MIB),
        name="sum_first",
    )(own, *got)


def _sum_second_kernel(own, g1, g2, g3, here, there):
    _, _, h, _, _ = _place()
    total = own[...]
    for g in (g1, g2, g3):
        total = total + g[...].astype(F32)
    low, high = total[:, :8], total[:, 8:]
    here[...] = jnp.where(h == 0, low, high)
    send = jnp.where(h == 0, high, low)
    there[...] = jnp.concatenate([send[0], send[1]], axis=0).astype(BF16)


def _sum_second(own, got):
    width = own.shape[-1]
    return pl.pallas_call(
        _sum_second_kernel,
        in_specs=[VMEM] * 4,
        out_specs=[VMEM] * 2,
        out_shape=[jax.ShapeDtypeStruct((2, 8, width), F32), jax.ShapeDtypeStruct((16, width), BF16)],
        compiler_params=pltpu.CompilerParams(vmem_limit_bytes=8 * MIB),
        name="sum_second",
    )(own, *got)


def _sum_last_kernel(here, got, own, cross):
    total = got[...].astype(F32)
    own[...] = here[0] + total[:8]
    cross[...] = here[1] + total[8:]


def _sum_last(here, got):
    part = jax.ShapeDtypeStruct((8, got.shape[-1]), F32)
    return pl.pallas_call(
        _sum_last_kernel,
        in_specs=[VMEM] * 2,
        out_specs=[VMEM] * 2,
        out_shape=[part, part],
        compiler_params=pltpu.CompilerParams(vmem_limit_bytes=8 * MIB),
        name="sum_last",
    )(here, got)


def local(tokens, gate_weight, up_weight, down_weight):
    core = lax.axis_index("c")
    mine, theirs = _order(tokens)
    other = _permute(theirs, _swap)
    quarter = jnp.stack([mine[:64], other[:64]])
    kept = [_permute(quarter, m) for m in (_z(-1), _z_two, _z(1))]
    gate_in, up_in, _ = lax.optimization_barrier((gate_weight, up_weight, other))
    gate_other = _permute(gate_in, _swap)
    up_other = _permute(up_in, _swap)
    weights = (gate_weight, gate_other, up_weight, up_other)

    packed = _pack(kept)
    packed, gate_other, up_other = lax.optimization_barrier((packed, gate_other, up_other))
    down_in, _ = lax.optimization_barrier((down_weight, packed))
    down_other = _permute(down_in, _swap)
    first_back, first_on, second_back, second_on = packed
    around = [
        _permute(first_back, _first(-1)),
        _permute(first_on, _first(1)),
        _permute(second_back, _second(-1)),
        _permute(second_on, _second(1)),
    ]
    mine, _ = lax.optimization_barrier((mine, packed))
    start = _own(mine, other, weights)

    hidden = _hidden(kept, around, start, weights)
    two, one, three = (_permute(hidden, _lo(-k)) for k in (2, 1, 3))

    own, *sends = _down((hidden, one, two, three), down_weight, down_other)
    own, *sends = _sum_first(own, [_permute(sends[k - 1], _first(k)) for k in (2, 1, 3)])
    here, there = _sum_second(own, [_permute(sends[k - 1], _second(k)) for k in (2, 1, 3)])
    own, cross = _sum_last(here, _permute(there, _z(4)))
    cross = _permute(cross, _swap)
    mine = lax.broadcasted_iota(jnp.int32, (2, 1, 1), 0) == core
    return jnp.where(mine, own[None], cross[None]).astype(BF16)


def solution(mesh):
    fine = Mesh(mesh.devices.reshape(SIZES), AXES)
    wide, narrow = ("x", "y", "h"), ("l", "c")
    return jax.shard_map(
        local,
        mesh=fine,
        in_specs=(
            P(None, None, narrow),
            P(wide + narrow, None),
            P(wide + narrow, None),
            P(wide, narrow),
        ),
        out_specs=P(None, wide, narrow),
        check_vma=False,
    )
```

time: 434 us -> 98.2 us (0.23)
  waiting for transfers between devices: 403 us -> 49.7 us
  starting transfers between devices: 0.08 us -> 37.3 us
  matrix products: 15.7 us -> 0 us
  between operations: 13.1 us -> 0.13 us
  Pallas kernels: 0 us -> 5.92 us
    reduce_scatter x1 -> x0, waiting for transfers between devices: 259 us -> none  [local(): lax.psum_scatter(jnp.einsum('brf,fd->rbd', hidden_all, down_weight, prefe...]
    all_gather x2 -> x0, waiting for transfers between devices: 143 us -> none  [the longest x1 107 us: local(): piece = lax.all_gather(tokens, 'narrow', axis=2, tiled=True)]
    ppermute x0 -> x22, waiting for transfers between devices: none -> 49.7 us  [_permute(): return lax.ppermute(a, AXES, _perm(move))]
    ppermute x0 -> x22, starting transfers between devices: none -> 37.3 us  [_permute(): return lax.ppermute(a, AXES, _perm(move))]
    dot_general x3 -> x0, matrix products: 15.7 us -> none  [the longest x1 7.86 us: local(): jnp.einsum('bk,fk->bf', flat_rows, gate_weight, preferred_element_type=jn...]
    pallas_call x0 -> x8, Pallas kernels: none -> 5.92 us  [the longest x1 2.57 us: _hidden(): pl.pallas_call(_hidden_kernel, in_specs=[VMEM] * 12, out_specs=VMEM, out_...]
  transfers between devices with their start and end apart: 3 -> 22, of which waited for: 3 -> 16; matrix products, arithmetic and copies ran while one was open for 0% -> 0% of each run, Pallas kernels for 0% -> 4%
where the time goes in v3:
time: 98.2 us; the launch traced here: 97 us
  waiting for transfers between devices  49.7 us (51%)
  starting transfers between devices  37.3 us (38%)
  Pallas kernels  5.92 us (6%)
  local copies, waits for them, and re-layouts  3.21 us (3%)
    ppermute x22, waiting for transfers between devices, _permute(): return lax.ppermute(a, AXES, _perm(move))  49.7 us
    ppermute x22, starting transfers between devices, _permute(): return lax.ppermute(a, AXES, _perm(move))  37.3 us
    unnamed x10, local copies, waits for them, and re-layouts  3.18 us
    pallas_call x1, Pallas kernels, _hidden(): pl.pallas_call(_hidden_kernel, in_specs=[VMEM] * 12, out_specs=VMEM, out_...  2.57 us
  transfers between devices with their start and end apart: 22, of which 16 were waited for; matrix products, arithmetic and copies ran while one was open for 0% of the time, Pallas kernels for 4%

profile of v3, /device:TPU:1, one launch (start us, length us, event | category | flops | bytes accessed | tf_op | source)
XLA Modules:
  0.0 97.0 jit_solution(9301064240095909178)
XLA Ops:
  0.0 0.0 copy-start
  0.0 0.0 copy-start.4
  0.0 1.4 %copy-done.4 = bf16[2,256,1152]{2,1,0:T(8,128)(2,1)S(1)} copy-done((bf16[2,256,1152]{2,1,0:T(8,128)(2,1)S(1)}, bf16[2,256,1152]{2,1,0:T(8,128)(2,1)}, u32[]{:S(2)}) %copy-start.4) | copy-done | bytes 1179672
  1.4 0.1 order_rows.1
  1.5 3.3 %collective-permute-start = (bf16[256,1152]{1,0:T(8,128)(2,1)S(1)}, bf16[256,1152]{1,0:T(8,128)(2,1)S(1)}, u32[]{:S(2)}, u32[]{:S(2)}) collective-permute-start(bf16[256,1152]{1,0:T(8,128)(2,1)S(1)} %get-tuple-element.32), channel_id=1, source_target_pairs={{0,1},{1,0},{2,3},{3,2},{4,5},{5,4},{6,7},{7,6},{8,9},{9,8},{10,11... | collective-permute-start | bytes 1769480 | tf_op jit(solution)/shard_map/ppermute | solution.py:27
  4.9 1.6 %collective-permute-done.other = bf16[256,1152]{1,0:T(8,128)(2,1)S(1)} collective-permute-done((bf16[256,1152]{1,0:T(8,128)(2,1)S(1)}, bf16[256,1152]{1,0:T(8,128)(2,1)S(1)}, u32[]{:S(2)}, u32[]{:S(2)}) %collective-permute-start) | collective-permute-done | bytes 589856 | tf_op jit(solution)/shard_map/ppermute | solution.py:27
  6.5 0.4 collective-permute-start.4
  6.9 0.1 collective-permute-start.5
  7.1 0.1 collective-permute-start.3
  7.2 2.9 %collective-permute-start.2 = (bf16[2,64,1152]{2,1,0:T(8,128)(2,1)S(1)}, bf16[2,64,1152]{2,1,0:T(8,128)(2,1)S(1)}, u32[]{:S(2)}, u32[]{:S(2)}) collective-permute-start(bf16[2,64,1152]{2,1,0:T(8,128)(2,1)S(1)} %pad_maximum_fusion), channel_id=1, source_target_pairs={{0,4},{1,5},{2,14},{3,15},{4,8},{5,9},{6,2},{7,3},{8,12},{9,13},{1... | collective-permute-start | bytes 884744 | tf_op jit(solution)/shard_map/ppermute | solution.py:27
  10.1 2.9 %collective-permute-start.1 = (bf16[2,64,1152]{2,1,0:T(8,128)(2,1)S(1)}, bf16[2,64,1152]{2,1,0:T(8,128)(2,1)S(1)}, u32[]{:S(2)}, u32[]{:S(2)}) collective-permute-start(bf16[2,64,1152]{2,1,0:T(8,128)(2,1)S(1)} %pad_maximum_fusion), channel_id=1, source_target_pairs={{0,14},{1,15},{2,0},{3,1},{4,2},{5,3},{6,4},{7,5},{8,6},{9,7},{10,... | collective-permute-start | bytes 884744 | tf_op jit(solution)/shard_map/ppermute | solution.py:27
  12.9 5.2 %collective-permute-done.3.p2.z2 = bf16[2,64,1152]{2,1,0:T(8,128)(2,1)S(1)} collective-permute-done((bf16[2,64,1152]{2,1,0:T(8,128)(2,1)S(1)}, bf16[2,64,1152]{2,1,0:T(8,128)(2,1)S(1)}, u32[]{:S(2)}, u32[]{:S(2)}) %collective-permute-start.3) | collective-permute-done | bytes 294944 | tf_op jit(solution)/shard_map/ppermute | solution.py:27
  18.1 7.2 %collective-permute-done.2.p1.z1 = bf16[2,64,1152]{2,1,0:T(8,128)(2,1)S(1)} collective-permute-done((bf16[2,64,1152]{2,1,0:T(8,128)(2,1)S(1)}, bf16[2,64,1152]{2,1,0:T(8,128)(2,1)S(1)}, u32[]{:S(2)}, u32[]{:S(2)}) %collective-permute-start.2) | collective-permute-done | bytes 294944 | tf_op jit(solution)/shard_map/ppermute | solution.py:27
  25.3 0.1 collective-permute-done.1.p0.z0
  25.4 0.2 pack_quarters.1
  25.6 0.0 collective-permute-done.4.g1
  25.6 0.0 collective-permute-done.5.u1
  25.6 1.3 %collective-permute-start.13 = (bf16[1152,1152]{1,0:T(8,128)(2,1)}, bf16[1152,1152]{1,0:T(8,128)(2,1)S(1)}, u32[]{:S(2)}, u32[]{:S(2)}) collective-permute-start(bf16[1152,1152]{1,0:T(8,128)(2,1)} %d0.1), channel_id=1, source_target_pairs={{0,1},{1,0},{2,3},{3,2},{4,5},{5,4},{6,7},{7,6},{8,9},{9,8},{10,11... | collective-permute-start | bytes 7962632 | tf_op jit(solution)/shard_map/ppermute | solution.py:27
  26.9 2.7 %collective-permute-start.6 = (bf16[6,48,1152]{2,1,0:T(8,128)(2,1)S(1)}, bf16[6,48,1152]{2,1,0:T(8,128)(2,1)S(1)}, u32[]{:S(2)}, u32[]{:S(2)}) collective-permute-start(bf16[6,48,1152]{2,1,0:T(8,128)(2,1)S(1)} %get-tuple-element.39), channel_id=1, source_target_pairs={{0,192},{1,49},{2,194},{3,51},{4,196},{5,53},{6,198},{7,55},{8,200... | collective-permute-start | bytes 1990664 | tf_op jit(solution)/shard_map/ppermute | solution.py:27
  29.6 0.0 collective-permute-start.7
  29.6 2.5 %collective-permute-start.8 = (bf16[6,48,1152]{2,1,0:T(8,128)(2,1)S(1)}, bf16[6,48,1152]{2,1,0:T(8,128)(2,1)S(1)}, u32[]{:S(2)}, u32[]{:S(2)}) collective-permute-start(bf16[6,48,1152]{2,1,0:T(8,128)(2,1)S(1)} %get-tuple-element.41), channel_id=1, source_target_pairs={{0,48},{1,193},{2,50},{3,195},{4,52},{5,197},{6,54},{7,199},{8,56}... | collective-permute-start | bytes 1990664 | tf_op jit(solution)/shard_map/ppermute | solution.py:27
  32.1 0.0 collective-permute-start.9
  32.1 0.0 copy-done
  32.1 0.0 copy-start.1
  32.1 1.7 %copy-done.1 = bf16[144,9216]{1,0:T(8,128)(2,1)S(1)} copy-done((bf16[144,9216]{1,0:T(8,128)(2,1)S(1)}, bf16[144,9216]{1,0:T(8,128)(2,1)}, u32[]{:S(2)}) %copy-start.1) | copy-done | bytes 2654232
  33.9 0.0 copy-start.2
  33.9 0.9 own_features.1.start
  34.8 0.0 copy-start.3
  34.8 6.1 %collective-permute-done.6.p1 = bf16[6,48,1152]{2,1,0:T(8,128)(2,1)S(1)} collective-permute-done((bf16[6,48,1152]{2,1,0:T(8,128)(2,1)S(1)}, bf16[6,48,1152]{2,1,0:T(8,128)(2,1)S(1)}, u32[]{:S(2)}, u32[]{:S(2)}) %collective-permute-start.6) | collective-permute-done | bytes 663584 | tf_op jit(solution)/shard_map/ppermute | solution.py:27
  41.0 3.1 %collective-permute-done.7.m1 = bf16[6,48,1152]{2,1,0:T(8,128)(2,1)S(1)} collective-permute-done((bf16[6,48,1152]{2,1,0:T(8,128)(2,1)S(1)}, bf16[6,48,1152]{2,1,0:T(8,128)(2,1)S(1)}, u32[]{:S(2)}, u32[]{:S(2)}) %collective-permute-start.7) | collective-permute-done | bytes 663584 | tf_op jit(solution)/shard_map/ppermute | solution.py:27
  44.1 0.6 collective-permute-done.8.p2
  44.7 3.4 %collective-permute-done.9.m2 = bf16[6,48,1152]{2,1,0:T(8,128)(2,1)S(1)} collective-permute-done((bf16[6,48,1152]{2,1,0:T(8,128)(2,1)S(1)}, bf16[6,48,1152]{2,1,0:T(8,128)(2,1)S(1)}, u32[]{:S(2)}, u32[]{:S(2)}) %collective-permute-start.9) | collective-permute-done | bytes 663584 | tf_op jit(solution)/shard_map/ppermute | solution.py:27
  48.1 0.0 copy-done.2
  48.1 2.6 %gate_up_silu.1.h0 = bf16[288,256]{1,0:T(8,128)(2,1)S(1)} custom-call(bf16[2,64,1152]{2,1,0:T(8,128)(2,1)S(1)} %collective-permute-done.1.p0.z0, bf16[2,64,1152]{2,1,0:T(8,128)(2,1)S(1)} %collective-permute-done.2.p1.z1, bf16[2,64,1152]{2,1,0:T(8,128)(2,1)S(1)} %collective-permute-done.3.p2.z2, bf16[6,48,1152]{2,1,0:T(8,128)(2,1)S(1)} %collective-permute-done.6.p1, ...), custom_call_target="tpu_custom_call" | custom-call | flops 2038431744 | bytes 7962624 | tf_op jit(solution)/shard_map/gate_up_silu/pallas_call | solution.py:197
  50.6 0.7 collective-permute-start.12
  51.3 2.7 %collective-permute-start.11 = (bf16[288,256]{1,0:T(8,128)(2,1)S(1)}, bf16[288,256]{1,0:T(8,128)(2,1)S(1)}, u32[]{:S(2)}, u32[]{:S(2)}) collective-permute-start(bf16[288,256]{1,0:T(8,128)(2,1)S(1)} %gate_up_silu.1.h0), channel_id=1, source_target_pairs={{0,4},{1,5},{2,6},{3,7},{4,0},{5,1},{6,2},{7,3},{8,12},{9,13},{10,... | collective-permute-start | bytes 442376 | tf_op jit(solution)/shard_map/ppermute | solution.py:27
  54.0 0.1 collective-permute-start.10
  54.1 3.8 %collective-permute-done.12.h3 = bf16[288,256]{1,0:T(8,128)(2,1)S(1)} collective-permute-done((bf16[288,256]{1,0:T(8,128)(2,1)S(1)}, bf16[288,256]{1,0:T(8,128)(2,1)S(1)}, u32[]{:S(2)}, u32[]{:S(2)}) %collective-permute-start.12) | collective-permute-done | bytes 147488 | tf_op jit(solution)/shard_map/ppermute | solution.py:27
  57.9 6.8 %collective-permute-done.11.h2 = bf16[288,256]{1,0:T(8,128)(2,1)S(1)} collective-permute-done((bf16[288,256]{1,0:T(8,128)(2,1)S(1)}, bf16[288,256]{1,0:T(8,128)(2,1)S(1)}, u32[]{:S(2)}, u32[]{:S(2)}) %collective-permute-start.11) | collective-permute-done | bytes 147488 | tf_op jit(solution)/shard_map/ppermute | solution.py:27
  64.6 0.0 collective-permute-done.10.h1
  64.7 0.0 collective-permute-done.13.d1
  64.7 0.0 copy-done.3
  64.7 1.9 %down.1 = (f32[2,64,1152]{2,1,0:T(8,128)S(1)}, bf16[2,64,1152]{2,1,0:T(8,128)(2,1)S(1)}, bf16[2,64,1152]{2,1,0:T(8,128)(2,1)S(1)}, bf16[2,64,1152]{2,1,0:T(8,128)(2,1)S(1)}) custom-call(bf16[288,256]{1,0:T(8,128)(2,1)S(1)} %gate_up_silu.1.h0, bf16[288,256]{1,0:T(8,128)(2,1)S(1)} %collective-permute-done.10.h1, ...), custom_call_target="tpu_custom_call" | custom-call | flops 1358954496 | bytes 5308416 | tf_op jit(solution)/shard_map/down/pallas_call | solution.py:237
  66.6 3.0 %collective-permute-start.14 = (bf16[2,64,1152]{2,1,0:T(8,128)(2,1)S(1)}, bf16[2,64,1152]{2,1,0:T(8,128)(2,1)S(1)}, u32[]{:S(2)}, u32[]{:S(2)}) collective-permute-start(bf16[2,64,1152]{2,1,0:T(8,128)(2,1)S(1)} %get-tuple-element.46), channel_id=1, source_target_pairs={{0,128},{1,33},{2,130},{3,35},{4,132},{5,37},{6,134},{7,39},{8,136... | collective-permute-start | bytes 884744 | tf_op jit(solution)/shard_map/ppermute | solution.py:27
  69.6 0.0 collective-permute-start.15
  69.6 2.7 %collective-permute-start.16 = (bf16[2,64,1152]{2,1,0:T(8,128)(2,1)S(1)}, bf16[2,64,1152]{2,1,0:T(8,128)(2,1)S(1)}, u32[]{:S(2)}, u32[]{:S(2)}) collective-permute-start(bf16[2,64,1152]{2,1,0:T(8,128)(2,1)S(1)} %get-tuple-element.48), channel_id=1, source_target_pairs={{0,192},{1,49},{2,194},{3,51},{4,196},{5,53},{6,198},{7,55},{8,200... | collective-permute-start | bytes 884744 | tf_op jit(solution)/shard_map/ppermute | solution.py:27
  72.3 1.8 %collective-permute-done.14.g1 = bf16[2,64,1152]{2,1,0:T(8,128)(2,1)S(1)} collective-permute-done((bf16[2,64,1152]{2,1,0:T(8,128)(2,1)S(1)}, bf16[2,64,1152]{2,1,0:T(8,128)(2,1)S(1)}, u32[]{:S(2)}, u32[]{:S(2)}) %collective-permute-start.14) | collective-permute-done | bytes 294944 | tf_op jit(solution)/shard_map/ppermute | solution.py:27
  74.0 3.2 %collective-permute-done.15.g2 = bf16[2,64,1152]{2,1,0:T(8,128)(2,1)S(1)} collective-permute-done((bf16[2,64,1152]{2,1,0:T(8,128)(2,1)S(1)}, bf16[2,64,1152]{2,1,0:T(8,128)(2,1)S(1)}, u32[]{:S(2)}, u32[]{:S(2)}) %collective-permute-start.15) | collective-permute-done | bytes 294944 | tf_op jit(solution)/shard_map/ppermute | solution.py:27
  77.2 0.0 collective-permute-done.16.g3
  77.2 0.1 sum_first.1
  77.3 0.1 collective-permute-start.17
  77.4 0.6 collective-permute-start.18
  78.1 2.1 %collective-permute-start.19 = (bf16[2,16,1152]{2,1,0:T(8,128)(2,1)S(1)}, bf16[2,16,1152]{2,1,0:T(8,128)(2,1)S(1)}, u32[]{:S(2)}, u32[]{:S(2)}) collective-permute-start(bf16[2,16,1152]{2,1,0:T(8,128)(2,1)S(1)} %get-tuple-element.52), channel_id=1, source_target_pairs={{0,48},{1,193},{2,50},{3,195},{4,52},{5,197},{6,54},{7,199},{8,56}... | collective-permute-start | bytes 221192 | tf_op jit(solution)/shard_map/ppermute | solution.py:27
  80.2 2.0 %collective-permute-done.17.g1 = bf16[2,16,1152]{2,1,0:T(8,128)(2,1)S(1)} collective-permute-done((bf16[2,16,1152]{2,1,0:T(8,128)(2,1)S(1)}, bf16[2,16,1152]{2,1,0:T(8,128)(2,1)S(1)}, u32[]{:S(2)}, u32[]{:S(2)}) %collective-permute-start.17) | collective-permute-done | bytes 73760 | tf_op jit(solution)/shard_map/ppermute | solution.py:27
  82.2 0.5 collective-permute-done.18.g2
  82.7 0.0 collective-permute-done.19.g3
  82.8 3.3 %collective-permute-start.20 = (bf16[16,1152]{1,0:T(8,128)(2,1)S(1)}, bf16[16,1152]{1,0:T(8,128)(2,1)S(1)}, u32[]{:S(2)}, u32[]{:S(2)}) collective-permute-start(bf16[16,1152]{1,0:T(8,128)(2,1)S(1)} %get-tuple-element.54), channel_id=1, source_target_pairs={{0,8},{1,9},{2,10},{3,11},{4,12},{5,13},{6,14},{7,15},{8,0},{9,1},... | collective-permute-start | bytes 110600 | tf_op jit(solution)/shard_map/ppermute | solution.py:27
  86.1 3.5 %collective-permute-done.20.got = bf16[16,1152]{1,0:T(8,128)(2,1)S(1)} collective-permute-done((bf16[16,1152]{1,0:T(8,128)(2,1)S(1)}, bf16[16,1152]{1,0:T(8,128)(2,1)S(1)}, u32[]{:S(2)}, u32[]{:S(2)}) %collective-permute-start.20) | collective-permute-done | bytes 36896 | tf_op jit(solution)/shard_map/ppermute | solution.py:27
  89.6 5.9 %collective-permute-start.21 = (bf16[8,1152]{1,0:T(8,128)(2,1)S(1)}, bf16[8,1152]{1,0:T(8,128)(2,1)S(1)}, u32[]{:S(2)}, u32[]{:S(2)}) collective-permute-start(bf16[8,1152]{1,0:T(8,128)(2,1)S(1)} %convert), channel_id=1, source_target_pairs={{0,1},{1,0},{2,3},{3,2},{4,5},{5,4},{6,7},{7,6},{8,9},{9,8},{10,11... | collective-permute-start | bytes 55304 | tf_op jit(solution)/shard_map/ppermute | solution.py:27
  95.5 0.8 collective-permute-done.21
  96.3 0.7 select_convert_fusion
  (7 shorter events, 0.1 us)
Async XLA Ops:
  0.0 32.1 %copy-start = (bf16[144,9216]{1,0:T(8,128)(2,1)S(1)}, bf16[144,9216]{1,0:T(8,128)(2,1)}, u32[]{:S(2)}) copy-start(bf16[144,9216]{1,0:T(8,128)(2,1)} %g0.3) | copy-start | bytes 7962628
  0.0 1.4 %copy-start.4 = (bf16[2,256,1152]{2,1,0:T(8,128)(2,1)S(1)}, bf16[2,256,1152]{2,1,0:T(8,128)(2,1)}, u32[]{:S(2)}) copy-start(bf16[2,256,1152]{2,1,0:T(8,128)(2,1)} %tokens.1) | copy-start | bytes 3538948
  1.5 5.0 %collective-permute-start = (bf16[256,1152]{1,0:T(8,128)(2,1)S(1)}, bf16[256,1152]{1,0:T(8,128)(2,1)S(1)}, u32[]{:S(2)}, u32[]{:S(2)}) collective-permute-start(bf16[256,1152]{1,0:T(8,128)(2,1)S(1)} %get-tuple-element.32), channel_id=1, source_target_pairs={{0,1},{1,0},{2,3},{3,2},{4,5},{5,4},{6,7},{7,6},{8,9},{9,8},{10,11... | collective-permute-start | bytes 1769480 | tf_op jit(solution)/shard_map/ppermute | solution.py:27
  6.5 19.1 %collective-permute-start.4 = (bf16[144,9216]{1,0:T(8,128)(2,1)}, bf16[144,9216]{1,0:T(8,128)(2,1)S(1)}, u32[]{:S(2)}, u32[]{:S(2)}) collective-permute-start(bf16[144,9216]{1,0:T(8,128)(2,1)} %g0.3), channel_id=1, source_target_pairs={{0,1},{1,0},{2,3},{3,2},{4,5},{5,4},{6,7},{7,6},{8,9},{9,8},{10,11... | collective-permute-start | bytes 7962632 | tf_op jit(solution)/shard_map/ppermute | solution.py:27
  6.9 18.7 %collective-permute-start.5 = (bf16[144,9216]{1,0:T(8,128)(2,1)}, bf16[144,9216]{1,0:T(8,128)(2,1)S(1)}, u32[]{:S(2)}, u32[]{:S(2)}) collective-permute-start(bf16[144,9216]{1,0:T(8,128)(2,1)} %u0.3), channel_id=1, source_target_pairs={{0,1},{1,0},{2,3},{3,2},{4,5},{5,4},{6,7},{7,6},{8,9},{9,8},{10,11... | collective-permute-start | bytes 7962632 | tf_op jit(solution)/shard_map/ppermute | solution.py:27
  7.1 11.0 %collective-permute-start.3 = (bf16[2,64,1152]{2,1,0:T(8,128)(2,1)S(1)}, bf16[2,64,1152]{2,1,0:T(8,128)(2,1)S(1)}, u32[]{:S(2)}, u32[]{:S(2)}) collective-permute-start(bf16[2,64,1152]{2,1,0:T(8,128)(2,1)S(1)} %pad_maximum_fusion), channel_id=1, source_target_pairs={{0,2},{1,3},{2,4},{3,5},{4,6},{5,7},{6,8},{7,9},{8,10},{9,11},{10,... | collective-permute-start | bytes 884744 | tf_op jit(solution)/shard_map/ppermute | solution.py:27
  7.2 18.1 %collective-permute-start.2 = (bf16[2,64,1152]{2,1,0:T(8,128)(2,1)S(1)}, bf16[2,64,1152]{2,1,0:T(8,128)(2,1)S(1)}, u32[]{:S(2)}, u32[]{:S(2)}) collective-permute-start(bf16[2,64,1152]{2,1,0:T(8,128)(2,1)S(1)} %pad_maximum_fusion), channel_id=1, source_target_pairs={{0,4},{1,5},{2,14},{3,15},{4,8},{5,9},{6,2},{7,3},{8,12},{9,13},{1... | collective-permute-start | bytes 884744 | tf_op jit(solution)/shard_map/ppermute | solution.py:27
  10.1 15.3 %collective-permute-start.1 = (bf16[2,64,1152]{2,1,0:T(8,128)(2,1)S(1)}, bf16[2,64,1152]{2,1,0:T(8,128)(2,1)S(1)}, u32[]{:S(2)}, u32[]{:S(2)}) collective-permute-start(bf16[2,64,1152]{2,1,0:T(8,128)(2,1)S(1)} %pad_maximum_fusion), channel_id=1, source_target_pairs={{0,14},{1,15},{2,0},{3,1},{4,2},{5,3},{6,4},{7,5},{8,6},{9,7},{10,... | collective-permute-start | bytes 884744 | tf_op jit(solution)/shard_map/ppermute | solution.py:27
  25.6 39.0 %collective-permute-start.13 = (bf16[1152,1152]{1,0:T(8,128)(2,1)}, bf16[1152,1152]{1,0:T(8,128)(2,1)S(1)}, u32[]{:S(2)}, u32[]{:S(2)}) collective-permute-start(bf16[1152,1152]{1,0:T(8,128)(2,1)} %d0.1), channel_id=1, source_target_pairs={{0,1},{1,0},{2,3},{3,2},{4,5},{5,4},{6,7},{7,6},{8,9},{9,8},{10,11... | collective-permute-start | bytes 7962632 | tf_op jit(solution)/shard_map/ppermute | solution.py:27
  26.9 14.1 %collective-permute-start.6 = (bf16[6,48,1152]{2,1,0:T(8,128)(2,1)S(1)}, bf16[6,48,1152]{2,1,0:T(8,128)(2,1)S(1)}, u32[]{:S(2)}, u32[]{:S(2)}) collective-permute-start(bf16[6,48,1152]{2,1,0:T(8,128)(2,1)S(1)} %get-tuple-element.39), channel_id=1, source_target_pairs={{0,192},{1,49},{2,194},{3,51},{4,196},{5,53},{6,198},{7,55},{8,200... | collective-permute-start | bytes 1990664 | tf_op jit(solution)/shard_map/ppermute | solution.py:27
  29.6 14.5 %collective-permute-start.7 = (bf16[6,48,1152]{2,1,0:T(8,128)(2,1)S(1)}, bf16[6,48,1152]{2,1,0:T(8,128)(2,1)S(1)}, u32[]{:S(2)}, u32[]{:S(2)}) collective-permute-start(bf16[6,48,1152]{2,1,0:T(8,128)(2,1)S(1)} %get-tuple-element.40), channel_id=1, source_target_pairs={{0,64},{1,17},{2,66},{3,19},{4,68},{5,21},{6,70},{7,23},{8,72},{9,... | collective-permute-start | bytes 1990664 | tf_op jit(solution)/shard_map/ppermute | solution.py:27
  29.6 15.0 %collective-permute-start.8 = (bf16[6,48,1152]{2,1,0:T(8,128)(2,1)S(1)}, bf16[6,48,1152]{2,1,0:T(8,128)(2,1)S(1)}, u32[]{:S(2)}, u32[]{:S(2)}) collective-permute-start(bf16[6,48,1152]{2,1,0:T(8,128)(2,1)S(1)} %get-tuple-element.41), channel_id=1, source_target_pairs={{0,48},{1,193},{2,50},{3,195},{4,52},{5,197},{6,54},{7,199},{8,56}... | collective-permute-start | bytes 1990664 | tf_op jit(solution)/shard_map/ppermute | solution.py:27
  32.1 15.9 %collective-permute-start.9 = (bf16[6,48,1152]{2,1,0:T(8,128)(2,1)S(1)}, bf16[6,48,1152]{2,1,0:T(8,128)(2,1)S(1)}, u32[]{:S(2)}, u32[]{:S(2)}) collective-permute-start(bf16[6,48,1152]{2,1,0:T(8,128)(2,1)S(1)} %get-tuple-element.42), channel_id=1, source_target_pairs={{0,16},{1,65},{2,18},{3,67},{4,20},{5,69},{6,22},{7,71},{8,24},{9,... | collective-permute-start | bytes 1990664 | tf_op jit(solution)/shard_map/ppermute | solution.py:27
  32.1 1.8 %copy-start.1 = (bf16[144,9216]{1,0:T(8,128)(2,1)S(1)}, bf16[144,9216]{1,0:T(8,128)(2,1)}, u32[]{:S(2)}) copy-start(bf16[144,9216]{1,0:T(8,128)(2,1)} %u0.3) | copy-start | bytes 7962628
  33.9 14.2 %copy-start.2 = (bf16[144,9216]{1,0:T(8,128)(2,1)S(1)}, bf16[144,9216]{1,0:T(8,128)(2,1)}, u32[]{:S(2)}) copy-start(bf16[144,9216]{1,0:T(8,128)(2,1)} %u0.3) | copy-start | bytes 7962628
  34.8 29.8 %copy-start.3 = (bf16[1152,1152]{1,0:T(8,128)(2,1)S(1)}, bf16[1152,1152]{1,0:T(8,128)(2,1)}, u32[]{:S(2)}) copy-start(bf16[1152,1152]{1,0:T(8,128)(2,1)} %d0.1) | copy-start | bytes 7962628
  50.6 7.2 %collective-permute-start.12 = (bf16[288,256]{1,0:T(8,128)(2,1)S(1)}, bf16[288,256]{1,0:T(8,128)(2,1)S(1)}, u32[]{:S(2)}, u32[]{:S(2)}) collective-permute-start(bf16[288,256]{1,0:T(8,128)(2,1)S(1)} %gate_up_silu.1.h0), channel_id=1, source_target_pairs={{0,2},{1,3},{2,4},{3,5},{4,6},{5,7},{6,0},{7,1},{8,10},{9,11},{10,... | collective-permute-start | bytes 442376 | tf_op jit(solution)/shard_map/ppermute | solution.py:27
  51.3 13.3 %collective-permute-start.11 = (bf16[288,256]{1,0:T(8,128)(2,1)S(1)}, bf16[288,256]{1,0:T(8,128)(2,1)S(1)}, u32[]{:S(2)}, u32[]{:S(2)}) collective-permute-start(bf16[288,256]{1,0:T(8,128)(2,1)S(1)} %gate_up_silu.1.h0), channel_id=1, source_target_pairs={{0,4},{1,5},{2,6},{3,7},{4,0},{5,1},{6,2},{7,3},{8,12},{9,13},{10,... | collective-permute-start | bytes 442376 | tf_op jit(solution)/shard_map/ppermute | solution.py:27
  54.0 10.6 %collective-permute-start.10 = (bf16[288,256]{1,0:T(8,128)(2,1)S(1)}, bf16[288,256]{1,0:T(8,128)(2,1)S(1)}, u32[]{:S(2)}, u32[]{:S(2)}) collective-permute-start(bf16[288,256]{1,0:T(8,128)(2,1)S(1)} %gate_up_silu.1.h0), channel_id=1, source_target_pairs={{0,6},{1,7},{2,0},{3,1},{4,2},{5,3},{6,4},{7,5},{8,14},{9,15},{10,... | collective-permute-start | bytes 442376 | tf_op jit(solution)/shard_map/ppermute | solution.py:27
  66.6 7.5 %collective-permute-start.14 = (bf16[2,64,1152]{2,1,0:T(8,128)(2,1)S(1)}, bf16[2,64,1152]{2,1,0:T(8,128)(2,1)S(1)}, u32[]{:S(2)}, u32[]{:S(2)}) collective-permute-start(bf16[2,64,1152]{2,1,0:T(8,128)(2,1)S(1)} %get-tuple-element.46), channel_id=1, source_target_pairs={{0,128},{1,33},{2,130},{3,35},{4,132},{5,37},{6,134},{7,39},{8,136... | collective-permute-start | bytes 884744 | tf_op jit(solution)/shard_map/ppermute | solution.py:27
  69.6 7.6 %collective-permute-start.15 = (bf16[2,64,1152]{2,1,0:T(8,128)(2,1)S(1)}, bf16[2,64,1152]{2,1,0:T(8,128)(2,1)S(1)}, u32[]{:S(2)}, u32[]{:S(2)}) collective-permute-start(bf16[2,64,1152]{2,1,0:T(8,128)(2,1)S(1)} %get-tuple-element.47), channel_id=1, source_target_pairs={{0,64},{1,17},{2,66},{3,19},{4,68},{5,21},{6,70},{7,23},{8,72},{9,... | collective-permute-start | bytes 884744 | tf_op jit(solution)/shard_map/ppermute | solution.py:27
  69.6 7.6 %collective-permute-start.16 = (bf16[2,64,1152]{2,1,0:T(8,128)(2,1)S(1)}, bf16[2,64,1152]{2,1,0:T(8,128)(2,1)S(1)}, u32[]{:S(2)}, u32[]{:S(2)}) collective-permute-start(bf16[2,64,1152]{2,1,0:T(8,128)(2,1)S(1)} %get-tuple-element.48), channel_id=1, source_target_pairs={{0,192},{1,49},{2,194},{3,51},{4,196},{5,53},{6,198},{7,55},{8,200... | collective-permute-start | bytes 884744 | tf_op jit(solution)/shard_map/ppermute | solution.py:27
  77.3 4.9 %collective-permute-start.17 = (bf16[2,16,1152]{2,1,0:T(8,128)(2,1)S(1)}, bf16[2,16,1152]{2,1,0:T(8,128)(2,1)S(1)}, u32[]{:S(2)}, u32[]{:S(2)}) collective-permute-start(bf16[2,16,1152]{2,1,0:T(8,128)(2,1)S(1)} %get-tuple-element.50), channel_id=1, source_target_pairs={{0,32},{1,129},{2,34},{3,131},{4,36},{5,133},{6,38},{7,135},{8,40}... | collective-permute-start | bytes 221192 | tf_op jit(solution)/shard_map/ppermute | solution.py:27
  77.4 5.3 %collective-permute-start.18 = (bf16[2,16,1152]{2,1,0:T(8,128)(2,1)S(1)}, bf16[2,16,1152]{2,1,0:T(8,128)(2,1)S(1)}, u32[]{:S(2)}, u32[]{:S(2)}) collective-permute-start(bf16[2,16,1152]{2,1,0:T(8,128)(2,1)S(1)} %get-tuple-element.51), channel_id=1, source_target_pairs={{0,16},{1,65},{2,18},{3,67},{4,20},{5,69},{6,22},{7,71},{8,24},{9,... | collective-permute-start | bytes 221192 | tf_op jit(solution)/shard_map/ppermute | solution.py:27
  78.1 4.7 %collective-permute-start.19 = (bf16[2,16,1152]{2,1,0:T(8,128)(2,1)S(1)}, bf16[2,16,1152]{2,1,0:T(8,128)(2,1)S(1)}, u32[]{:S(2)}, u32[]{:S(2)}) collective-permute-start(bf16[2,16,1152]{2,1,0:T(8,128)(2,1)S(1)} %get-tuple-element.52), channel_id=1, source_target_pairs={{0,48},{1,193},{2,50},{3,195},{4,52},{5,197},{6,54},{7,199},{8,56}... | collective-permute-start | bytes 221192 | tf_op jit(solution)/shard_map/ppermute | solution.py:27
  82.8 6.8 %collective-permute-start.20 = (bf16[16,1152]{1,0:T(8,128)(2,1)S(1)}, bf16[16,1152]{1,0:T(8,128)(2,1)S(1)}, u32[]{:S(2)}, u32[]{:S(2)}) collective-permute-start(bf16[16,1152]{1,0:T(8,128)(2,1)S(1)} %get-tuple-element.54), channel_id=1, source_target_pairs={{0,8},{1,9},{2,10},{3,11},{4,12},{5,13},{6,14},{7,15},{8,0},{9,1},... | collective-permute-start | bytes 110600 | tf_op jit(solution)/shard_map/ppermute | solution.py:27
  89.6 6.7 %collective-permute-start.21 = (bf16[8,1152]{1,0:T(8,128)(2,1)S(1)}, bf16[8,1152]{1,0:T(8,128)(2,1)S(1)}, u32[]{:S(2)}, u32[]{:S(2)}) collective-permute-start(bf16[8,1152]{1,0:T(8,128)(2,1)S(1)} %convert), channel_id=1, source_target_pairs={{0,1},{1,0},{2,3},{3,2},{4,5},{5,4},{6,7},{7,6},{8,9},{9,8},{10,11... | collective-permute-start | bytes 55304 | tf_op jit(solution)/shard_map/ppermute | solution.py:27

commit v4 on v3

--- a/solution.py
+++ b/solution.py
@@ -41,6 +41,10 @@
 
 def _z(k):
     return lambda x, y, z, c: (x, y, z + k, c)
+
+
+def _up_or_down(k):
+    return lambda x, y, z, c: (x, y, z + k if c == 0 else z - k, c)
 
 
 def _z_two(x, y, z, c):
@@ -100,13 +104,16 @@
     return jnp.concatenate([w[:, pl.ds(column, width)] for w in weights], axis=0)
 
 
+def _in_order(rows):
+    return jnp.concatenate([rows[:32], rows[64:160], rows[32:64], rows[160:]], axis=0)
+
+
 def _own_kernel(mine, other, g0, g1, u0, u1, out):
     _, _, _, l, c = _place()
     width = mine.shape[1]
     for k, own in enumerate((mine, other)):
         w = _weight_columns((g0, g1, u0, u1), 2 * l + (c if k == 0 else 1 - c), width)
-        t = jnp.concatenate([own[:32], own[64:160], own[32:64], own[160:]], axis=0)
-        part = lax.dot_general(w, t, NT, preferred_element_type=F32)
+        part = lax.dot_general(w, _in_order(own), NT, preferred_element_type=F32)
         if k == 0:
             out[...] = part
         else:
@@ -128,8 +135,8 @@
     )(mine, other, *weights)
 
 
-def _pack_kernel(p0, p1, p2, first_back, first_on, second_back, second_on):
-    for i, piece in enumerate((p0, p1, p2)):
+def _pack_kernel(near, two, first_back, first_on, second_back, second_on):
+    for i, piece in enumerate((near, two)):
         for j in range(2):
             k = 2 * i + j
             a, b = piece[j, :32], piece[j, 32:]
@@ -140,10 +147,10 @@
 
 
 def _pack(pieces):
-    send = jax.ShapeDtypeStruct((6, 48, pieces[0].shape[-1]), BF16)
+    send = jax.ShapeDtypeStruct((4, 48, pieces[0].shape[-1]), BF16)
     return pl.pallas_call(
         _pack_kernel,
-        in_specs=[VMEM] * 3,
+        in_specs=[VMEM] * 2,
         out_specs=[VMEM] * 4,
         out_shape=[send] * 4,
         compiler_params=pltpu.CompilerParams(vmem_limit_bytes=16 * MIB),
@@ -151,30 +158,34 @@
     )(*pieces)
 
 
-def _hidden_kernel(z0, z1, z2, p1, m1, p2, m2, start, g0, g1, u0, u1, out, acc):
+def _hidden_kernel(near, two, p1, m1, p2, m2, direct, start, g0, g1, u0, u1, out, acc):
     x, y, _, l, c = _place()
     first, second = _along(c, x, y)
-    width = z0.shape[-1]
+    width = near.shape[-1]
     units = g0.shape[0]
+    ahead = (jnp.where(c == 0, 3, 1), 2, jnp.where(c == 0, 1, 3))
     for k in range(6):
-        block = 2 * lax.rem(l + 1 + k // 2, 4) + (c if k % 2 == 0 else 1 - c)
+        block = 2 * lax.rem(l + ahead[k // 2], 4) + (c if k % 2 == 0 else 1 - c)
         w = _weight_columns((g0, g1, u0, u1), block, width)
-        kept = (z0, z1, z2)[k // 2][k % 2]
-        t = jnp.concatenate(
-            [
-                kept[:32],
-                p1[k, :32],
-                p2[k, :16],
-                m2[k, :16],
-                m1[k, :32],
-                kept[32:],
-                p2[k, 16:],
-                p1[k, 32:],
-                m1[k, 32:],
-                m2[k, 16:],
-            ],
-            axis=0,
-        )
+        if k < 4:
+            kept = (near, two)[k // 2][k % 2]
+            t = jnp.concatenate(
+                [
+                    kept[:32],
+                    p1[k, :32],
+                    p2[k, :16],
+                    m2[k, :16],
+                    m1[k, :32],
+                    kept[32:],
+                    p2[k, 16:],
+                    p1[k, 32:],
+                    m1[k, 32:],
+                    m2[k, 16:],
+                ],
+                axis=0,
+            )
+        else:
+            t = _in_order(direct[k - 4])
         part = lax.dot_general(w, t, NT, preferred_element_type=F32)
         if k == 0:
             acc[...] = start[...] + part
@@ -191,7 +202,7 @@
         out[:, i * half : (i + 1) * half] = part.astype(BF16)
 
 
-def _hidden(kept, around, start, weights):
+def _hidden(kept, around, direct, start, weights):
     units, width = weights[0].shape[0], kept[0].shape[-1]
     rows = start.shape[1]
     return pl.pallas_call(
@@ -207,7 +218,7 @@
             transcendentals=2 * units * rows,
         ),
         name="gate_up_silu",
-    )(*kept, *around, start, *weights)
+    )(*kept, *around, direct, start, *weights)
 
 
 def _down_kernel(h0, h1, h2, h3, d0, d1, own, s1, s2, s3, ht):
@@ -318,16 +329,17 @@
     mine, theirs = _order(tokens)
     other = _permute(theirs, _swap)
     quarter = jnp.stack([mine[:64], other[:64]])
-    kept = [_permute(quarter, m) for m in (_z(-1), _z_two, _z(1))]
+    near = _permute(quarter, _up_or_down(1))
+    two = _permute(quarter, _z_two)
     gate_in, up_in, _ = lax.optimization_barrier((gate_weight, up_weight, other))
     gate_other = _permute(gate_in, _swap)
     up_other = _permute(up_in, _swap)
     weights = (gate_weight, gate_other, up_weight, up_other)
-
-    packed = _pack(kept)
+    whole, near, two = lax.optimization_barrier((jnp.stack([mine, other]), near, two))
+    direct = _permute(whole, _up_or_down(-1))
+
+    packed = _pack((near, two))
     packed, gate_other, up_other = lax.optimization_barrier((packed, gate_other, up_other))
-    down_in, _ = lax.optimization_barrier((down_weight, packed))
-    down_other = _permute(down_in, _swap)
     first_back, first_on, second_back, second_on = packed
     around = [
         _permute(first_back, _first(-1)),
@@ -338,7 +350,9 @@
     mine, _ = lax.optimization_barrier((mine, packed))
     start = _own(mine, other, weights)
 
-    hidden = _hidden(kept, around, start, weights)
+    hidden = _hidden((near, two), around, direct, start, weights)
+    down_in, _ = lax.optimization_barrier((down_weight, hidden))
+    down_other = _permute(down_in, _swap)
     two, one, three = (_permute(hidden, _lo(-k)) for k in (2, 1, 3))
 
     own, *sends = _down((hidden, one, two, three), down_weight, down_other)

time: 98.2 us -> 90.3 us (0.920)
  waiting for transfers between devices: 49.7 us -> 46.3 us
  starting transfers between devices: 37.3 us -> 35 us
  local copies, waits for them, and re-layouts: 3.21 us -> 1.46 us
    ppermute x22, waiting for transfers between devices: 49.7 us -> 46.3 us  [_permute(): return lax.ppermute(a, AXES, _perm(move))]
    ppermute x22, starting transfers between devices: 37.3 us -> 35 us  [_permute(): return lax.ppermute(a, AXES, _perm(move))]
    unnamed x10 -> x8, local copies, waits for them, and re-layouts: 3.18 us -> 1.43 us
  transfers between devices with their start and end apart: 22 -> 22, of which waited for: 16 -> 14; matrix products, arithmetic and copies ran while one was open for 0% -> 0% of each run, Pallas kernels for 4% -> 1%
where the time goes in v4:
time: 90.3 us; the launch traced here: 89.6 us
  waiting for transfers between devices  46.3 us (51%)
  starting transfers between devices  35 us (39%)
  Pallas kernels  5.85 us (6%)
  local copies, waits for them, and re-layouts  1.46 us (2%)
    ppermute x22, waiting for transfers between devices, _permute(): return lax.ppermute(a, AXES, _perm(move))  46.3 us
    ppermute x22, starting transfers between devices, _permute(): return lax.ppermute(a, AXES, _perm(move))  35 us
    pallas_call x1, Pallas kernels, _hidden(): pl.pallas_call(_hidden_kernel, in_specs=[VMEM] * 12, out_specs=VMEM, out_...  2.56 us
    pallas_call x1, Pallas kernels, _down(): pl.pallas_call(_down_kernel, in_specs=[VMEM] * 6, out_specs=[VMEM] * 4, o...  1.91 us
  transfers between devices with their start and end apart: 22, of which 14 were waited for; matrix products, arithmetic and copies ran while one was open for 0% of the time, Pallas kernels for 1%

profile of v4, /device:TPU:1, one launch (start us, length us, event | category | flops | bytes accessed | tf_op | source)
XLA Modules:
  0.0 89.6 jit_solution(8835630611829801581)
XLA Ops:
  0.0 0.0 copy-start.1
  0.0 0.0 copy-start
  0.0 0.0 copy-start.3
  0.0 1.4 %copy-done.3 = bf16[2,256,1152]{2,1,0:T(8,128)(2,1)S(1)} copy-done((bf16[2,256,1152]{2,1,0:T(8,128)(2,1)S(1)}, bf16[2,256,1152]{2,1,0:T(8,128)(2,1)}, u32[]{:S(2)}) %copy-start.3) | copy-done | bytes 1179672
  1.4 0.1 order_rows.1
  1.5 3.3 %collective-permute-start = (bf16[256,1152]{1,0:T(8,128)(2,1)S(1)}, bf16[256,1152]{1,0:T(8,128)(2,1)S(1)}, u32[]{:S(2)}, u32[]{:S(2)}) collective-permute-start(bf16[256,1152]{1,0:T(8,128)(2,1)S(1)} %get-tuple-element.35), channel_id=1, source_target_pairs={{0,1},{1,0},{2,3},{3,2},{4,5},{5,4},{6,7},{7,6},{8,9},{9,8},{10,11... | collective-permute-start | bytes 1769480 | tf_op jit(solution)/shard_map/ppermute | solution.py:27
  4.9 1.6 %collective-permute-done.other = bf16[256,1152]{1,0:T(8,128)(2,1)S(1)} collective-permute-done((bf16[256,1152]{1,0:T(8,128)(2,1)S(1)}, bf16[256,1152]{1,0:T(8,128)(2,1)S(1)}, u32[]{:S(2)}, u32[]{:S(2)}) %collective-permute-start) | collective-permute-done | bytes 589856 | tf_op jit(solution)/shard_map/ppermute | solution.py:27
  6.5 0.4 collective-permute-start.3
  6.9 0.1 collective-permute-start.4
  7.1 1.3 %collective-permute-start.2 = (bf16[2,64,1152]{2,1,0:T(8,128)(2,1)S(1)}, bf16[2,64,1152]{2,1,0:T(8,128)(2,1)S(1)}, u32[]{:S(2)}, u32[]{:S(2)}) collective-permute-start(bf16[2,64,1152]{2,1,0:T(8,128)(2,1)S(1)} %pad_maximum_fusion.1), channel_id=1, source_target_pairs={{0,4},{1,5},{2,14},{3,15},{4,8},{5,9},{6,2},{7,3},{8,12},{9,13},{1... | collective-permute-start | bytes 884744 | tf_op jit(solution)/shard_map/ppermute | solution.py:27
  8.4 3.8 %collective-permute-start.1 = (bf16[2,64,1152]{2,1,0:T(8,128)(2,1)S(1)}, bf16[2,64,1152]{2,1,0:T(8,128)(2,1)S(1)}, u32[]{:S(2)}, u32[]{:S(2)}) collective-permute-start(bf16[2,64,1152]{2,1,0:T(8,128)(2,1)S(1)} %pad_maximum_fusion.1), channel_id=1, source_target_pairs={{0,2},{1,15},{2,4},{3,1},{4,6},{5,3},{6,8},{7,5},{8,10},{9,7},{10,... | collective-permute-start | bytes 884744 | tf_op jit(solution)/shard_map/ppermute | solution.py:27
  12.2 0.1 pad_maximum_fusion
  12.3 6.3 %collective-permute-done.2.two = bf16[2,64,1152]{2,1,0:T(8,128)(2,1)S(1)} collective-permute-done((bf16[2,64,1152]{2,1,0:T(8,128)(2,1)S(1)}, bf16[2,64,1152]{2,1,0:T(8,128)(2,1)S(1)}, u32[]{:S(2)}, u32[]{:S(2)}) %collective-permute-start.2) | collective-permute-done | bytes 294944 | tf_op jit(solution)/shard_map/ppermute | solution.py:27
  18.6 4.1 %collective-permute-done.1.near = bf16[2,64,1152]{2,1,0:T(8,128)(2,1)S(1)} collective-permute-done((bf16[2,64,1152]{2,1,0:T(8,128)(2,1)S(1)}, bf16[2,64,1152]{2,1,0:T(8,128)(2,1)S(1)}, u32[]{:S(2)}, u32[]{:S(2)}) %collective-permute-start.1) | collective-permute-done | bytes 294944 | tf_op jit(solution)/shard_map/ppermute | solution.py:27
  22.7 0.0 collective-permute-start.9
  22.7 0.1 pack_quarters.1
  22.8 0.0 collective-permute-done.3.g1
  22.8 0.0 collective-permute-done.4.u1
  22.8 2.8 %collective-permute-start.5 = (bf16[4,48,1152]{2,1,0:T(8,128)(2,1)S(1)}, bf16[4,48,1152]{2,1,0:T(8,128)(2,1)S(1)}, u32[]{:S(2)}, u32[]{:S(2)}) collective-permute-start(bf16[4,48,1152]{2,1,0:T(8,128)(2,1)S(1)} %get-tuple-element.44), channel_id=1, source_target_pairs={{0,192},{1,49},{2,194},{3,51},{4,196},{5,53},{6,198},{7,55},{8,200... | collective-permute-start | bytes 1327112 | tf_op jit(solution)/shard_map/ppermute | solution.py:27
  25.6 0.0 collective-permute-start.6
  25.6 2.5 %collective-permute-start.7 = (bf16[4,48,1152]{2,1,0:T(8,128)(2,1)S(1)}, bf16[4,48,1152]{2,1,0:T(8,128)(2,1)S(1)}, u32[]{:S(2)}, u32[]{:S(2)}) collective-permute-start(bf16[4,48,1152]{2,1,0:T(8,128)(2,1)S(1)} %get-tuple-element.46), channel_id=1, source_target_pairs={{0,48},{1,193},{2,50},{3,195},{4,52},{5,197},{6,54},{7,199},{8,56}... | collective-permute-start | bytes 1327112 | tf_op jit(solution)/shard_map/ppermute | solution.py:27
  28.1 0.0 collective-permute-start.8
  28.1 0.0 copy-done.1
  28.1 0.0 copy-done
  28.1 0.9 %own_features.1.start = f32[576,256]{1,0:T(8,128)S(1)} custom-call(bf16[256,1152]{1,0:T(8,128)(2,1)S(1)} %get-tuple-element.49.mine, bf16[256,1152]{1,0:T(8,128)(2,1)S(1)} %collective-permute-done.other, bf16[144,9216]{1,0:T(8,128)(2,1)S(1)} %copy-done, bf16[144,9216]{1,0:T(8,128)(2,1)S(1)} %collective-permute-done.3.g1, bf16[144,9216]{1,0:T(8,128)(2,1)S(1)} %copy-done.1, ...), custom_call_target="tpu_custom_call" | custom-call | flops 679477248 | bytes 3317760 | tf_op jit(solution)/shard_map/own_features/pallas_call | solution.py:125
  29.1 0.0 copy-start.2
  29.1 10.1 %collective-permute-done.9.direct = bf16[2,256,1152]{2,1,0:T(8,128)(2,1)S(1)} collective-permute-done((bf16[2,256,1152]{2,1,0:T(8,128)(2,1)S(1)}, bf16[2,256,1152]{2,1,0:T(8,128)(2,1)S(1)}, u32[]{:S(2)}, u32[]{:S(2)}) %collective-permute-start.9) | collective-permute-done | bytes 1179680 | tf_op jit(solution)/shard_map/ppermute | solution.py:27
  39.2 0.0 collective-permute-done.5.p1
  39.2 0.0 collective-permute-done.6.m1
  39.2 0.0 collective-permute-done.7.p2
  39.2 1.0 %collective-permute-done.8.m2 = bf16[4,48,1152]{2,1,0:T(8,128)(2,1)S(1)} collective-permute-done((bf16[4,48,1152]{2,1,0:T(8,128)(2,1)S(1)}, bf16[4,48,1152]{2,1,0:T(8,128)(2,1)S(1)}, u32[]{:S(2)}, u32[]{:S(2)}) %collective-permute-start.8) | collective-permute-done | bytes 442400 | tf_op jit(solution)/shard_map/ppermute | solution.py:27
  40.2 2.6 %gate_up_silu.1.h0 = bf16[288,256]{1,0:T(8,128)(2,1)S(1)} custom-call(bf16[2,64,1152]{2,1,0:T(8,128)(2,1)S(1)} %collective-permute-done.1.near, bf16[2,64,1152]{2,1,0:T(8,128)(2,1)S(1)} %collective-permute-done.2.two, bf16[4,48,1152]{2,1,0:T(8,128)(2,1)S(1)} %collective-permute-done.5.p1, bf16[4,48,1152]{2,1,0:T(8,128)(2,1)S(1)} %collective-permute-done.6.m1, ...), custom_call_target="tpu_custom_call" | custom-call | flops 2038431744 | bytes 7962624 | tf_op jit(solution)/shard_map/gate_up_silu/pallas_call | solution.py:208
  42.8 0.0 copy-done.2
  42.8 0.1 collective-permute-start.13
  42.9 1.2 %collective-permute-start.12 = (bf16[288,256]{1,0:T(8,128)(2,1)S(1)}, bf16[288,256]{1,0:T(8,128)(2,1)S(1)}, u32[]{:S(2)}, u32[]{:S(2)}) collective-permute-start(bf16[288,256]{1,0:T(8,128)(2,1)S(1)} %gate_up_silu.1.h0), channel_id=1, source_target_pairs={{0,2},{1,3},{2,4},{3,5},{4,6},{5,7},{6,0},{7,1},{8,10},{9,11},{10,... | collective-permute-start | bytes 442376 | tf_op jit(solution)/shard_map/ppermute | solution.py:27
  44.1 1.2 %collective-permute-start.11 = (bf16[288,256]{1,0:T(8,128)(2,1)S(1)}, bf16[288,256]{1,0:T(8,128)(2,1)S(1)}, u32[]{:S(2)}, u32[]{:S(2)}) collective-permute-start(bf16[288,256]{1,0:T(8,128)(2,1)S(1)} %gate_up_silu.1.h0), channel_id=1, source_target_pairs={{0,4},{1,5},{2,6},{3,7},{4,0},{5,1},{6,2},{7,3},{8,12},{9,13},{10,... | collective-permute-start | bytes 442376 | tf_op jit(solution)/shard_map/ppermute | solution.py:27
  45.4 0.9 collective-permute-start.10
  46.2 3.6 %collective-permute-done.12.h3 = bf16[288,256]{1,0:T(8,128)(2,1)S(1)} collective-permute-done((bf16[288,256]{1,0:T(8,128)(2,1)S(1)}, bf16[288,256]{1,0:T(8,128)(2,1)S(1)}, u32[]{:S(2)}, u32[]{:S(2)}) %collective-permute-start.12) | collective-permute-done | bytes 147488 | tf_op jit(solution)/shard_map/ppermute | solution.py:27
  49.8 7.1 %collective-permute-done.11.h2 = bf16[288,256]{1,0:T(8,128)(2,1)S(1)} collective-permute-done((bf16[288,256]{1,0:T(8,128)(2,1)S(1)}, bf16[288,256]{1,0:T(8,128)(2,1)S(1)}, u32[]{:S(2)}, u32[]{:S(2)}) %collective-permute-start.11) | collective-permute-done | bytes 147488 | tf_op jit(solution)/shard_map/ppermute | solution.py:27
  56.9 0.0 collective-permute-done.10.h1
  56.9 0.0 collective-permute-done.13.d1
  56.9 1.9 %down.1 = (f32[2,64,1152]{2,1,0:T(8,128)S(1)}, bf16[2,64,1152]{2,1,0:T(8,128)(2,1)S(1)}, bf16[2,64,1152]{2,1,0:T(8,128)(2,1)S(1)}, bf16[2,64,1152]{2,1,0:T(8,128)(2,1)S(1)}) custom-call(bf16[288,256]{1,0:T(8,128)(2,1)S(1)} %gate_up_silu.1.h0, bf16[288,256]{1,0:T(8,128)(2,1)S(1)} %collective-permute-done.10.h1, ...), custom_call_target="tpu_custom_call" | custom-call | flops 1358954496 | bytes 5308416 | tf_op jit(solution)/shard_map/down/pallas_call | solution.py:248
  58.8 1.9 %collective-permute-start.14 = (bf16[2,64,1152]{2,1,0:T(8,128)(2,1)S(1)}, bf16[2,64,1152]{2,1,0:T(8,128)(2,1)S(1)}, u32[]{:S(2)}, u32[]{:S(2)}) collective-permute-start(bf16[2,64,1152]{2,1,0:T(8,128)(2,1)S(1)} %get-tuple-element.52), channel_id=1, source_target_pairs={{0,128},{1,33},{2,130},{3,35},{4,132},{5,37},{6,134},{7,39},{8,136... | collective-permute-start | bytes 884744 | tf_op jit(solution)/shard_map/ppermute | solution.py:27
  60.7 1.5 %collective-permute-start.15 = (bf16[2,64,1152]{2,1,0:T(8,128)(2,1)S(1)}, bf16[2,64,1152]{2,1,0:T(8,128)(2,1)S(1)}, u32[]{:S(2)}, u32[]{:S(2)}) collective-permute-start(bf16[2,64,1152]{2,1,0:T(8,128)(2,1)S(1)} %get-tuple-element.53), channel_id=1, source_target_pairs={{0,64},{1,17},{2,66},{3,19},{4,68},{5,21},{6,70},{7,23},{8,72},{9,... | collective-permute-start | bytes 884744 | tf_op jit(solution)/shard_map/ppermute | solution.py:27
  62.2 1.2 %collective-permute-start.16 = (bf16[2,64,1152]{2,1,0:T(8,128)(2,1)S(1)}, bf16[2,64,1152]{2,1,0:T(8,128)(2,1)S(1)}, u32[]{:S(2)}, u32[]{:S(2)}) collective-permute-start(bf16[2,64,1152]{2,1,0:T(8,128)(2,1)S(1)} %get-tuple-element.54), channel_id=1, source_target_pairs={{0,192},{1,49},{2,194},{3,51},{4,196},{5,53},{6,198},{7,55},{8,200... | collective-permute-start | bytes 884744 | tf_op jit(solution)/shard_map/ppermute | solution.py:27
  63.4 2.9 %collective-permute-done.14.g1 = bf16[2,64,1152]{2,1,0:T(8,128)(2,1)S(1)} collective-permute-done((bf16[2,64,1152]{2,1,0:T(8,128)(2,1)S(1)}, bf16[2,64,1152]{2,1,0:T(8,128)(2,1)S(1)}, u32[]{:S(2)}, u32[]{:S(2)}) %collective-permute-start.14) | collective-permute-done | bytes 294944 | tf_op jit(solution)/shard_map/ppermute | solution.py:27
  66.3 3.1 %collective-permute-done.15.g2 = bf16[2,64,1152]{2,1,0:T(8,128)(2,1)S(1)} collective-permute-done((bf16[2,64,1152]{2,1,0:T(8,128)(2,1)S(1)}, bf16[2,64,1152]{2,1,0:T(8,128)(2,1)S(1)}, u32[]{:S(2)}, u32[]{:S(2)}) %collective-permute-start.15) | collective-permute-done | bytes 294944 | tf_op jit(solution)/shard_map/ppermute | solution.py:27
  69.5 0.4 collective-permute-done.16.g3
  69.8 0.1 sum_first.1
  70.0 1.6 %collective-permute-start.17 = (bf16[2,16,1152]{2,1,0:T(8,128)(2,1)S(1)}, bf16[2,16,1152]{2,1,0:T(8,128)(2,1)S(1)}, u32[]{:S(2)}, u32[]{:S(2)}) collective-permute-start(bf16[2,16,1152]{2,1,0:T(8,128)(2,1)S(1)} %get-tuple-element.56), channel_id=1, source_target_pairs={{0,32},{1,129},{2,34},{3,131},{4,36},{5,133},{6,38},{7,135},{8,40}... | collective-permute-start | bytes 221192 | tf_op jit(solution)/shard_map/ppermute | solution.py:27
  71.6 0.3 collective-permute-start.18
  71.9 2.4 %collective-permute-start.19 = (bf16[2,16,1152]{2,1,0:T(8,128)(2,1)S(1)}, bf16[2,16,1152]{2,1,0:T(8,128)(2,1)S(1)}, u32[]{:S(2)}, u32[]{:S(2)}) collective-permute-start(bf16[2,16,1152]{2,1,0:T(8,128)(2,1)S(1)} %get-tuple-element.58), channel_id=1, source_target_pairs={{0,48},{1,193},{2,50},{3,195},{4,52},{5,197},{6,54},{7,199},{8,56}... | collective-permute-start | bytes 221192 | tf_op jit(solution)/shard_map/ppermute | solution.py:27
  74.3 0.5 collective-permute-done.17.g1
  74.8 1.6 %collective-permute-done.18.g2 = bf16[2,16,1152]{2,1,0:T(8,128)(2,1)S(1)} collective-permute-done((bf16[2,16,1152]{2,1,0:T(8,128)(2,1)S(1)}, bf16[2,16,1152]{2,1,0:T(8,128)(2,1)S(1)}, u32[]{:S(2)}, u32[]{:S(2)}) %collective-permute-start.18) | collective-permute-done | bytes 73760 | tf_op jit(solution)/shard_map/ppermute | solution.py:27
  76.3 0.0 collective-permute-done.19.g3
  76.4 3.6 %collective-permute-start.20 = (bf16[16,1152]{1,0:T(8,128)(2,1)S(1)}, bf16[16,1152]{1,0:T(8,128)(2,1)S(1)}, u32[]{:S(2)}, u32[]{:S(2)}) collective-permute-start(bf16[16,1152]{1,0:T(8,128)(2,1)S(1)} %get-tuple-element.60), channel_id=1, source_target_pairs={{0,8},{1,9},{2,10},{3,11},{4,12},{5,13},{6,14},{7,15},{8,0},{9,1},... | collective-permute-start | bytes 110600 | tf_op jit(solution)/shard_map/ppermute | solution.py:27
  79.9 3.2 %collective-permute-done.20.got = bf16[16,1152]{1,0:T(8,128)(2,1)S(1)} collective-permute-done((bf16[16,1152]{1,0:T(8,128)(2,1)S(1)}, bf16[16,1152]{1,0:T(8,128)(2,1)S(1)}, u32[]{:S(2)}, u32[]{:S(2)}) %collective-permute-start.20) | collective-permute-done | bytes 36896 | tf_op jit(solution)/shard_map/ppermute | solution.py:27
  83.2 4.9 %collective-permute-start.21 = (bf16[8,1152]{1,0:T(8,128)(2,1)S(1)}, bf16[8,1152]{1,0:T(8,128)(2,1)S(1)}, u32[]{:S(2)}, u32[]{:S(2)}) collective-permute-start(bf16[8,1152]{1,0:T(8,128)(2,1)S(1)} %convert), channel_id=1, source_target_pairs={{0,1},{1,0},{2,3},{3,2},{4,5},{5,4},{6,7},{7,6},{8,9},{9,8},{10,11... | collective-permute-start | bytes 55304 | tf_op jit(solution)/shard_map/ppermute | solution.py:27
  88.1 0.8 collective-permute-done.21
  88.9 0.7 select_convert_fusion
  (7 shorter events, 0.1 us)
Async XLA Ops:
  0.0 28.1 %copy-start.1 = (bf16[144,9216]{1,0:T(8,128)(2,1)S(1)}, bf16[144,9216]{1,0:T(8,128)(2,1)}, u32[]{:S(2)}) copy-start(bf16[144,9216]{1,0:T(8,128)(2,1)} %u0.3) | copy-start | bytes 7962628
  0.0 28.1 %copy-start = (bf16[144,9216]{1,0:T(8,128)(2,1)S(1)}, bf16[144,9216]{1,0:T(8,128)(2,1)}, u32[]{:S(2)}) copy-start(bf16[144,9216]{1,0:T(8,128)(2,1)} %g0.3) | copy-start | bytes 7962628
  0.0 1.4 %copy-start.3 = (bf16[2,256,1152]{2,1,0:T(8,128)(2,1)S(1)}, bf16[2,256,1152]{2,1,0:T(8,128)(2,1)}, u32[]{:S(2)}) copy-start(bf16[2,256,1152]{2,1,0:T(8,128)(2,1)} %tokens.1) | copy-start | bytes 3538948
  1.5 5.0 %collective-permute-start = (bf16[256,1152]{1,0:T(8,128)(2,1)S(1)}, bf16[256,1152]{1,0:T(8,128)(2,1)S(1)}, u32[]{:S(2)}, u32[]{:S(2)}) collective-permute-start(bf16[256,1152]{1,0:T(8,128)(2,1)S(1)} %get-tuple-element.35), channel_id=1, source_target_pairs={{0,1},{1,0},{2,3},{3,2},{4,5},{5,4},{6,7},{7,6},{8,9},{9,8},{10,11... | collective-permute-start | bytes 1769480 | tf_op jit(solution)/shard_map/ppermute | solution.py:27
  6.5 16.3 %collective-permute-start.3 = (bf16[144,9216]{1,0:T(8,128)(2,1)}, bf16[144,9216]{1,0:T(8,128)(2,1)S(1)}, u32[]{:S(2)}, u32[]{:S(2)}) collective-permute-start(bf16[144,9216]{1,0:T(8,128)(2,1)} %g0.3), channel_id=1, source_target_pairs={{0,1},{1,0},{2,3},{3,2},{4,5},{5,4},{6,7},{7,6},{8,9},{9,8},{10,11... | collective-permute-start | bytes 7962632 | tf_op jit(solution)/shard_map/ppermute | solution.py:27
  6.9 15.9 %collective-permute-start.4 = (bf16[144,9216]{1,0:T(8,128)(2,1)}, bf16[144,9216]{1,0:T(8,128)(2,1)S(1)}, u32[]{:S(2)}, u32[]{:S(2)}) collective-permute-start(bf16[144,9216]{1,0:T(8,128)(2,1)} %u0.3), channel_id=1, source_target_pairs={{0,1},{1,0},{2,3},{3,2},{4,5},{5,4},{6,7},{7,6},{8,9},{9,8},{10,11... | collective-permute-start | bytes 7962632 | tf_op jit(solution)/shard_map/ppermute | solution.py:27
  7.1 11.5 %collective-permute-start.2 = (bf16[2,64,1152]{2,1,0:T(8,128)(2,1)S(1)}, bf16[2,64,1152]{2,1,0:T(8,128)(2,1)S(1)}, u32[]{:S(2)}, u32[]{:S(2)}) collective-permute-start(bf16[2,64,1152]{2,1,0:T(8,128)(2,1)S(1)} %pad_maximum_fusion.1), channel_id=1, source_target_pairs={{0,4},{1,5},{2,14},{3,15},{4,8},{5,9},{6,2},{7,3},{8,12},{9,13},{1... | collective-permute-start | bytes 884744 | tf_op jit(solution)/shard_map/ppermute | solution.py:27
  8.4 14.2 %collective-permute-start.1 = (bf16[2,64,1152]{2,1,0:T(8,128)(2,1)S(1)}, bf16[2,64,1152]{2,1,0:T(8,128)(2,1)S(1)}, u32[]{:S(2)}, u32[]{:S(2)}) collective-permute-start(bf16[2,64,1152]{2,1,0:T(8,128)(2,1)S(1)} %pad_maximum_fusion.1), channel_id=1, source_target_pairs={{0,2},{1,15},{2,4},{3,1},{4,6},{5,3},{6,8},{7,5},{8,10},{9,7},{10,... | collective-permute-start | bytes 884744 | tf_op jit(solution)/shard_map/ppermute | solution.py:27
  22.7 16.6 %collective-permute-start.9 = (bf16[2,256,1152]{2,1,0:T(8,128)(2,1)S(1)}, bf16[2,256,1152]{2,1,0:T(8,128)(2,1)S(1)}, u32[]{:S(2)}, u32[]{:S(2)}) collective-permute-start(bf16[2,256,1152]{2,1,0:T(8,128)(2,1)S(1)} %pad_maximum_fusion), channel_id=1, source_target_pairs={{0,14},{1,3},{2,0},{3,5},{4,2},{5,7},{6,4},{7,9},{8,6},{9,11},{10,... | collective-permute-start | bytes 3538952 | tf_op jit(solution)/shard_map/ppermute | solution.py:27
  22.8 16.4 %collective-permute-start.5 = (bf16[4,48,1152]{2,1,0:T(8,128)(2,1)S(1)}, bf16[4,48,1152]{2,1,0:T(8,128)(2,1)S(1)}, u32[]{:S(2)}, u32[]{:S(2)}) collective-permute-start(bf16[4,48,1152]{2,1,0:T(8,128)(2,1)S(1)} %get-tuple-element.44), channel_id=1, source_target_pairs={{0,192},{1,49},{2,194},{3,51},{4,196},{5,53},{6,198},{7,55},{8,200... | collective-permute-start | bytes 1327112 | tf_op jit(solution)/shard_map/ppermute | solution.py:27
  25.6 13.6 %collective-permute-start.6 = (bf16[4,48,1152]{2,1,0:T(8,128)(2,1)S(1)}, bf16[4,48,1152]{2,1,0:T(8,128)(2,1)S(1)}, u32[]{:S(2)}, u32[]{:S(2)}) collective-permute-start(bf16[4,48,1152]{2,1,0:T(8,128)(2,1)S(1)} %get-tuple-element.45), channel_id=1, source_target_pairs={{0,64},{1,17},{2,66},{3,19},{4,68},{5,21},{6,70},{7,23},{8,72},{9,... | collective-permute-start | bytes 1327112 | tf_op jit(solution)/shard_map/ppermute | solution.py:27
  25.6 13.6 %collective-permute-start.7 = (bf16[4,48,1152]{2,1,0:T(8,128)(2,1)S(1)}, bf16[4,48,1152]{2,1,0:T(8,128)(2,1)S(1)}, u32[]{:S(2)}, u32[]{:S(2)}) collective-permute-start(bf16[4,48,1152]{2,1,0:T(8,128)(2,1)S(1)} %get-tuple-element.46), channel_id=1, source_target_pairs={{0,48},{1,193},{2,50},{3,195},{4,52},{5,197},{6,54},{7,199},{8,56}... | collective-permute-start | bytes 1327112 | tf_op jit(solution)/shard_map/ppermute | solution.py:27
  28.1 12.1 %collective-permute-start.8 = (bf16[4,48,1152]{2,1,0:T(8,128)(2,1)S(1)}, bf16[4,48,1152]{2,1,0:T(8,128)(2,1)S(1)}, u32[]{:S(2)}, u32[]{:S(2)}) collective-permute-start(bf16[4,48,1152]{2,1,0:T(8,128)(2,1)S(1)} %get-tuple-element.47), channel_id=1, source_target_pairs={{0,16},{1,65},{2,18},{3,67},{4,20},{5,69},{6,22},{7,71},{8,24},{9,... | collective-permute-start | bytes 1327112 | tf_op jit(solution)/shard_map/ppermute | solution.py:27
  29.1 13.7 %copy-start.2 = (bf16[1152,1152]{1,0:T(8,128)(2,1)S(1)}, bf16[1152,1152]{1,0:T(8,128)(2,1)}, u32[]{:S(2)}) copy-start(bf16[1152,1152]{1,0:T(8,128)(2,1)} %d0.1) | copy-start | bytes 7962628
  42.8 14.1 %collective-permute-start.13 = (bf16[1152,1152]{1,0:T(8,128)(2,1)S(1)}, bf16[1152,1152]{1,0:T(8,128)(2,1)S(1)}, u32[]{:S(2)}, u32[]{:S(2)}) collective-permute-start(bf16[1152,1152]{1,0:T(8,128)(2,1)S(1)} %copy-done.2), channel_id=1, source_target_pairs={{0,1},{1,0},{2,3},{3,2},{4,5},{5,4},{6,7},{7,6},{8,9},{9,8},{10,11... | collective-permute-start | bytes 7962632 | tf_op jit(solution)/shard_map/ppermute | solution.py:27
  42.9 6.9 %collective-permute-start.12 = (bf16[288,256]{1,0:T(8,128)(2,1)S(1)}, bf16[288,256]{1,0:T(8,128)(2,1)S(1)}, u32[]{:S(2)}, u32[]{:S(2)}) collective-permute-start(bf16[288,256]{1,0:T(8,128)(2,1)S(1)} %gate_up_silu.1.h0), channel_id=1, source_target_pairs={{0,2},{1,3},{2,4},{3,5},{4,6},{5,7},{6,0},{7,1},{8,10},{9,11},{10,... | collective-permute-start | bytes 442376 | tf_op jit(solution)/shard_map/ppermute | solution.py:27
  44.1 12.8 %collective-permute-start.11 = (bf16[288,256]{1,0:T(8,128)(2,1)S(1)}, bf16[288,256]{1,0:T(8,128)(2,1)S(1)}, u32[]{:S(2)}, u32[]{:S(2)}) collective-permute-start(bf16[288,256]{1,0:T(8,128)(2,1)S(1)} %gate_up_silu.1.h0), channel_id=1, source_target_pairs={{0,4},{1,5},{2,6},{3,7},{4,0},{5,1},{6,2},{7,3},{8,12},{9,13},{10,... | collective-permute-start | bytes 442376 | tf_op jit(solution)/shard_map/ppermute | solution.py:27
  45.4 11.6 %collective-permute-start.10 = (bf16[288,256]{1,0:T(8,128)(2,1)S(1)}, bf16[288,256]{1,0:T(8,128)(2,1)S(1)}, u32[]{:S(2)}, u32[]{:S(2)}) collective-permute-start(bf16[288,256]{1,0:T(8,128)(2,1)S(1)} %gate_up_silu.1.h0), channel_id=1, source_target_pairs={{0,6},{1,7},{2,0},{3,1},{4,2},{5,3},{6,4},{7,5},{8,14},{9,15},{10,... | collective-permute-start | bytes 442376 | tf_op jit(solution)/shard_map/ppermute | solution.py:27
  58.8 7.5 %collective-permute-start.14 = (bf16[2,64,1152]{2,1,0:T(8,128)(2,1)S(1)}, bf16[2,64,1152]{2,1,0:T(8,128)(2,1)S(1)}, u32[]{:S(2)}, u32[]{:S(2)}) collective-permute-start(bf16[2,64,1152]{2,1,0:T(8,128)(2,1)S(1)} %get-tuple-element.52), channel_id=1, source_target_pairs={{0,128},{1,33},{2,130},{3,35},{4,132},{5,37},{6,134},{7,39},{8,136... | collective-permute-start | bytes 884744 | tf_op jit(solution)/shard_map/ppermute | solution.py:27
  60.7 8.7 %collective-permute-start.15 = (bf16[2,64,1152]{2,1,0:T(8,128)(2,1)S(1)}, bf16[2,64,1152]{2,1,0:T(8,128)(2,1)S(1)}, u32[]{:S(2)}, u32[]{:S(2)}) collective-permute-start(bf16[2,64,1152]{2,1,0:T(8,128)(2,1)S(1)} %get-tuple-element.53), channel_id=1, source_target_pairs={{0,64},{1,17},{2,66},{3,19},{4,68},{5,21},{6,70},{7,23},{8,72},{9,... | collective-permute-start | bytes 884744 | tf_op jit(solution)/shard_map/ppermute | solution.py:27
  62.2 7.6 %collective-permute-start.16 = (bf16[2,64,1152]{2,1,0:T(8,128)(2,1)S(1)}, bf16[2,64,1152]{2,1,0:T(8,128)(2,1)S(1)}, u32[]{:S(2)}, u32[]{:S(2)}) collective-permute-start(bf16[2,64,1152]{2,1,0:T(8,128)(2,1)S(1)} %get-tuple-element.54), channel_id=1, source_target_pairs={{0,192},{1,49},{2,194},{3,51},{4,196},{5,53},{6,198},{7,55},{8,200... | collective-permute-start | bytes 884744 | tf_op jit(solution)/shard_map/ppermute | solution.py:27
  70.0 4.8 %collective-permute-start.17 = (bf16[2,16,1152]{2,1,0:T(8,128)(2,1)S(1)}, bf16[2,16,1152]{2,1,0:T(8,128)(2,1)S(1)}, u32[]{:S(2)}, u32[]{:S(2)}) collective-permute-start(bf16[2,16,1152]{2,1,0:T(8,128)(2,1)S(1)} %get-tuple-element.56), channel_id=1, source_target_pairs={{0,32},{1,129},{2,34},{3,131},{4,36},{5,133},{6,38},{7,135},{8,40}... | collective-permute-start | bytes 221192 | tf_op jit(solution)/shard_map/ppermute | solution.py:27
  71.6 4.7 %collective-permute-start.18 = (bf16[2,16,1152]{2,1,0:T(8,128)(2,1)S(1)}, bf16[2,16,1152]{2,1,0:T(8,128)(2,1)S(1)}, u32[]{:S(2)}, u32[]{:S(2)}) collective-permute-start(bf16[2,16,1152]{2,1,0:T(8,128)(2,1)S(1)} %get-tuple-element.57), channel_id=1, source_target_pairs={{0,16},{1,65},{2,18},{3,67},{4,20},{5,69},{6,22},{7,71},{8,24},{9,... | collective-permute-start | bytes 221192 | tf_op jit(solution)/shard_map/ppermute | solution.py:27
  71.9 4.4 %collective-permute-start.19 = (bf16[2,16,1152]{2,1,0:T(8,128)(2,1)S(1)}, bf16[2,16,1152]{2,1,0:T(8,128)(2,1)S(1)}, u32[]{:S(2)}, u32[]{:S(2)}) collective-permute-start(bf16[2,16,1152]{2,1,0:T(8,128)(2,1)S(1)} %get-tuple-element.58), channel_id=1, source_target_pairs={{0,48},{1,193},{2,50},{3,195},{4,52},{5,197},{6,54},{7,199},{8,56}... | collective-permute-start | bytes 221192 | tf_op jit(solution)/shard_map/ppermute | solution.py:27
  76.4 6.8 %collective-permute-start.20 = (bf16[16,1152]{1,0:T(8,128)(2,1)S(1)}, bf16[16,1152]{1,0:T(8,128)(2,1)S(1)}, u32[]{:S(2)}, u32[]{:S(2)}) collective-permute-start(bf16[16,1152]{1,0:T(8,128)(2,1)S(1)} %get-tuple-element.60), channel_id=1, source_target_pairs={{0,8},{1,9},{2,10},{3,11},{4,12},{5,13},{6,14},{7,15},{8,0},{9,1},... | collective-permute-start | bytes 110600 | tf_op jit(solution)/shard_map/ppermute | solution.py:27
  83.2 5.7 %collective-permute-start.21 = (bf16[8,1152]{1,0:T(8,128)(2,1)S(1)}, bf16[8,1152]{1,0:T(8,128)(2,1)S(1)}, u32[]{:S(2)}, u32[]{:S(2)}) collective-permute-start(bf16[8,1152]{1,0:T(8,128)(2,1)S(1)} %convert), channel_id=1, source_target_pairs={{0,1},{1,0},{2,3},{3,2},{4,5},{5,4},{6,7},{7,6},{8,9},{9,8},{10,11... | collective-permute-start | bytes 55304 | tf_op jit(solution)/shard_map/ppermute | solution.py:27

commit v5 on v4

--- a/solution.py
+++ b/solution.py
@@ -71,32 +71,57 @@
     return jnp.where(core == 0, x, y), jnp.where(core == 0, y, x)
 
 
-def _order_kernel(tokens, mine, theirs):
+def _order(tokens, out):
     x, y, _, _, c = _place()
-    for core, out in ((c, mine), (1 - c, theirs)):
-        first, second = _along(core, x, y)
-        for half, q in enumerate((first + 2 * second, 2 * first + second)):
-            for i in range(4):
-                a = lax.rem(q + i, 4)
-                base = 64 + half * 96 + (i - 1) * 32 if i else half * 32
-                for j in range(2):
-                    b = 2 * half + j
-                    block = jnp.where(core == 0, a * 4 + b, b * 4 + a)
-                    row = pl.multiple_of(block * 16, 16)
-                    out[pl.ds(base + j * 16, 16), :] = tokens[core, pl.ds(row, 16), :]
-
-
-def _order(tokens):
+    first, second = _along(c, x, y)
+    for half, q in enumerate((first + 2 * second, 2 * first + second)):
+        for i in range(4):
+            a = lax.rem(q + i, 4)
+            base = 64 + half * 96 + (i - 1) * 32 if i else half * 32
+            for j in range(2):
+                b = 2 * half + j
+                block = jnp.where(c == 0, a * 4 + b, b * 4 + a)
+                row = pl.multiple_of(block * 16, 16)
+                out[pl.ds(base + j * 16, 16), :] = tokens[c, pl.ds(row, 16), :]
+
+
+def _mine_kernel(tokens, mine):
+    _order(tokens, mine)
+
+
+def _mine(tokens):
     _, rows, width = tokens.shape
-    shape = jax.ShapeDtypeStruct((rows, width), BF16)
-    return pl.pallas_call(
-        _order_kernel,
+    return pl.pallas_call(
+        _mine_kernel,
         in_specs=[VMEM],
+        out_specs=VMEM,
+        out_shape=jax.ShapeDtypeStruct((rows, width), BF16),
+        compiler_params=pltpu.CompilerParams(vmem_limit_bytes=8 * MIB),
+        name="order_own",
+    )(tokens)
+
+
+def _join_kernel(mine, swapped, quarter, whole):
+    lead = quarter.shape[1]
+    whole[0] = mine[...]
+    _order(swapped, whole.at[1])
+    quarter[0] = mine[:lead]
+    quarter[1] = whole[1, :lead]
+
+
+def _join(mine, swapped):
+    rows, width = mine.shape
+    return pl.pallas_call(
+        _join_kernel,
+        in_specs=[VMEM] * 2,
         out_specs=[VMEM] * 2,
-        out_shape=[shape, shape],
+        out_shape=[
+            jax.ShapeDtypeStruct((2, rows // 4, width), BF16),
+            jax.ShapeDtypeStruct((2, rows, width), BF16),
+        ],
         compiler_params=pltpu.CompilerParams(vmem_limit_bytes=8 * MIB),
-        name="order_rows",
-    )(tokens)
+        name="order_other",
+    )(mine, swapped)
 
 
 def _weight_columns(weights, block, width):
@@ -108,23 +133,23 @@
     return jnp.concatenate([rows[:32], rows[64:160], rows[32:64], rows[160:]], axis=0)
 
 
-def _own_kernel(mine, other, g0, g1, u0, u1, out):
+def _own_kernel(whole, g0, g1, u0, u1, out):
     _, _, _, l, c = _place()
-    width = mine.shape[1]
-    for k, own in enumerate((mine, other)):
+    width = whole.shape[-1]
+    for k in range(2):
         w = _weight_columns((g0, g1, u0, u1), 2 * l + (c if k == 0 else 1 - c), width)
-        part = lax.dot_general(w, _in_order(own), NT, preferred_element_type=F32)
+        part = lax.dot_general(w, _in_order(whole[k]), NT, preferred_element_type=F32)
         if k == 0:
             out[...] = part
         else:
             out[...] += part
 
 
-def _own(mine, other, weights):
-    units, (rows, width) = weights[0].shape[0], mine.shape
+def _own(whole, weights):
+    units, (_, rows, width) = weights[0].shape[0], whole.shape
     return pl.pallas_call(
         _own_kernel,
-        in_specs=[VMEM] * 6,
+        in_specs=[VMEM] * 5,
         out_specs=VMEM,
         out_shape=jax.ShapeDtypeStruct((4 * units, rows), F32),
         compiler_params=pltpu.CompilerParams(vmem_limit_bytes=16 * MIB),
@@ -132,7 +157,7 @@
             flops=2 * 8 * units * rows * width, bytes_accessed=20 * units * width, transcendentals=0
         ),
         name="own_features",
-    )(mine, other, *weights)
+    )(whole, *weights)
 
 
 def _pack_kernel(near, two, first_back, first_on, second_back, second_on):
@@ -326,17 +351,16 @@
 
 def local(tokens, gate_weight, up_weight, down_weight):
     core = lax.axis_index("c")
-    mine, theirs = _order(tokens)
-    other = _permute(theirs, _swap)
-    quarter = jnp.stack([mine[:64], other[:64]])
+    swapped = _permute(tokens, _swap)
+    quarter, whole = _join(_mine(tokens), swapped)
     near = _permute(quarter, _up_or_down(1))
     two = _permute(quarter, _z_two)
-    gate_in, up_in, _ = lax.optimization_barrier((gate_weight, up_weight, other))
+    gate_in, up_in, _ = lax.optimization_barrier((gate_weight, up_weight, quarter))
     gate_other = _permute(gate_in, _swap)
     up_other = _permute(up_in, _swap)
     weights = (gate_weight, gate_other, up_weight, up_other)
-    whole, near, two = lax.optimization_barrier((jnp.stack([mine, other]), near, two))
-    direct = _permute(whole, _up_or_down(-1))
+    later, near, two = lax.optimization_barrier((whole, near, two))
+    direct = _permute(later, _up_or_down(-1))
 
     packed = _pack((near, two))
     packed, gate_other, up_other = lax.optimization_barrier((packed, gate_other, up_other))
@@ -347,8 +371,8 @@
         _permute(second_back, _second(-1)),
         _permute(second_on, _second(1)),
     ]
-    mine, _ = lax.optimization_barrier((mine, packed))
-    start = _own(mine, other, weights)
+    whole, _ = lax.optimization_barrier((whole, packed))
+    start = _own(whole, weights)
 
     hidden = _hidden((near, two), around, direct, start, weights)
     down_in, _ = lax.optimization_barrier((down_weight, hidden))

time: 90.3 us -> 89.9 us (level)
  waiting for transfers between devices: 46.3 us -> 44.4 us
  local copies, waits for them, and re-layouts: 1.46 us -> 3.03 us
    ppermute x22, waiting for transfers between devices: 46.3 us -> 44.4 us  [_permute(): return lax.ppermute(a, AXES, _perm(move))]
    unnamed x8 -> x10, local copies, waits for them, and re-layouts: 1.43 us -> 3.03 us
where the time goes in v5:
time: 89.9 us; the launch traced here: 89.1 us
  waiting for transfers between devices  44.4 us (49%)
  starting transfers between devices  34.9 us (39%)
  Pallas kernels  5.89 us (7%)
  local copies, waits for them, and re-layouts  3.03 us (3%)
    ppermute x22, waiting for transfers between devices, _permute(): return lax.ppermute(a, AXES, _perm(move))  44.4 us
    ppermute x22, starting transfers between devices, _permute(): return lax.ppermute(a, AXES, _perm(move))  34.9 us
    unnamed x10, local copies, waits for them, and re-layouts  3.03 us
    pallas_call x1, Pallas kernels, _hidden(): pl.pallas_call(_hidden_kernel, in_specs=[VMEM] * 12, out_specs=VMEM, out_...  2.56 us
    pallas_call x1, Pallas kernels, _down(): pl.pallas_call(_down_kernel, in_specs=[VMEM] * 6, out_specs=[VMEM] * 4, o...  1.91 us
  transfers between devices with their start and end apart: 22, of which 14 were waited for; matrix products, arithmetic and copies ran while one was open for 0% of the time, Pallas kernels for 1%

profile of v5, /device:TPU:1, one launch (start us, length us, event | category | flops | bytes accessed | tf_op | source)
XLA Modules:
  0.0 89.1 jit_solution(3954066368950607334)
XLA Ops:
  0.0 0.0 copy-start
  0.0 3.2 %collective-permute-start = (bf16[2,256,1152]{2,1,0:T(8,128)(2,1)}, bf16[2,256,1152]{2,1,0:T(8,128)(2,1)S(1)}, u32[]{:S(2)}, u32[]{:S(2)}) collective-permute-start(bf16[2,256,1152]{2,1,0:T(8,128)(2,1)} %tokens.1), channel_id=1, source_target_pairs={{0,1},{1,0},{2,3},{3,2},{4,5},{5,4},{6,7},{7,6},{8,9},{9,8},{10,11... | collective-permute-start | bytes 3538952 | tf_op jit(solution)/shard_map/ppermute | solution.py:27
  3.2 0.0 copy-start.4
  3.2 1.3 %copy-done.4 = bf16[2,256,1152]{2,1,0:T(8,128)(2,1)S(1)} copy-done((bf16[2,256,1152]{2,1,0:T(8,128)(2,1)S(1)}, bf16[2,256,1152]{2,1,0:T(8,128)(2,1)}, u32[]{:S(2)}) %copy-start.4) | copy-done | bytes 1179672
  4.5 0.1 order_own.1.mine
  4.6 1.4 %collective-permute-done.swapped = bf16[2,256,1152]{2,1,0:T(8,128)(2,1)S(1)} collective-permute-done((bf16[2,256,1152]{2,1,0:T(8,128)(2,1)}, bf16[2,256,1152]{2,1,0:T(8,128)(2,1)S(1)}, u32[]{:S(2)}, u32[]{:S(2)}) %collective-permute-start) | collective-permute-done | bytes 1179680 | tf_op jit(solution)/shard_map/ppermute | solution.py:27
  5.9 0.1 order_other.1
  6.0 0.0 copy-done
  6.1 0.5 collective-permute-start.3
  6.5 0.1 collective-permute-start.4
  6.7 1.3 %collective-permute-start.2 = (bf16[2,64,1152]{2,1,0:T(8,128)(2,1)S(1)}, bf16[2,64,1152]{2,1,0:T(8,128)(2,1)S(1)}, u32[]{:S(2)}, u32[]{:S(2)}) collective-permute-start(bf16[2,64,1152]{2,1,0:T(8,128)(2,1)S(1)} %get-tuple-element.35), channel_id=1, source_target_pairs={{0,4},{1,5},{2,14},{3,15},{4,8},{5,9},{6,2},{7,3},{8,12},{9,13},{1... | collective-permute-start | bytes 884744 | tf_op jit(solution)/shard_map/ppermute | solution.py:27
  7.9 3.8 %collective-permute-start.1 = (bf16[2,64,1152]{2,1,0:T(8,128)(2,1)S(1)}, bf16[2,64,1152]{2,1,0:T(8,128)(2,1)S(1)}, u32[]{:S(2)}, u32[]{:S(2)}) collective-permute-start(bf16[2,64,1152]{2,1,0:T(8,128)(2,1)S(1)} %get-tuple-element.35), channel_id=1, source_target_pairs={{0,2},{1,15},{2,4},{3,1},{4,6},{5,3},{6,8},{7,5},{8,10},{9,7},{10,... | collective-permute-start | bytes 884744 | tf_op jit(solution)/shard_map/ppermute | solution.py:27
  11.7 6.4 %collective-permute-done.2.two = bf16[2,64,1152]{2,1,0:T(8,128)(2,1)S(1)} collective-permute-done((bf16[2,64,1152]{2,1,0:T(8,128)(2,1)S(1)}, bf16[2,64,1152]{2,1,0:T(8,128)(2,1)S(1)}, u32[]{:S(2)}, u32[]{:S(2)}) %collective-permute-start.2) | collective-permute-done | bytes 294944 | tf_op jit(solution)/shard_map/ppermute | solution.py:27
  18.1 4.1 %collective-permute-done.1.near = bf16[2,64,1152]{2,1,0:T(8,128)(2,1)S(1)} collective-permute-done((bf16[2,64,1152]{2,1,0:T(8,128)(2,1)S(1)}, bf16[2,64,1152]{2,1,0:T(8,128)(2,1)S(1)}, u32[]{:S(2)}, u32[]{:S(2)}) %collective-permute-start.1) | collective-permute-done | bytes 294944 | tf_op jit(solution)/shard_map/ppermute | solution.py:27
  22.1 0.0 collective-permute-start.9
  22.2 0.1 pack_quarters.1
  22.3 0.0 collective-permute-done.3.g1
  22.3 0.0 collective-permute-done.4.u1
  22.3 2.8 %collective-permute-start.5 = (bf16[4,48,1152]{2,1,0:T(8,128)(2,1)S(1)}, bf16[4,48,1152]{2,1,0:T(8,128)(2,1)S(1)}, u32[]{:S(2)}, u32[]{:S(2)}) collective-permute-start(bf16[4,48,1152]{2,1,0:T(8,128)(2,1)S(1)} %get-tuple-element.44), channel_id=1, source_target_pairs={{0,192},{1,49},{2,194},{3,51},{4,196},{5,53},{6,198},{7,55},{8,200... | collective-permute-start | bytes 1327112 | tf_op jit(solution)/shard_map/ppermute | solution.py:27
  25.1 0.0 collective-permute-start.6
  25.1 2.5 %collective-permute-start.7 = (bf16[4,48,1152]{2,1,0:T(8,128)(2,1)S(1)}, bf16[4,48,1152]{2,1,0:T(8,128)(2,1)S(1)}, u32[]{:S(2)}, u32[]{:S(2)}) collective-permute-start(bf16[4,48,1152]{2,1,0:T(8,128)(2,1)S(1)} %get-tuple-element.46), channel_id=1, source_target_pairs={{0,48},{1,193},{2,50},{3,195},{4,52},{5,197},{6,54},{7,199},{8,56}... | collective-permute-start | bytes 1327112 | tf_op jit(solution)/shard_map/ppermute | solution.py:27
  27.6 0.0 collective-permute-start.8
  27.6 0.0 copy-start.1
  27.6 1.7 %copy-done.1 = bf16[144,9216]{1,0:T(8,128)(2,1)S(1)} copy-done((bf16[144,9216]{1,0:T(8,128)(2,1)S(1)}, bf16[144,9216]{1,0:T(8,128)(2,1)}, u32[]{:S(2)}) %copy-start.1) | copy-done | bytes 2654232
  29.4 0.0 copy-start.2
  29.4 0.9 %own_features.1.start = f32[576,256]{1,0:T(8,128)S(1)} custom-call(bf16[2,256,1152]{2,1,0:T(8,128)(2,1)S(1)} %get-tuple-element.49.whole, bf16[144,9216]{1,0:T(8,128)(2,1)S(1)} %copy-done, bf16[144,9216]{1,0:T(8,128)(2,1)S(1)} %collective-permute-done.3.g1, bf16[144,9216]{1,0:T(8,128)(2,1)S(1)} %copy-done.1, bf16[144,9216]{1,0:T(8,128)(2,1)S(1)} %collective-permute-done.4.u1), custom_call_target="tpu_custom_call" | custom-call | flops 679477248 | bytes 3317760 | tf_op jit(solution)/shard_map/own_features/pallas_call | solution.py:150
  30.3 0.0 copy-start.3
  30.3 8.4 %collective-permute-done.9.direct = bf16[2,256,1152]{2,1,0:T(8,128)(2,1)S(1)} collective-permute-done((bf16[2,256,1152]{2,1,0:T(8,128)(2,1)S(1)}, bf16[2,256,1152]{2,1,0:T(8,128)(2,1)S(1)}, u32[]{:S(2)}, u32[]{:S(2)}) %collective-permute-start.9) | collective-permute-done | bytes 1179680 | tf_op jit(solution)/shard_map/ppermute | solution.py:27
  38.7 0.0 collective-permute-done.5.p1
  38.7 0.0 collective-permute-done.6.m1
  38.7 0.0 collective-permute-done.7.p2
  38.7 1.0 %collective-permute-done.8.m2 = bf16[4,48,1152]{2,1,0:T(8,128)(2,1)S(1)} collective-permute-done((bf16[4,48,1152]{2,1,0:T(8,128)(2,1)S(1)}, bf16[4,48,1152]{2,1,0:T(8,128)(2,1)S(1)}, u32[]{:S(2)}, u32[]{:S(2)}) %collective-permute-start.8) | collective-permute-done | bytes 442400 | tf_op jit(solution)/shard_map/ppermute | solution.py:27
  39.7 0.0 copy-done.2
  39.7 2.6 %gate_up_silu.1.h0 = bf16[288,256]{1,0:T(8,128)(2,1)S(1)} custom-call(bf16[2,64,1152]{2,1,0:T(8,128)(2,1)S(1)} %collective-permute-done.1.near, bf16[2,64,1152]{2,1,0:T(8,128)(2,1)S(1)} %collective-permute-done.2.two, bf16[4,48,1152]{2,1,0:T(8,128)(2,1)S(1)} %collective-permute-done.5.p1, bf16[4,48,1152]{2,1,0:T(8,128)(2,1)S(1)} %collective-permute-done.6.m1, ...), custom_call_target="tpu_custom_call" | custom-call | flops 2038431744 | bytes 7962624 | tf_op jit(solution)/shard_map/gate_up_silu/pallas_call | solution.py:233
  42.3 0.0 copy-done.3
  42.3 0.1 collective-permute-start.13
  42.4 1.2 %collective-permute-start.12 = (bf16[288,256]{1,0:T(8,128)(2,1)S(1)}, bf16[288,256]{1,0:T(8,128)(2,1)S(1)}, u32[]{:S(2)}, u32[]{:S(2)}) collective-permute-start(bf16[288,256]{1,0:T(8,128)(2,1)S(1)} %gate_up_silu.1.h0), channel_id=1, source_target_pairs={{0,2},{1,3},{2,4},{3,5},{4,6},{5,7},{6,0},{7,1},{8,10},{9,11},{10,... | collective-permute-start | bytes 442376 | tf_op jit(solution)/shard_map/ppermute | solution.py:27
  43.6 1.2 %collective-permute-start.11 = (bf16[288,256]{1,0:T(8,128)(2,1)S(1)}, bf16[288,256]{1,0:T(8,128)(2,1)S(1)}, u32[]{:S(2)}, u32[]{:S(2)}) collective-permute-start(bf16[288,256]{1,0:T(8,128)(2,1)S(1)} %gate_up_silu.1.h0), channel_id=1, source_target_pairs={{0,4},{1,5},{2,6},{3,7},{4,0},{5,1},{6,2},{7,3},{8,12},{9,13},{10,... | collective-permute-start | bytes 442376 | tf_op jit(solution)/shard_map/ppermute | solution.py:27
  44.9 0.9 collective-permute-start.10
  45.7 3.6 %collective-permute-done.12.h3 = bf16[288,256]{1,0:T(8,128)(2,1)S(1)} collective-permute-done((bf16[288,256]{1,0:T(8,128)(2,1)S(1)}, bf16[288,256]{1,0:T(8,128)(2,1)S(1)}, u32[]{:S(2)}, u32[]{:S(2)}) %collective-permute-start.12) | collective-permute-done | bytes 147488 | tf_op jit(solution)/shard_map/ppermute | solution.py:27
  49.3 7.1 %collective-permute-done.11.h2 = bf16[288,256]{1,0:T(8,128)(2,1)S(1)} collective-permute-done((bf16[288,256]{1,0:T(8,128)(2,1)S(1)}, bf16[288,256]{1,0:T(8,128)(2,1)S(1)}, u32[]{:S(2)}, u32[]{:S(2)}) %collective-permute-start.11) | collective-permute-done | bytes 147488 | tf_op jit(solution)/shard_map/ppermute | solution.py:27
  56.4 0.0 collective-permute-done.10.h1
  56.4 0.0 collective-permute-done.13.d1
  56.4 1.9 %down.1 = (f32[2,64,1152]{2,1,0:T(8,128)S(1)}, bf16[2,64,1152]{2,1,0:T(8,128)(2,1)S(1)}, bf16[2,64,1152]{2,1,0:T(8,128)(2,1)S(1)}, bf16[2,64,1152]{2,1,0:T(8,128)(2,1)S(1)}) custom-call(bf16[288,256]{1,0:T(8,128)(2,1)S(1)} %gate_up_silu.1.h0, bf16[288,256]{1,0:T(8,128)(2,1)S(1)} %collective-permute-done.10.h1, ...), custom_call_target="tpu_custom_call" | custom-call | flops 1358954496 | bytes 5308416 | tf_op jit(solution)/shard_map/down/pallas_call | solution.py:273
  58.3 1.9 %collective-permute-start.14 = (bf16[2,64,1152]{2,1,0:T(8,128)(2,1)S(1)}, bf16[2,64,1152]{2,1,0:T(8,128)(2,1)S(1)}, u32[]{:S(2)}, u32[]{:S(2)}) collective-permute-start(bf16[2,64,1152]{2,1,0:T(8,128)(2,1)S(1)} %get-tuple-element.52), channel_id=1, source_target_pairs={{0,128},{1,33},{2,130},{3,35},{4,132},{5,37},{6,134},{7,39},{8,136... | collective-permute-start | bytes 884744 | tf_op jit(solution)/shard_map/ppermute | solution.py:27
  60.2 1.5 %collective-permute-start.15 = (bf16[2,64,1152]{2,1,0:T(8,128)(2,1)S(1)}, bf16[2,64,1152]{2,1,0:T(8,128)(2,1)S(1)}, u32[]{:S(2)}, u32[]{:S(2)}) collective-permute-start(bf16[2,64,1152]{2,1,0:T(8,128)(2,1)S(1)} %get-tuple-element.53), channel_id=1, source_target_pairs={{0,64},{1,17},{2,66},{3,19},{4,68},{5,21},{6,70},{7,23},{8,72},{9,... | collective-permute-start | bytes 884744 | tf_op jit(solution)/shard_map/ppermute | solution.py:27
  61.7 1.2 %collective-permute-start.16 = (bf16[2,64,1152]{2,1,0:T(8,128)(2,1)S(1)}, bf16[2,64,1152]{2,1,0:T(8,128)(2,1)S(1)}, u32[]{:S(2)}, u32[]{:S(2)}) collective-permute-start(bf16[2,64,1152]{2,1,0:T(8,128)(2,1)S(1)} %get-tuple-element.54), channel_id=1, source_target_pairs={{0,192},{1,49},{2,194},{3,51},{4,196},{5,53},{6,198},{7,55},{8,200... | collective-permute-start | bytes 884744 | tf_op jit(solution)/shard_map/ppermute | solution.py:27
  62.9 2.9 %collective-permute-done.14.g1 = bf16[2,64,1152]{2,1,0:T(8,128)(2,1)S(1)} collective-permute-done((bf16[2,64,1152]{2,1,0:T(8,128)(2,1)S(1)}, bf16[2,64,1152]{2,1,0:T(8,128)(2,1)S(1)}, u32[]{:S(2)}, u32[]{:S(2)}) %collective-permute-start.14) | collective-permute-done | bytes 294944 | tf_op jit(solution)/shard_map/ppermute | solution.py:27
  65.8 3.1 %collective-permute-done.15.g2 = bf16[2,64,1152]{2,1,0:T(8,128)(2,1)S(1)} collective-permute-done((bf16[2,64,1152]{2,1,0:T(8,128)(2,1)S(1)}, bf16[2,64,1152]{2,1,0:T(8,128)(2,1)S(1)}, u32[]{:S(2)}, u32[]{:S(2)}) %collective-permute-start.15) | collective-permute-done | bytes 294944 | tf_op jit(solution)/shard_map/ppermute | solution.py:27
  69.0 0.4 collective-permute-done.16.g3
  69.3 0.1 sum_first.1
  69.5 1.6 %collective-permute-start.17 = (bf16[2,16,1152]{2,1,0:T(8,128)(2,1)S(1)}, bf16[2,16,1152]{2,1,0:T(8,128)(2,1)S(1)}, u32[]{:S(2)}, u32[]{:S(2)}) collective-permute-start(bf16[2,16,1152]{2,1,0:T(8,128)(2,1)S(1)} %get-tuple-element.56), channel_id=1, source_target_pairs={{0,32},{1,129},{2,34},{3,131},{4,36},{5,133},{6,38},{7,135},{8,40}... | collective-permute-start | bytes 221192 | tf_op jit(solution)/shard_map/ppermute | solution.py:27
  71.1 0.3 collective-permute-start.18
  71.4 2.4 %collective-permute-start.19 = (bf16[2,16,1152]{2,1,0:T(8,128)(2,1)S(1)}, bf16[2,16,1152]{2,1,0:T(8,128)(2,1)S(1)}, u32[]{:S(2)}, u32[]{:S(2)}) collective-permute-start(bf16[2,16,1152]{2,1,0:T(8,128)(2,1)S(1)} %get-tuple-element.58), channel_id=1, source_target_pairs={{0,48},{1,193},{2,50},{3,195},{4,52},{5,197},{6,54},{7,199},{8,56}... | collective-permute-start | bytes 221192 | tf_op jit(solution)/shard_map/ppermute | solution.py:27
  73.8 0.5 collective-permute-done.17.g1
  74.3 1.6 %collective-permute-done.18.g2 = bf16[2,16,1152]{2,1,0:T(8,128)(2,1)S(1)} collective-permute-done((bf16[2,16,1152]{2,1,0:T(8,128)(2,1)S(1)}, bf16[2,16,1152]{2,1,0:T(8,128)(2,1)S(1)}, u32[]{:S(2)}, u32[]{:S(2)}) %collective-permute-start.18) | collective-permute-done | bytes 73760 | tf_op jit(solution)/shard_map/ppermute | solution.py:27
  75.8 0.0 collective-permute-done.19.g3
  75.9 3.6 %collective-permute-start.20 = (bf16[16,1152]{1,0:T(8,128)(2,1)S(1)}, bf16[16,1152]{1,0:T(8,128)(2,1)S(1)}, u32[]{:S(2)}, u32[]{:S(2)}) collective-permute-start(bf16[16,1152]{1,0:T(8,128)(2,1)S(1)} %get-tuple-element.60), channel_id=1, source_target_pairs={{0,8},{1,9},{2,10},{3,11},{4,12},{5,13},{6,14},{7,15},{8,0},{9,1},... | collective-permute-start | bytes 110600 | tf_op jit(solution)/shard_map/ppermute | solution.py:27
  79.4 3.2 %collective-permute-done.20.got = bf16[16,1152]{1,0:T(8,128)(2,1)S(1)} collective-permute-done((bf16[16,1152]{1,0:T(8,128)(2,1)S(1)}, bf16[16,1152]{1,0:T(8,128)(2,1)S(1)}, u32[]{:S(2)}, u32[]{:S(2)}) %collective-permute-start.20) | collective-permute-done | bytes 36896 | tf_op jit(solution)/shard_map/ppermute | solution.py:27
  82.7 4.9 %collective-permute-start.21 = (bf16[8,1152]{1,0:T(8,128)(2,1)S(1)}, bf16[8,1152]{1,0:T(8,128)(2,1)S(1)}, u32[]{:S(2)}, u32[]{:S(2)}) collective-permute-start(bf16[8,1152]{1,0:T(8,128)(2,1)S(1)} %convert), channel_id=1, source_target_pairs={{0,1},{1,0},{2,3},{3,2},{4,5},{5,4},{6,7},{7,6},{8,9},{9,8},{10,11... | collective-permute-start | bytes 55304 | tf_op jit(solution)/shard_map/ppermute | solution.py:27
  87.6 0.8 collective-permute-done.21
  88.4 0.7 select_convert_fusion
  (4 shorter events, 0.1 us)
Async XLA Ops:
  0.0 6.0 %copy-start = (bf16[144,9216]{1,0:T(8,128)(2,1)S(1)}, bf16[144,9216]{1,0:T(8,128)(2,1)}, u32[]{:S(2)}) copy-start(bf16[144,9216]{1,0:T(8,128)(2,1)} %g0.3) | copy-start | bytes 7962628
  0.0 5.9 %collective-permute-start = (bf16[2,256,1152]{2,1,0:T(8,128)(2,1)}, bf16[2,256,1152]{2,1,0:T(8,128)(2,1)S(1)}, u32[]{:S(2)}, u32[]{:S(2)}) collective-permute-start(bf16[2,256,1152]{2,1,0:T(8,128)(2,1)} %tokens.1), channel_id=1, source_target_pairs={{0,1},{1,0},{2,3},{3,2},{4,5},{5,4},{6,7},{7,6},{8,9},{9,8},{10,11... | collective-permute-start | bytes 3538952 | tf_op jit(solution)/shard_map/ppermute | solution.py:27
  3.2 1.3 %copy-start.4 = (bf16[2,256,1152]{2,1,0:T(8,128)(2,1)S(1)}, bf16[2,256,1152]{2,1,0:T(8,128)(2,1)}, u32[]{:S(2)}) copy-start(bf16[2,256,1152]{2,1,0:T(8,128)(2,1)} %tokens.1) | copy-start | bytes 3538948
  6.1 16.2 %collective-permute-start.3 = (bf16[144,9216]{1,0:T(8,128)(2,1)S(1)}, bf16[144,9216]{1,0:T(8,128)(2,1)S(1)}, u32[]{:S(2)}, u32[]{:S(2)}) collective-permute-start(bf16[144,9216]{1,0:T(8,128)(2,1)S(1)} %copy-done), channel_id=1, source_target_pairs={{0,1},{1,0},{2,3},{3,2},{4,5},{5,4},{6,7},{7,6},{8,9},{9,8},{10,11... | collective-permute-start | bytes 7962632 | tf_op jit(solution)/shard_map/ppermute | solution.py:27
  6.5 15.8 %collective-permute-start.4 = (bf16[144,9216]{1,0:T(8,128)(2,1)}, bf16[144,9216]{1,0:T(8,128)(2,1)S(1)}, u32[]{:S(2)}, u32[]{:S(2)}) collective-permute-start(bf16[144,9216]{1,0:T(8,128)(2,1)} %u0.3), channel_id=1, source_target_pairs={{0,1},{1,0},{2,3},{3,2},{4,5},{5,4},{6,7},{7,6},{8,9},{9,8},{10,11... | collective-permute-start | bytes 7962632 | tf_op jit(solution)/shard_map/ppermute | solution.py:27
  6.7 11.4 %collective-permute-start.2 = (bf16[2,64,1152]{2,1,0:T(8,128)(2,1)S(1)}, bf16[2,64,1152]{2,1,0:T(8,128)(2,1)S(1)}, u32[]{:S(2)}, u32[]{:S(2)}) collective-permute-start(bf16[2,64,1152]{2,1,0:T(8,128)(2,1)S(1)} %get-tuple-element.35), channel_id=1, source_target_pairs={{0,4},{1,5},{2,14},{3,15},{4,8},{5,9},{6,2},{7,3},{8,12},{9,13},{1... | collective-permute-start | bytes 884744 | tf_op jit(solution)/shard_map/ppermute | solution.py:27
  7.9 14.2 %collective-permute-start.1 = (bf16[2,64,1152]{2,1,0:T(8,128)(2,1)S(1)}, bf16[2,64,1152]{2,1,0:T(8,128)(2,1)S(1)}, u32[]{:S(2)}, u32[]{:S(2)}) collective-permute-start(bf16[2,64,1152]{2,1,0:T(8,128)(2,1)S(1)} %get-tuple-element.35), channel_id=1, source_target_pairs={{0,2},{1,15},{2,4},{3,1},{4,6},{5,3},{6,8},{7,5},{8,10},{9,7},{10,... | collective-permute-start | bytes 884744 | tf_op jit(solution)/shard_map/ppermute | solution.py:27
  22.1 16.6 %collective-permute-start.9 = (bf16[2,256,1152]{2,1,0:T(8,128)(2,1)S(1)}, bf16[2,256,1152]{2,1,0:T(8,128)(2,1)S(1)}, u32[]{:S(2)}, u32[]{:S(2)}) collective-permute-start(bf16[2,256,1152]{2,1,0:T(8,128)(2,1)S(1)} %get-tuple-element.49.whole), channel_id=1, source_target_pairs={{0,14},{1,3},{2,0},{3,5},{4,2},{5,7},{6,4},{7,9},{8,6},{9,11},{10,... | collective-permute-start | bytes 3538952 | tf_op jit(solution)/shard_map/ppermute | solution.py:27
  22.3 16.4 %collective-permute-start.5 = (bf16[4,48,1152]{2,1,0:T(8,128)(2,1)S(1)}, bf16[4,48,1152]{2,1,0:T(8,128)(2,1)S(1)}, u32[]{:S(2)}, u32[]{:S(2)}) collective-permute-start(bf16[4,48,1152]{2,1,0:T(8,128)(2,1)S(1)} %get-tuple-element.44), channel_id=1, source_target_pairs={{0,192},{1,49},{2,194},{3,51},{4,196},{5,53},{6,198},{7,55},{8,200... | collective-permute-start | bytes 1327112 | tf_op jit(solution)/shard_map/ppermute | solution.py:27
  25.1 13.6 %collective-permute-start.6 = (bf16[4,48,1152]{2,1,0:T(8,128)(2,1)S(1)}, bf16[4,48,1152]{2,1,0:T(8,128)(2,1)S(1)}, u32[]{:S(2)}, u32[]{:S(2)}) collective-permute-start(bf16[4,48,1152]{2,1,0:T(8,128)(2,1)S(1)} %get-tuple-element.45), channel_id=1, source_target_pairs={{0,64},{1,17},{2,66},{3,19},{4,68},{5,21},{6,70},{7,23},{8,72},{9,... | collective-permute-start | bytes 1327112 | tf_op jit(solution)/shard_map/ppermute | solution.py:27
  25.1 13.6 %collective-permute-start.7 = (bf16[4,48,1152]{2,1,0:T(8,128)(2,1)S(1)}, bf16[4,48,1152]{2,1,0:T(8,128)(2,1)S(1)}, u32[]{:S(2)}, u32[]{:S(2)}) collective-permute-start(bf16[4,48,1152]{2,1,0:T(8,128)(2,1)S(1)} %get-tuple-element.46), channel_id=1, source_target_pairs={{0,48},{1,193},{2,50},{3,195},{4,52},{5,197},{6,54},{7,199},{8,56}... | collective-permute-start | bytes 1327112 | tf_op jit(solution)/shard_map/ppermute | solution.py:27
  27.6 12.1 %collective-permute-start.8 = (bf16[4,48,1152]{2,1,0:T(8,128)(2,1)S(1)}, bf16[4,48,1152]{2,1,0:T(8,128)(2,1)S(1)}, u32[]{:S(2)}, u32[]{:S(2)}) collective-permute-start(bf16[4,48,1152]{2,1,0:T(8,128)(2,1)S(1)} %get-tuple-element.47), channel_id=1, source_target_pairs={{0,16},{1,65},{2,18},{3,67},{4,20},{5,69},{6,22},{7,71},{8,24},{9,... | collective-permute-start | bytes 1327112 | tf_op jit(solution)/shard_map/ppermute | solution.py:27
  27.6 1.8 %copy-start.1 = (bf16[144,9216]{1,0:T(8,128)(2,1)S(1)}, bf16[144,9216]{1,0:T(8,128)(2,1)}, u32[]{:S(2)}) copy-start(bf16[144,9216]{1,0:T(8,128)(2,1)} %u0.3) | copy-start | bytes 7962628
  29.4 10.4 %copy-start.2 = (bf16[144,9216]{1,0:T(8,128)(2,1)S(1)}, bf16[144,9216]{1,0:T(8,128)(2,1)}, u32[]{:S(2)}) copy-start(bf16[144,9216]{1,0:T(8,128)(2,1)} %u0.3) | copy-start | bytes 7962628
  30.3 12.0 %copy-start.3 = (bf16[1152,1152]{1,0:T(8,128)(2,1)S(1)}, bf16[1152,1152]{1,0:T(8,128)(2,1)}, u32[]{:S(2)}) copy-start(bf16[1152,1152]{1,0:T(8,128)(2,1)} %d0.1) | copy-start | bytes 7962628
  42.3 14.1 %collective-permute-start.13 = (bf16[1152,1152]{1,0:T(8,128)(2,1)S(1)}, bf16[1152,1152]{1,0:T(8,128)(2,1)S(1)}, u32[]{:S(2)}, u32[]{:S(2)}) collective-permute-start(bf16[1152,1152]{1,0:T(8,128)(2,1)S(1)} %copy-done.3), channel_id=1, source_target_pairs={{0,1},{1,0},{2,3},{3,2},{4,5},{5,4},{6,7},{7,6},{8,9},{9,8},{10,11... | collective-permute-start | bytes 7962632 | tf_op jit(solution)/shard_map/ppermute | solution.py:27
  42.4 6.9 %collective-permute-start.12 = (bf16[288,256]{1,0:T(8,128)(2,1)S(1)}, bf16[288,256]{1,0:T(8,128)(2,1)S(1)}, u32[]{:S(2)}, u32[]{:S(2)}) collective-permute-start(bf16[288,256]{1,0:T(8,128)(2,1)S(1)} %gate_up_silu.1.h0), channel_id=1, source_target_pairs={{0,2},{1,3},{2,4},{3,5},{4,6},{5,7},{6,0},{7,1},{8,10},{9,11},{10,... | collective-permute-start | bytes 442376 | tf_op jit(solution)/shard_map/ppermute | solution.py:27
  43.6 12.8 %collective-permute-start.11 = (bf16[288,256]{1,0:T(8,128)(2,1)S(1)}, bf16[288,256]{1,0:T(8,128)(2,1)S(1)}, u32[]{:S(2)}, u32[]{:S(2)}) collective-permute-start(bf16[288,256]{1,0:T(8,128)(2,1)S(1)} %gate_up_silu.1.h0), channel_id=1, source_target_pairs={{0,4},{1,5},{2,6},{3,7},{4,0},{5,1},{6,2},{7,3},{8,12},{9,13},{10,... | collective-permute-start | bytes 442376 | tf_op jit(solution)/shard_map/ppermute | solution.py:27
  44.9 11.6 %collective-permute-start.10 = (bf16[288,256]{1,0:T(8,128)(2,1)S(1)}, bf16[288,256]{1,0:T(8,128)(2,1)S(1)}, u32[]{:S(2)}, u32[]{:S(2)}) collective-permute-start(bf16[288,256]{1,0:T(8,128)(2,1)S(1)} %gate_up_silu.1.h0), channel_id=1, source_target_pairs={{0,6},{1,7},{2,0},{3,1},{4,2},{5,3},{6,4},{7,5},{8,14},{9,15},{10,... | collective-permute-start | bytes 442376 | tf_op jit(solution)/shard_map/ppermute | solution.py:27
  58.3 7.5 %collective-permute-start.14 = (bf16[2,64,1152]{2,1,0:T(8,128)(2,1)S(1)}, bf16[2,64,1152]{2,1,0:T(8,128)(2,1)S(1)}, u32[]{:S(2)}, u32[]{:S(2)}) collective-permute-start(bf16[2,64,1152]{2,1,0:T(8,128)(2,1)S(1)} %get-tuple-element.52), channel_id=1, source_target_pairs={{0,128},{1,33},{2,130},{3,35},{4,132},{5,37},{6,134},{7,39},{8,136... | collective-permute-start | bytes 884744 | tf_op jit(solution)/shard_map/ppermute | solution.py:27
  60.2 8.7 %collective-permute-start.15 = (bf16[2,64,1152]{2,1,0:T(8,128)(2,1)S(1)}, bf16[2,64,1152]{2,1,0:T(8,128)(2,1)S(1)}, u32[]{:S(2)}, u32[]{:S(2)}) collective-permute-start(bf16[2,64,1152]{2,1,0:T(8,128)(2,1)S(1)} %get-tuple-element.53), channel_id=1, source_target_pairs={{0,64},{1,17},{2,66},{3,19},{4,68},{5,21},{6,70},{7,23},{8,72},{9,... | collective-permute-start | bytes 884744 | tf_op jit(solution)/shard_map/ppermute | solution.py:27
  61.7 7.6 %collective-permute-start.16 = (bf16[2,64,1152]{2,1,0:T(8,128)(2,1)S(1)}, bf16[2,64,1152]{2,1,0:T(8,128)(2,1)S(1)}, u32[]{:S(2)}, u32[]{:S(2)}) collective-permute-start(bf16[2,64,1152]{2,1,0:T(8,128)(2,1)S(1)} %get-tuple-element.54), channel_id=1, source_target_pairs={{0,192},{1,49},{2,194},{3,51},{4,196},{5,53},{6,198},{7,55},{8,200... | collective-permute-start | bytes 884744 | tf_op jit(solution)/shard_map/ppermute | solution.py:27
  69.5 4.8 %collective-permute-start.17 = (bf16[2,16,1152]{2,1,0:T(8,128)(2,1)S(1)}, bf16[2,16,1152]{2,1,0:T(8,128)(2,1)S(1)}, u32[]{:S(2)}, u32[]{:S(2)}) collective-permute-start(bf16[2,16,1152]{2,1,0:T(8,128)(2,1)S(1)} %get-tuple-element.56), channel_id=1, source_target_pairs={{0,32},{1,129},{2,34},{3,131},{4,36},{5,133},{6,38},{7,135},{8,40}... | collective-permute-start | bytes 221192 | tf_op jit(solution)/shard_map/ppermute | solution.py:27
  71.1 4.7 %collective-permute-start.18 = (bf16[2,16,1152]{2,1,0:T(8,128)(2,1)S(1)}, bf16[2,16,1152]{2,1,0:T(8,128)(2,1)S(1)}, u32[]{:S(2)}, u32[]{:S(2)}) collective-permute-start(bf16[2,16,1152]{2,1,0:T(8,128)(2,1)S(1)} %get-tuple-element.57), channel_id=1, source_target_pairs={{0,16},{1,65},{2,18},{3,67},{4,20},{5,69},{6,22},{7,71},{8,24},{9,... | collective-permute-start | bytes 221192 | tf_op jit(solution)/shard_map/ppermute | solution.py:27
  71.4 4.4 %collective-permute-start.19 = (bf16[2,16,1152]{2,1,0:T(8,128)(2,1)S(1)}, bf16[2,16,1152]{2,1,0:T(8,128)(2,1)S(1)}, u32[]{:S(2)}, u32[]{:S(2)}) collective-permute-start(bf16[2,16,1152]{2,1,0:T(8,128)(2,1)S(1)} %get-tuple-element.58), channel_id=1, source_target_pairs={{0,48},{1,193},{2,50},{3,195},{4,52},{5,197},{6,54},{7,199},{8,56}... | collective-permute-start | bytes 221192 | tf_op jit(solution)/shard_map/ppermute | solution.py:27
  75.9 6.8 %collective-permute-start.20 = (bf16[16,1152]{1,0:T(8,128)(2,1)S(1)}, bf16[16,1152]{1,0:T(8,128)(2,1)S(1)}, u32[]{:S(2)}, u32[]{:S(2)}) collective-permute-start(bf16[16,1152]{1,0:T(8,128)(2,1)S(1)} %get-tuple-element.60), channel_id=1, source_target_pairs={{0,8},{1,9},{2,10},{3,11},{4,12},{5,13},{6,14},{7,15},{8,0},{9,1},... | collective-permute-start | bytes 110600 | tf_op jit(solution)/shard_map/ppermute | solution.py:27
  82.7 5.7 %collective-permute-start.21 = (bf16[8,1152]{1,0:T(8,128)(2,1)S(1)}, bf16[8,1152]{1,0:T(8,128)(2,1)S(1)}, u32[]{:S(2)}, u32[]{:S(2)}) collective-permute-start(bf16[8,1152]{1,0:T(8,128)(2,1)S(1)} %convert), channel_id=1, source_target_pairs={{0,1},{1,0},{2,3},{3,2},{4,5},{5,4},{6,7},{7,6},{8,9},{9,8},{10,11... | collective-permute-start | bytes 55304 | tf_op jit(solution)/shard_map/ppermute | solution.py:27

commit v6 on v5

--- a/solution.py
+++ b/solution.py
@@ -183,35 +183,61 @@
     )(*pieces)
 
 
-def _hidden_kernel(near, two, p1, m1, p2, m2, direct, start, g0, g1, u0, u1, out, acc):
+def _around_kernel(near, two, p1, m1, p2, m2, start, g0, g1, u0, u1, out):
+    _, _, _, l, c = _place()
+    width = near.shape[-1]
+    ahead = (jnp.where(c == 0, 3, 1), 2)
+    for k in range(4):
+        block = 2 * lax.rem(l + ahead[k // 2], 4) + (c if k % 2 == 0 else 1 - c)
+        w = _weight_columns((g0, g1, u0, u1), block, width)
+        kept = (near, two)[k // 2][k % 2]
+        t = jnp.concatenate(
+            [
+                kept[:32],
+                p1[k, :32],
+                p2[k, :16],
+                m2[k, :16],
+                m1[k, :32],
+                kept[32:],
+                p2[k, 16:],
+                p1[k, 32:],
+                m1[k, 32:],
+                m2[k, 16:],
+            ],
+            axis=0,
+        )
+        part = lax.dot_general(w, t, NT, preferred_element_type=F32)
+        if k == 0:
+            out[...] = start[...] + part
+        else:
+            out[...] += part
+
+
+def _around(kept, around, start, weights):
+    units, width = weights[0].shape[0], kept[0].shape[-1]
+    rows = start.shape[1]
+    return pl.pallas_call(
+        _around_kernel,
+        in_specs=[VMEM] * 11,
+        out_specs=VMEM,
+        out_shape=jax.ShapeDtypeStruct(start.shape, F32),
+        compiler_params=pltpu.CompilerParams(vmem_limit_bytes=16 * MIB),
+        cost_estimate=pl.CostEstimate(
+            flops=2 * 16 * units * rows * width, bytes_accessed=32 * units * width, transcendentals=0
+        ),
+        name="gate_up_around",
+    )(*kept, *around, start, *weights)
+
+
+def _hidden_kernel(direct, start, g0, g1, u0, u1, out, acc):
     x, y, _, l, c = _place()
     first, second = _along(c, x, y)
-    width = near.shape[-1]
+    width = direct.shape[-1]
     units = g0.shape[0]
-    ahead = (jnp.where(c == 0, 3, 1), 2, jnp.where(c == 0, 1, 3))
-    for k in range(6):
-        block = 2 * lax.rem(l + ahead[k // 2], 4) + (c if k % 2 == 0 else 1 - c)
+    for k in range(2):
+        block = 2 * lax.rem(l + jnp.where(c == 0, 1, 3), 4) + (c if k == 0 else 1 - c)
         w = _weight_columns((g0, g1, u0, u1), block, width)
-        if k < 4:
-            kept = (near, two)[k // 2][k % 2]
-            t = jnp.concatenate(
-                [
-                    kept[:32],
-                    p1[k, :32],
-                    p2[k, :16],
-                    m2[k, :16],
-                    m1[k, :32],
-                    kept[32:],
-                    p2[k, 16:],
-                    p1[k, 32:],
-                    m1[k, 32:],
-                    m2[k, 16:],
-                ],
-                axis=0,
-            )
-        else:
-            t = _in_order(direct[k - 4])
-        part = lax.dot_general(w, t, NT, preferred_element_type=F32)
+        part = lax.dot_general(w, _in_order(direct[k]), NT, preferred_element_type=F32)
         if k == 0:
             acc[...] = start[...] + part
         else:
@@ -227,23 +253,22 @@
         out[:, i * half : (i + 1) * half] = part.astype(BF16)
 
 
-def _hidden(kept, around, direct, start, weights):
-    units, width = weights[0].shape[0], kept[0].shape[-1]
-    rows = start.shape[1]
+def _hidden(direct, start, weights):
+    units, (_, rows, width) = weights[0].shape[0], direct.shape
     return pl.pallas_call(
         _hidden_kernel,
-        in_specs=[VMEM] * 12,
+        in_specs=[VMEM] * 6,
         out_specs=VMEM,
         out_shape=jax.ShapeDtypeStruct((2 * units, rows), BF16),
         scratch_shapes=[pltpu.VMEM((4 * units, rows), F32)],
-        compiler_params=pltpu.CompilerParams(vmem_limit_bytes=24 * MIB),
+        compiler_params=pltpu.CompilerParams(vmem_limit_bytes=16 * MIB),
         cost_estimate=pl.CostEstimate(
-            flops=2 * 24 * units * rows * width,
-            bytes_accessed=48 * units * width,
+            flops=2 * 8 * units * rows * width,
+            bytes_accessed=16 * units * width,
             transcendentals=2 * units * rows,
         ),
         name="gate_up_silu",
-    )(*kept, *around, direct, start, *weights)
+    )(direct, start, *weights)
 
 
 def _down_kernel(h0, h1, h2, h3, d0, d1, own, s1, s2, s3, ht):
@@ -355,15 +380,18 @@
     quarter, whole = _join(_mine(tokens), swapped)
     near = _permute(quarter, _up_or_down(1))
     two = _permute(quarter, _z_two)
-    gate_in, up_in, _ = lax.optimization_barrier((gate_weight, up_weight, quarter))
+    gate_in, up_in, down_in, _ = lax.optimization_barrier((gate_weight, up_weight, down_weight, quarter))
     gate_other = _permute(gate_in, _swap)
     up_other = _permute(up_in, _swap)
+    down_other = _permute(down_in, _swap)
     weights = (gate_weight, gate_other, up_weight, up_other)
     later, near, two = lax.optimization_barrier((whole, near, two))
     direct = _permute(later, _up_or_down(-1))
 
     packed = _pack((near, two))
-    packed, gate_other, up_other = lax.optimization_barrier((packed, gate_other, up_other))
+    packed, gate_other, up_other, down_other = lax.optimization_barrier(
+        (packed, gate_other, up_other, down_other)
+    )
     first_back, first_on, second_back, second_on = packed
     around = [
         _permute(first_back, _first(-1)),
@@ -374,9 +402,8 @@
     whole, _ = lax.optimization_barrier((whole, packed))
     start = _own(whole, weights)
 
-    hidden = _hidden((near, two), around, direct, start, weights)
-    down_in, _ = lax.optimization_barrier((down_weight, hidden))
-    down_other = _permute(down_in, _swap)
+    start = _around((near, two), around, start, weights)
+    hidden = _hidden(direct, start, weights)
     two, one, three = (_permute(hidden, _lo(-k)) for k in (2, 1, 3))
 
     own, *sends = _down((hidden, one, two, three), down_weight, down_other)

time: 89.9 us -> 88.4 us (0.983)
  starting transfers between devices: 34.9 us -> 33.8 us
    ppermute x22, starting transfers between devices: 34.9 us -> 33.8 us  [_permute(): return lax.ppermute(a, AXES, _perm(move))]
    pallas_call x1 -> x2, Pallas kernels: 2.56 us -> 2.75 us  [the longest x1 1.72 us: _around(): pl.pallas_call(_around_kernel, in_specs=[VMEM] * 11, out_specs=VMEM, out_...]
  transfers between devices with their start and end apart: 22 -> 22, of which waited for: 14 -> 17; matrix products, arithmetic and copies ran while one was open for 0% -> 0% of each run, Pallas kernels for 1% -> 3%
where the time goes in v6:
time: 88.4 us; the launch traced here: 88.3 us
  waiting for transfers between devices  44.6 us (50%)
  starting transfers between devices  33.8 us (38%)
  Pallas kernels  6.09 us (7%)
  local copies, waits for them, and re-layouts  3.03 us (3%)
    ppermute x22, waiting for transfers between devices, _permute(): return lax.ppermute(a, AXES, _perm(move))  44.6 us
    ppermute x22, starting transfers between devices, _permute(): return lax.ppermute(a, AXES, _perm(move))  33.8 us
    unnamed x10, local copies, waits for them, and re-layouts  3.03 us
    pallas_call x1, Pallas kernels, _down(): pl.pallas_call(_down_kernel, in_specs=[VMEM] * 6, out_specs=[VMEM] * 4, o...  1.91 us
  transfers between devices with their start and end apart: 22, of which 17 were waited for; matrix products, arithmetic and copies ran while one was open for 0% of the time, Pallas kernels for 3%

profile of v6, /device:TPU:1, one launch (start us, length us, event | category | flops | bytes accessed | tf_op | source)
XLA Modules:
  0.0 88.3 jit_solution(16685687432352922426)
XLA Ops:
  0.0 0.0 copy-start
  0.0 3.2 %collective-permute-start = (bf16[2,256,1152]{2,1,0:T(8,128)(2,1)}, bf16[2,256,1152]{2,1,0:T(8,128)(2,1)S(1)}, u32[]{:S(2)}, u32[]{:S(2)}) collective-permute-start(bf16[2,256,1152]{2,1,0:T(8,128)(2,1)} %tokens.1), channel_id=1, source_target_pairs={{0,1},{1,0},{2,3},{3,2},{4,5},{5,4},{6,7},{7,6},{8,9},{9,8},{10,11... | collective-permute-start | bytes 3538952 | tf_op jit(solution)/shard_map/ppermute | solution.py:27
  3.2 0.0 copy-start.4
  3.2 1.3 %copy-done.4 = bf16[2,256,1152]{2,1,0:T(8,128)(2,1)S(1)} copy-done((bf16[2,256,1152]{2,1,0:T(8,128)(2,1)S(1)}, bf16[2,256,1152]{2,1,0:T(8,128)(2,1)}, u32[]{:S(2)}) %copy-start.4) | copy-done | bytes 1179672
  4.5 0.1 order_own.1.mine
  4.6 1.4 %collective-permute-done.swapped = bf16[2,256,1152]{2,1,0:T(8,128)(2,1)S(1)} collective-permute-done((bf16[2,256,1152]{2,1,0:T(8,128)(2,1)}, bf16[2,256,1152]{2,1,0:T(8,128)(2,1)S(1)}, u32[]{:S(2)}, u32[]{:S(2)}) %collective-permute-start) | collective-permute-done | bytes 1179680 | tf_op jit(solution)/shard_map/ppermute | solution.py:27
  5.9 0.1 order_other.1
  6.0 0.0 copy-done
  6.1 0.5 collective-permute-start.4
  6.5 0.1 collective-permute-start.5
  6.7 0.4 collective-permute-start.6
  7.0 3.8 %collective-permute-start.1 = (bf16[2,64,1152]{2,1,0:T(8,128)(2,1)S(1)}, bf16[2,64,1152]{2,1,0:T(8,128)(2,1)S(1)}, u32[]{:S(2)}, u32[]{:S(2)}) collective-permute-start(bf16[2,64,1152]{2,1,0:T(8,128)(2,1)S(1)} %get-tuple-element.36), channel_id=1, source_target_pairs={{0,2},{1,15},{2,4},{3,1},{4,6},{5,3},{6,8},{7,5},{8,10},{9,7},{10,... | collective-permute-start | bytes 884744 | tf_op jit(solution)/shard_map/ppermute | solution.py:27
  10.9 0.0 collective-permute-start.2
  10.9 10.0 %collective-permute-done.1.near = bf16[2,64,1152]{2,1,0:T(8,128)(2,1)S(1)} collective-permute-done((bf16[2,64,1152]{2,1,0:T(8,128)(2,1)S(1)}, bf16[2,64,1152]{2,1,0:T(8,128)(2,1)S(1)}, u32[]{:S(2)}, u32[]{:S(2)}) %collective-permute-start.1) | collective-permute-done | bytes 294944 | tf_op jit(solution)/shard_map/ppermute | solution.py:27
  20.9 1.2 %collective-permute-done.2.two = bf16[2,64,1152]{2,1,0:T(8,128)(2,1)S(1)} collective-permute-done((bf16[2,64,1152]{2,1,0:T(8,128)(2,1)S(1)}, bf16[2,64,1152]{2,1,0:T(8,128)(2,1)S(1)}, u32[]{:S(2)}, u32[]{:S(2)}) %collective-permute-start.2) | collective-permute-done | bytes 294944 | tf_op jit(solution)/shard_map/ppermute | solution.py:27
  22.1 0.0 collective-permute-start.3
  22.1 0.1 pack_quarters.1
  22.2 0.0 collective-permute-done.4.g1
  22.2 0.0 collective-permute-done.5.u1
  22.2 0.0 collective-permute-done.6.d1
  22.2 1.3 %collective-permute-start.10 = (bf16[4,48,1152]{2,1,0:T(8,128)(2,1)S(1)}, bf16[4,48,1152]{2,1,0:T(8,128)(2,1)S(1)}, u32[]{:S(2)}, u32[]{:S(2)}) collective-permute-start(bf16[4,48,1152]{2,1,0:T(8,128)(2,1)S(1)} %get-tuple-element.50), channel_id=1, source_target_pairs={{0,16},{1,65},{2,18},{3,67},{4,20},{5,69},{6,22},{7,71},{8,24},{9,... | collective-permute-start | bytes 1327112 | tf_op jit(solution)/shard_map/ppermute | solution.py:27
  23.5 2.7 %collective-permute-start.7 = (bf16[4,48,1152]{2,1,0:T(8,128)(2,1)S(1)}, bf16[4,48,1152]{2,1,0:T(8,128)(2,1)S(1)}, u32[]{:S(2)}, u32[]{:S(2)}) collective-permute-start(bf16[4,48,1152]{2,1,0:T(8,128)(2,1)S(1)} %get-tuple-element.47), channel_id=1, source_target_pairs={{0,192},{1,49},{2,194},{3,51},{4,196},{5,53},{6,198},{7,55},{8,200... | collective-permute-start | bytes 1327112 | tf_op jit(solution)/shard_map/ppermute | solution.py:27
  26.3 0.0 collective-permute-start.8
  26.3 1.5 %collective-permute-start.9 = (bf16[4,48,1152]{2,1,0:T(8,128)(2,1)S(1)}, bf16[4,48,1152]{2,1,0:T(8,128)(2,1)S(1)}, u32[]{:S(2)}, u32[]{:S(2)}) collective-permute-start(bf16[4,48,1152]{2,1,0:T(8,128)(2,1)S(1)} %get-tuple-element.49), channel_id=1, source_target_pairs={{0,48},{1,193},{2,50},{3,195},{4,52},{5,197},{6,54},{7,199},{8,56}... | collective-permute-start | bytes 1327112 | tf_op jit(solution)/shard_map/ppermute | solution.py:27
  27.7 0.0 copy-start.1
  27.7 1.7 %copy-done.1 = bf16[144,9216]{1,0:T(8,128)(2,1)S(1)} copy-done((bf16[144,9216]{1,0:T(8,128)(2,1)S(1)}, bf16[144,9216]{1,0:T(8,128)(2,1)}, u32[]{:S(2)}) %copy-start.1) | copy-done | bytes 2654232
  29.5 0.0 copy-start.2
  29.5 0.9 %own_features.1.start = f32[576,256]{1,0:T(8,128)S(1)} custom-call(bf16[2,256,1152]{2,1,0:T(8,128)(2,1)S(1)} %get-tuple-element.51.whole, bf16[144,9216]{1,0:T(8,128)(2,1)S(1)} %copy-done, bf16[144,9216]{1,0:T(8,128)(2,1)S(1)} %collective-permute-done.4.g1, bf16[144,9216]{1,0:T(8,128)(2,1)S(1)} %copy-done.1, bf16[144,9216]{1,0:T(8,128)(2,1)S(1)} %collective-permute-done.5.u1), custom_call_target="tpu_custom_call" | custom-call | flops 679477248 | bytes 3317760 | tf_op jit(solution)/shard_map/own_features/pallas_call | solution.py:150
  30.4 0.5 collective-permute-done.10.m2
  31.0 1.3 %collective-permute-done.7.p1 = bf16[4,48,1152]{2,1,0:T(8,128)(2,1)S(1)} collective-permute-done((bf16[4,48,1152]{2,1,0:T(8,128)(2,1)S(1)}, bf16[4,48,1152]{2,1,0:T(8,128)(2,1)S(1)}, u32[]{:S(2)}, u32[]{:S(2)}) %collective-permute-start.7) | collective-permute-done | bytes 442400 | tf_op jit(solution)/shard_map/ppermute | solution.py:27
  32.3 5.3 %collective-permute-done.8.m1 = bf16[4,48,1152]{2,1,0:T(8,128)(2,1)S(1)} collective-permute-done((bf16[4,48,1152]{2,1,0:T(8,128)(2,1)S(1)}, bf16[4,48,1152]{2,1,0:T(8,128)(2,1)S(1)}, u32[]{:S(2)}, u32[]{:S(2)}) %collective-permute-start.8) | collective-permute-done | bytes 442400 | tf_op jit(solution)/shard_map/ppermute | solution.py:27
  37.6 0.7 collective-permute-done.9.p2
  38.2 0.0 copy-done.2
  38.2 1.7 %gate_up_around.1.start = f32[576,256]{1,0:T(8,128)S(1)} custom-call(bf16[2,64,1152]{2,1,0:T(8,128)(2,1)S(1)} %collective-permute-done.1.near, bf16[2,64,1152]{2,1,0:T(8,128)(2,1)S(1)} %collective-permute-done.2.two, bf16[4,48,1152]{2,1,0:T(8,128)(2,1)S(1)} %collective-permute-done.7.p1, bf16[4,48,1152]{2,1,0:T(8,128)(2,1)S(1)} %collective-permute-done.8.m1, ...), custom_call_target="tpu_custom_call" | custom-call | flops 1358954496 | bytes 5308416 | tf_op jit(solution)/shard_map/gate_up_around/pallas_call | solution.py:219
  40.0 0.0 copy-start.3
  40.0 0.0 collective-permute-done.3.direct
  40.0 1.0 %gate_up_silu.1.h0 = bf16[288,256]{1,0:T(8,128)(2,1)S(1)} custom-call(bf16[2,256,1152]{2,1,0:T(8,128)(2,1)S(1)} %collective-permute-done.3.direct, f32[576,256]{1,0:T(8,128)S(1)} %gate_up_around.1.start, bf16[144,9216]{1,0:T(8,128)(2,1)S(1)} %copy-done, bf16[144,9216]{1,0:T(8,128)(2,1)S(1)} %collective-permute-done.4.g1, bf16[144,9216]{1,0:T(8,128)(2,1)S(1)} %copy-done.2, ...), custom_call_target="tpu_custom_call" | custom-call | flops 679477248 | bytes 2654208 | tf_op jit(solution)/shard_map/gate_up_silu/pallas_call | solution.py:258
  41.0 1.4 %collective-permute-start.11 = (bf16[288,256]{1,0:T(8,128)(2,1)S(1)}, bf16[288,256]{1,0:T(8,128)(2,1)S(1)}, u32[]{:S(2)}, u32[]{:S(2)}) collective-permute-start(bf16[288,256]{1,0:T(8,128)(2,1)S(1)} %gate_up_silu.1.h0), channel_id=1, source_target_pairs={{0,6},{1,7},{2,0},{3,1},{4,2},{5,3},{6,4},{7,5},{8,14},{9,15},{10,... | collective-permute-start | bytes 442376 | tf_op jit(solution)/shard_map/ppermute | solution.py:27
  42.4 0.0 collective-permute-start.12
  42.4 0.4 collective-permute-start.13
  42.8 3.8 %collective-permute-done.11.h1 = bf16[288,256]{1,0:T(8,128)(2,1)S(1)} collective-permute-done((bf16[288,256]{1,0:T(8,128)(2,1)S(1)}, bf16[288,256]{1,0:T(8,128)(2,1)S(1)}, u32[]{:S(2)}, u32[]{:S(2)}) %collective-permute-start.11) | collective-permute-done | bytes 147488 | tf_op jit(solution)/shard_map/ppermute | solution.py:27
  46.5 8.8 %collective-permute-done.12.h2 = bf16[288,256]{1,0:T(8,128)(2,1)S(1)} collective-permute-done((bf16[288,256]{1,0:T(8,128)(2,1)S(1)}, bf16[288,256]{1,0:T(8,128)(2,1)S(1)}, u32[]{:S(2)}, u32[]{:S(2)}) %collective-permute-start.12) | collective-permute-done | bytes 147488 | tf_op jit(solution)/shard_map/ppermute | solution.py:27
  55.4 0.0 collective-permute-done.13.h3
  55.4 0.0 copy-done.3
  55.4 1.9 %down.1 = (f32[2,64,1152]{2,1,0:T(8,128)S(1)}, bf16[2,64,1152]{2,1,0:T(8,128)(2,1)S(1)}, bf16[2,64,1152]{2,1,0:T(8,128)(2,1)S(1)}, bf16[2,64,1152]{2,1,0:T(8,128)(2,1)S(1)}) custom-call(bf16[288,256]{1,0:T(8,128)(2,1)S(1)} %gate_up_silu.1.h0, bf16[288,256]{1,0:T(8,128)(2,1)S(1)} %collective-permute-done.11.h1, ...), custom_call_target="tpu_custom_call" | custom-call | flops 1358954496 | bytes 5308416 | tf_op jit(solution)/shard_map/down/pallas_call | solution.py:298
  57.3 2.1 %collective-permute-start.14 = (bf16[2,64,1152]{2,1,0:T(8,128)(2,1)S(1)}, bf16[2,64,1152]{2,1,0:T(8,128)(2,1)S(1)}, u32[]{:S(2)}, u32[]{:S(2)}) collective-permute-start(bf16[2,64,1152]{2,1,0:T(8,128)(2,1)S(1)} %get-tuple-element.54), channel_id=1, source_target_pairs={{0,128},{1,33},{2,130},{3,35},{4,132},{5,37},{6,134},{7,39},{8,136... | collective-permute-start | bytes 884744 | tf_op jit(solution)/shard_map/ppermute | solution.py:27
  59.4 1.1 %collective-permute-start.15 = (bf16[2,64,1152]{2,1,0:T(8,128)(2,1)S(1)}, bf16[2,64,1152]{2,1,0:T(8,128)(2,1)S(1)}, u32[]{:S(2)}, u32[]{:S(2)}) collective-permute-start(bf16[2,64,1152]{2,1,0:T(8,128)(2,1)S(1)} %get-tuple-element.55), channel_id=1, source_target_pairs={{0,64},{1,17},{2,66},{3,19},{4,68},{5,21},{6,70},{7,23},{8,72},{9,... | collective-permute-start | bytes 884744 | tf_op jit(solution)/shard_map/ppermute | solution.py:27
  60.4 1.6 %collective-permute-start.16 = (bf16[2,64,1152]{2,1,0:T(8,128)(2,1)S(1)}, bf16[2,64,1152]{2,1,0:T(8,128)(2,1)S(1)}, u32[]{:S(2)}, u32[]{:S(2)}) collective-permute-start(bf16[2,64,1152]{2,1,0:T(8,128)(2,1)S(1)} %get-tuple-element.56), channel_id=1, source_target_pairs={{0,192},{1,49},{2,194},{3,51},{4,196},{5,53},{6,198},{7,55},{8,200... | collective-permute-start | bytes 884744 | tf_op jit(solution)/shard_map/ppermute | solution.py:27
  62.0 2.7 %collective-permute-done.14.g1 = bf16[2,64,1152]{2,1,0:T(8,128)(2,1)S(1)} collective-permute-done((bf16[2,64,1152]{2,1,0:T(8,128)(2,1)S(1)}, bf16[2,64,1152]{2,1,0:T(8,128)(2,1)S(1)}, u32[]{:S(2)}, u32[]{:S(2)}) %collective-permute-start.14) | collective-permute-done | bytes 294944 | tf_op jit(solution)/shard_map/ppermute | solution.py:27
  64.8 3.2 %collective-permute-done.15.g2 = bf16[2,64,1152]{2,1,0:T(8,128)(2,1)S(1)} collective-permute-done((bf16[2,64,1152]{2,1,0:T(8,128)(2,1)S(1)}, bf16[2,64,1152]{2,1,0:T(8,128)(2,1)S(1)}, u32[]{:S(2)}, u32[]{:S(2)}) %collective-permute-start.15) | collective-permute-done | bytes 294944 | tf_op jit(solution)/shard_map/ppermute | solution.py:27
  67.9 0.1 collective-permute-done.16.g3
  68.0 0.1 sum_first.1
  68.1 2.0 %collective-permute-start.17 = (bf16[2,16,1152]{2,1,0:T(8,128)(2,1)S(1)}, bf16[2,16,1152]{2,1,0:T(8,128)(2,1)S(1)}, u32[]{:S(2)}, u32[]{:S(2)}) collective-permute-start(bf16[2,16,1152]{2,1,0:T(8,128)(2,1)S(1)} %get-tuple-element.58), channel_id=1, source_target_pairs={{0,32},{1,129},{2,34},{3,131},{4,36},{5,133},{6,38},{7,135},{8,40}... | collective-permute-start | bytes 221192 | tf_op jit(solution)/shard_map/ppermute | solution.py:27
  70.2 1.5 %collective-permute-start.18 = (bf16[2,16,1152]{2,1,0:T(8,128)(2,1)S(1)}, bf16[2,16,1152]{2,1,0:T(8,128)(2,1)S(1)}, u32[]{:S(2)}, u32[]{:S(2)}) collective-permute-start(bf16[2,16,1152]{2,1,0:T(8,128)(2,1)S(1)} %get-tuple-element.59), channel_id=1, source_target_pairs={{0,16},{1,65},{2,18},{3,67},{4,20},{5,69},{6,22},{7,71},{8,24},{9,... | collective-permute-start | bytes 221192 | tf_op jit(solution)/shard_map/ppermute | solution.py:27
  71.6 1.2 %collective-permute-start.19 = (bf16[2,16,1152]{2,1,0:T(8,128)(2,1)S(1)}, bf16[2,16,1152]{2,1,0:T(8,128)(2,1)S(1)}, u32[]{:S(2)}, u32[]{:S(2)}) collective-permute-start(bf16[2,16,1152]{2,1,0:T(8,128)(2,1)S(1)} %get-tuple-element.60), channel_id=1, source_target_pairs={{0,48},{1,193},{2,50},{3,195},{4,52},{5,197},{6,54},{7,199},{8,56}... | collective-permute-start | bytes 221192 | tf_op jit(solution)/shard_map/ppermute | solution.py:27
  72.8 0.1 collective-permute-done.17.g1
  72.9 1.6 %collective-permute-done.18.g2 = bf16[2,16,1152]{2,1,0:T(8,128)(2,1)S(1)} collective-permute-done((bf16[2,16,1152]{2,1,0:T(8,128)(2,1)S(1)}, bf16[2,16,1152]{2,1,0:T(8,128)(2,1)S(1)}, u32[]{:S(2)}, u32[]{:S(2)}) %collective-permute-start.18) | collective-permute-done | bytes 73760 | tf_op jit(solution)/shard_map/ppermute | solution.py:27
  74.6 0.5 collective-permute-done.19.g3
  75.2 4.3 %collective-permute-start.20 = (bf16[16,1152]{1,0:T(8,128)(2,1)S(1)}, bf16[16,1152]{1,0:T(8,128)(2,1)S(1)}, u32[]{:S(2)}, u32[]{:S(2)}) collective-permute-start(bf16[16,1152]{1,0:T(8,128)(2,1)S(1)} %get-tuple-element.62), channel_id=1, source_target_pairs={{0,8},{1,9},{2,10},{3,11},{4,12},{5,13},{6,14},{7,15},{8,0},{9,1},... | collective-permute-start | bytes 110600 | tf_op jit(solution)/shard_map/ppermute | solution.py:27
  79.5 2.5 %collective-permute-done.20.got = bf16[16,1152]{1,0:T(8,128)(2,1)S(1)} collective-permute-done((bf16[16,1152]{1,0:T(8,128)(2,1)S(1)}, bf16[16,1152]{1,0:T(8,128)(2,1)S(1)}, u32[]{:S(2)}, u32[]{:S(2)}) %collective-permute-start.20) | collective-permute-done | bytes 36896 | tf_op jit(solution)/shard_map/ppermute | solution.py:27
  82.0 4.7 %collective-permute-start.21 = (bf16[8,1152]{1,0:T(8,128)(2,1)S(1)}, bf16[8,1152]{1,0:T(8,128)(2,1)S(1)}, u32[]{:S(2)}, u32[]{:S(2)}) collective-permute-start(bf16[8,1152]{1,0:T(8,128)(2,1)S(1)} %convert), channel_id=1, source_target_pairs={{0,1},{1,0},{2,3},{3,2},{4,5},{5,4},{6,7},{7,6},{8,9},{9,8},{10,11... | collective-permute-start | bytes 55304 | tf_op jit(solution)/shard_map/ppermute | solution.py:27
  86.7 0.8 collective-permute-done.21
  87.6 0.7 select_convert_fusion
  (4 shorter events, 0.1 us)
Async XLA Ops:
  0.0 6.0 %copy-start = (bf16[144,9216]{1,0:T(8,128)(2,1)S(1)}, bf16[144,9216]{1,0:T(8,128)(2,1)}, u32[]{:S(2)}) copy-start(bf16[144,9216]{1,0:T(8,128)(2,1)} %g0.5) | copy-start | bytes 7962628
  0.0 5.9 %collective-permute-start = (bf16[2,256,1152]{2,1,0:T(8,128)(2,1)}, bf16[2,256,1152]{2,1,0:T(8,128)(2,1)S(1)}, u32[]{:S(2)}, u32[]{:S(2)}) collective-permute-start(bf16[2,256,1152]{2,1,0:T(8,128)(2,1)} %tokens.1), channel_id=1, source_target_pairs={{0,1},{1,0},{2,3},{3,2},{4,5},{5,4},{6,7},{7,6},{8,9},{9,8},{10,11... | collective-permute-start | bytes 3538952 | tf_op jit(solution)/shard_map/ppermute | solution.py:27
  3.2 1.3 %copy-start.4 = (bf16[2,256,1152]{2,1,0:T(8,128)(2,1)S(1)}, bf16[2,256,1152]{2,1,0:T(8,128)(2,1)}, u32[]{:S(2)}) copy-start(bf16[2,256,1152]{2,1,0:T(8,128)(2,1)} %tokens.1) | copy-start | bytes 3538948
  6.1 16.2 %collective-permute-start.4 = (bf16[144,9216]{1,0:T(8,128)(2,1)S(1)}, bf16[144,9216]{1,0:T(8,128)(2,1)S(1)}, u32[]{:S(2)}, u32[]{:S(2)}) collective-permute-start(bf16[144,9216]{1,0:T(8,128)(2,1)S(1)} %copy-done), channel_id=1, source_target_pairs={{0,1},{1,0},{2,3},{3,2},{4,5},{5,4},{6,7},{7,6},{8,9},{9,8},{10,11... | collective-permute-start | bytes 7962632 | tf_op jit(solution)/shard_map/ppermute | solution.py:27
  6.5 15.7 %collective-permute-start.5 = (bf16[144,9216]{1,0:T(8,128)(2,1)}, bf16[144,9216]{1,0:T(8,128)(2,1)S(1)}, u32[]{:S(2)}, u32[]{:S(2)}) collective-permute-start(bf16[144,9216]{1,0:T(8,128)(2,1)} %u0.5), channel_id=1, source_target_pairs={{0,1},{1,0},{2,3},{3,2},{4,5},{5,4},{6,7},{7,6},{8,9},{9,8},{10,11... | collective-permute-start | bytes 7962632 | tf_op jit(solution)/shard_map/ppermute | solution.py:27
  6.7 15.6 %collective-permute-start.6 = (bf16[1152,1152]{1,0:T(8,128)(2,1)}, bf16[1152,1152]{1,0:T(8,128)(2,1)S(1)}, u32[]{:S(2)}, u32[]{:S(2)}) collective-permute-start(bf16[1152,1152]{1,0:T(8,128)(2,1)} %d0.1), channel_id=1, source_target_pairs={{0,1},{1,0},{2,3},{3,2},{4,5},{5,4},{6,7},{7,6},{8,9},{9,8},{10,11... | collective-permute-start | bytes 7962632 | tf_op jit(solution)/shard_map/ppermute | solution.py:27
  7.0 13.8 %collective-permute-start.1 = (bf16[2,64,1152]{2,1,0:T(8,128)(2,1)S(1)}, bf16[2,64,1152]{2,1,0:T(8,128)(2,1)S(1)}, u32[]{:S(2)}, u32[]{:S(2)}) collective-permute-start(bf16[2,64,1152]{2,1,0:T(8,128)(2,1)S(1)} %get-tuple-element.36), channel_id=1, source_target_pairs={{0,2},{1,15},{2,4},{3,1},{4,6},{5,3},{6,8},{7,5},{8,10},{9,7},{10,... | collective-permute-start | bytes 884744 | tf_op jit(solution)/shard_map/ppermute | solution.py:27
  10.9 11.2 %collective-permute-start.2 = (bf16[2,64,1152]{2,1,0:T(8,128)(2,1)S(1)}, bf16[2,64,1152]{2,1,0:T(8,128)(2,1)S(1)}, u32[]{:S(2)}, u32[]{:S(2)}) collective-permute-start(bf16[2,64,1152]{2,1,0:T(8,128)(2,1)S(1)} %get-tuple-element.36), channel_id=1, source_target_pairs={{0,4},{1,5},{2,14},{3,15},{4,8},{5,9},{6,2},{7,3},{8,12},{9,13},{1... | collective-permute-start | bytes 884744 | tf_op jit(solution)/shard_map/ppermute | solution.py:27
  22.1 17.9 %collective-permute-start.3 = (bf16[2,256,1152]{2,1,0:T(8,128)(2,1)S(1)}, bf16[2,256,1152]{2,1,0:T(8,128)(2,1)S(1)}, u32[]{:S(2)}, u32[]{:S(2)}) collective-permute-start(bf16[2,256,1152]{2,1,0:T(8,128)(2,1)S(1)} %get-tuple-element.51.whole), channel_id=1, source_target_pairs={{0,14},{1,3},{2,0},{3,5},{4,2},{5,7},{6,4},{7,9},{8,6},{9,11},{10,... | collective-permute-start | bytes 3538952 | tf_op jit(solution)/shard_map/ppermute | solution.py:27
  22.2 8.7 %collective-permute-start.10 = (bf16[4,48,1152]{2,1,0:T(8,128)(2,1)S(1)}, bf16[4,48,1152]{2,1,0:T(8,128)(2,1)S(1)}, u32[]{:S(2)}, u32[]{:S(2)}) collective-permute-start(bf16[4,48,1152]{2,1,0:T(8,128)(2,1)S(1)} %get-tuple-element.50), channel_id=1, source_target_pairs={{0,16},{1,65},{2,18},{3,67},{4,20},{5,69},{6,22},{7,71},{8,24},{9,... | collective-permute-start | bytes 1327112 | tf_op jit(solution)/shard_map/ppermute | solution.py:27
  23.5 8.7 %collective-permute-start.7 = (bf16[4,48,1152]{2,1,0:T(8,128)(2,1)S(1)}, bf16[4,48,1152]{2,1,0:T(8,128)(2,1)S(1)}, u32[]{:S(2)}, u32[]{:S(2)}) collective-permute-start(bf16[4,48,1152]{2,1,0:T(8,128)(2,1)S(1)} %get-tuple-element.47), channel_id=1, source_target_pairs={{0,192},{1,49},{2,194},{3,51},{4,196},{5,53},{6,198},{7,55},{8,200... | collective-permute-start | bytes 1327112 | tf_op jit(solution)/shard_map/ppermute | solution.py:27
  26.3 11.3 %collective-permute-start.8 = (bf16[4,48,1152]{2,1,0:T(8,128)(2,1)S(1)}, bf16[4,48,1152]{2,1,0:T(8,128)(2,1)S(1)}, u32[]{:S(2)}, u32[]{:S(2)}) collective-permute-start(bf16[4,48,1152]{2,1,0:T(8,128)(2,1)S(1)} %get-tuple-element.48), channel_id=1, source_target_pairs={{0,64},{1,17},{2,66},{3,19},{4,68},{5,21},{6,70},{7,23},{8,72},{9,... | collective-permute-start | bytes 1327112 | tf_op jit(solution)/shard_map/ppermute | solution.py:27
  26.3 12.0 %collective-permute-start.9 = (bf16[4,48,1152]{2,1,0:T(8,128)(2,1)S(1)}, bf16[4,48,1152]{2,1,0:T(8,128)(2,1)S(1)}, u32[]{:S(2)}, u32[]{:S(2)}) collective-permute-start(bf16[4,48,1152]{2,1,0:T(8,128)(2,1)S(1)} %get-tuple-element.49), channel_id=1, source_target_pairs={{0,48},{1,193},{2,50},{3,195},{4,52},{5,197},{6,54},{7,199},{8,56}... | collective-permute-start | bytes 1327112 | tf_op jit(solution)/shard_map/ppermute | solution.py:27
  27.7 1.7 %copy-start.1 = (bf16[144,9216]{1,0:T(8,128)(2,1)S(1)}, bf16[144,9216]{1,0:T(8,128)(2,1)}, u32[]{:S(2)}) copy-start(bf16[144,9216]{1,0:T(8,128)(2,1)} %u0.5) | copy-start | bytes 7962628
  29.5 8.8 %copy-start.2 = (bf16[144,9216]{1,0:T(8,128)(2,1)S(1)}, bf16[144,9216]{1,0:T(8,128)(2,1)}, u32[]{:S(2)}) copy-start(bf16[144,9216]{1,0:T(8,128)(2,1)} %u0.5) | copy-start | bytes 7962628
  40.0 15.4 %copy-start.3 = (bf16[1152,1152]{1,0:T(8,128)(2,1)S(1)}, bf16[1152,1152]{1,0:T(8,128)(2,1)}, u32[]{:S(2)}) copy-start(bf16[1152,1152]{1,0:T(8,128)(2,1)} %d0.1) | copy-start | bytes 7962628
  41.0 5.5 %collective-permute-start.11 = (bf16[288,256]{1,0:T(8,128)(2,1)S(1)}, bf16[288,256]{1,0:T(8,128)(2,1)S(1)}, u32[]{:S(2)}, u32[]{:S(2)}) collective-permute-start(bf16[288,256]{1,0:T(8,128)(2,1)S(1)} %gate_up_silu.1.h0), channel_id=1, source_target_pairs={{0,6},{1,7},{2,0},{3,1},{4,2},{5,3},{6,4},{7,5},{8,14},{9,15},{10,... | collective-permute-start | bytes 442376 | tf_op jit(solution)/shard_map/ppermute | solution.py:27
  42.4 13.0 %collective-permute-start.12 = (bf16[288,256]{1,0:T(8,128)(2,1)S(1)}, bf16[288,256]{1,0:T(8,128)(2,1)S(1)}, u32[]{:S(2)}, u32[]{:S(2)}) collective-permute-start(bf16[288,256]{1,0:T(8,128)(2,1)S(1)} %gate_up_silu.1.h0), channel_id=1, source_target_pairs={{0,4},{1,5},{2,6},{3,7},{4,0},{5,1},{6,2},{7,3},{8,12},{9,13},{10,... | collective-permute-start | bytes 442376 | tf_op jit(solution)/shard_map/ppermute | solution.py:27
  42.4 13.0 %collective-permute-start.13 = (bf16[288,256]{1,0:T(8,128)(2,1)S(1)}, bf16[288,256]{1,0:T(8,128)(2,1)S(1)}, u32[]{:S(2)}, u32[]{:S(2)}) collective-permute-start(bf16[288,256]{1,0:T(8,128)(2,1)S(1)} %gate_up_silu.1.h0), channel_id=1, source_target_pairs={{0,2},{1,3},{2,4},{3,5},{4,6},{5,7},{6,0},{7,1},{8,10},{9,11},{10,... | collective-permute-start | bytes 442376 | tf_op jit(solution)/shard_map/ppermute | solution.py:27
  57.3 7.5 %collective-permute-start.14 = (bf16[2,64,1152]{2,1,0:T(8,128)(2,1)S(1)}, bf16[2,64,1152]{2,1,0:T(8,128)(2,1)S(1)}, u32[]{:S(2)}, u32[]{:S(2)}) collective-permute-start(bf16[2,64,1152]{2,1,0:T(8,128)(2,1)S(1)} %get-tuple-element.54), channel_id=1, source_target_pairs={{0,128},{1,33},{2,130},{3,35},{4,132},{5,37},{6,134},{7,39},{8,136... | collective-permute-start | bytes 884744 | tf_op jit(solution)/shard_map/ppermute | solution.py:27
  59.4 8.6 %collective-permute-start.15 = (bf16[2,64,1152]{2,1,0:T(8,128)(2,1)S(1)}, bf16[2,64,1152]{2,1,0:T(8,128)(2,1)S(1)}, u32[]{:S(2)}, u32[]{:S(2)}) collective-permute-start(bf16[2,64,1152]{2,1,0:T(8,128)(2,1)S(1)} %get-tuple-element.55), channel_id=1, source_target_pairs={{0,64},{1,17},{2,66},{3,19},{4,68},{5,21},{6,70},{7,23},{8,72},{9,... | collective-permute-start | bytes 884744 | tf_op jit(solution)/shard_map/ppermute | solution.py:27
  60.4 7.6 %collective-permute-start.16 = (bf16[2,64,1152]{2,1,0:T(8,128)(2,1)S(1)}, bf16[2,64,1152]{2,1,0:T(8,128)(2,1)S(1)}, u32[]{:S(2)}, u32[]{:S(2)}) collective-permute-start(bf16[2,64,1152]{2,1,0:T(8,128)(2,1)S(1)} %get-tuple-element.56), channel_id=1, source_target_pairs={{0,192},{1,49},{2,194},{3,51},{4,196},{5,53},{6,198},{7,55},{8,200... | collective-permute-start | bytes 884744 | tf_op jit(solution)/shard_map/ppermute | solution.py:27
  68.1 4.8 %collective-permute-start.17 = (bf16[2,16,1152]{2,1,0:T(8,128)(2,1)S(1)}, bf16[2,16,1152]{2,1,0:T(8,128)(2,1)S(1)}, u32[]{:S(2)}, u32[]{:S(2)}) collective-permute-start(bf16[2,16,1152]{2,1,0:T(8,128)(2,1)S(1)} %get-tuple-element.58), channel_id=1, source_target_pairs={{0,32},{1,129},{2,34},{3,131},{4,36},{5,133},{6,38},{7,135},{8,40}... | collective-permute-start | bytes 221192 | tf_op jit(solution)/shard_map/ppermute | solution.py:27
  70.2 4.4 %collective-permute-start.18 = (bf16[2,16,1152]{2,1,0:T(8,128)(2,1)S(1)}, bf16[2,16,1152]{2,1,0:T(8,128)(2,1)S(1)}, u32[]{:S(2)}, u32[]{:S(2)}) collective-permute-start(bf16[2,16,1152]{2,1,0:T(8,128)(2,1)S(1)} %get-tuple-element.59), channel_id=1, source_target_pairs={{0,16},{1,65},{2,18},{3,67},{4,20},{5,69},{6,22},{7,71},{8,24},{9,... | collective-permute-start | bytes 221192 | tf_op jit(solution)/shard_map/ppermute | solution.py:27
  71.6 3.5 %collective-permute-start.19 = (bf16[2,16,1152]{2,1,0:T(8,128)(2,1)S(1)}, bf16[2,16,1152]{2,1,0:T(8,128)(2,1)S(1)}, u32[]{:S(2)}, u32[]{:S(2)}) collective-permute-start(bf16[2,16,1152]{2,1,0:T(8,128)(2,1)S(1)} %get-tuple-element.60), channel_id=1, source_target_pairs={{0,48},{1,193},{2,50},{3,195},{4,52},{5,197},{6,54},{7,199},{8,56}... | collective-permute-start | bytes 221192 | tf_op jit(solution)/shard_map/ppermute | solution.py:27
  75.2 6.8 %collective-permute-start.20 = (bf16[16,1152]{1,0:T(8,128)(2,1)S(1)}, bf16[16,1152]{1,0:T(8,128)(2,1)S(1)}, u32[]{:S(2)}, u32[]{:S(2)}) collective-permute-start(bf16[16,1152]{1,0:T(8,128)(2,1)S(1)} %get-tuple-element.62), channel_id=1, source_target_pairs={{0,8},{1,9},{2,10},{3,11},{4,12},{5,13},{6,14},{7,15},{8,0},{9,1},... | collective-permute-start | bytes 110600 | tf_op jit(solution)/shard_map/ppermute | solution.py:27
  82.0 5.6 %collective-permute-start.21 = (bf16[8,1152]{1,0:T(8,128)(2,1)S(1)}, bf16[8,1152]{1,0:T(8,128)(2,1)S(1)}, u32[]{:S(2)}, u32[]{:S(2)}) collective-permute-start(bf16[8,1152]{1,0:T(8,128)(2,1)S(1)} %convert), channel_id=1, source_target_pairs={{0,1},{1,0},{2,3},{3,2},{4,5},{5,4},{6,7},{7,6},{8,9},{9,8},{10,11... | collective-permute-start | bytes 55304 | tf_op jit(solution)/shard_map/ppermute | solution.py:27

commit v7 on v6

--- a/solution.py
+++ b/solution.py
@@ -271,19 +271,30 @@
     )(direct, start, *weights)
 
 
-def _down_kernel(h0, h1, h2, h3, d0, d1, own, s1, s2, s3, ht):
+def _down_part(hidden, ahead, d, ht):
     _, _, _, l, c = _place()
-    units = h0.shape[0] // 2
-    for k, part in enumerate((h0, h1, h2, h3)):
-        base = lax.rem(l + k, 4) * (2 * units)
+    units = hidden[0].shape[0] // 2
+    for n, part in enumerate(hidden):
         for i, core in enumerate((c, 1 - c)):
-            row = pl.multiple_of(base + core * units, 16)
+            row = pl.multiple_of(n * 2 * units + core * units, 16)
             ht[pl.ds(row, units), :] = part[pl.ds(i * units, units), :]
-    hidden = ht[...].T
-    half = hidden.shape[0] // 2
-    group = half // 4
-    for i, d in enumerate((d0, d1)):
-        result = jnp.dot(hidden, d[...], preferred_element_type=F32)
+    left = ht[...].T
+    starts = [pl.multiple_of(lax.rem(l + k, 4) * 2 * units, 16) for k in ahead]
+    for i, w in enumerate(d):
+        right = jnp.concatenate([w[pl.ds(row, 2 * units), :] for row in starts], axis=0)
+        yield i, jnp.dot(left, right, preferred_element_type=F32)
+
+
+def _down_near_kernel(h0, h1, d0, d1, out, ht):
+    for i, result in _down_part((h0, h1), (0, 1), (d0, d1), ht):
+        out[i] = result
+
+
+def _down_far_kernel(h2, h3, near, d0, d1, own, s1, s2, s3, ht):
+    for i, result in _down_part((h2, h3), (2, 3), (d0, d1), ht):
+        result = near[i] + result
+        half = result.shape[0] // 2
+        group = half // 4
         for k, out in enumerate((own, s1, s2, s3)):
             for j in range(2):
                 rows = result[j * half + k * group : j * half + (k + 1) * group]
@@ -291,22 +302,33 @@
 
 
 def _down(hs, d0, d1):
-    rows = hs[0].shape[1]
+    units, rows = hs[0].shape
     depth, width = d0.shape
     block = rows // 4
     send = jax.ShapeDtypeStruct((2, block, width), BF16)
-    return pl.pallas_call(
-        _down_kernel,
-        in_specs=[VMEM] * 6,
+    common = dict(
+        scratch_shapes=[pltpu.VMEM((2 * units, rows), BF16)],
+        compiler_params=pltpu.CompilerParams(vmem_limit_bytes=16 * MIB),
+        cost_estimate=pl.CostEstimate(
+            flops=2 * rows * depth * width, bytes_accessed=2 * depth * width, transcendentals=0
+        ),
+    )
+    near = pl.pallas_call(
+        _down_near_kernel,
+        in_specs=[VMEM] * 4,
+        out_specs=VMEM,
+        out_shape=jax.ShapeDtypeStruct((2, rows, width), F32),
+        name="down_near",
+        **common,
+    )(hs[0], hs[1], d0, d1)
+    return pl.pallas_call(
+        _down_far_kernel,
+        in_specs=[VMEM] * 5,
         out_specs=[VMEM] * 4,
         out_shape=[jax.ShapeDtypeStruct((2, block, width), F32), send, send, send],
-        scratch_shapes=[pltpu.VMEM((depth, rows), BF16)],
-        compiler_params=pltpu.CompilerParams(vmem_limit_bytes=24 * MIB),
-        cost_estimate=pl.CostEstimate(
-            flops=4 * rows * depth * width, bytes_accessed=4 * depth * width, transcendentals=0
-        ),
-        name="down",
-    )(*hs, d0, d1)
+        name="down_far",
+        **common,
+    )(hs[2], hs[3], near, d0, d1)
 
 
 def _sum_first_kernel(own, g1, g2, g3, kept, s1, s2, s3):

time: 88.4 us -> 87.7 us (level)
  waiting for transfers between devices: 44.6 us -> 43.3 us
    ppermute x22, waiting for transfers between devices: 44.6 us -> 43.3 us  [_permute(): return lax.ppermute(a, AXES, _perm(move))]
    pallas_call x1 -> x2, Pallas kernels: 1.91 us -> 2.45 us  [the longest x1 1.23 us: _down(): pl.pallas_call(_down_far_kernel, in_specs=[VMEM] * 5, out_specs=[VMEM] *...]
  transfers between devices with their start and end apart: 22 -> 22, of which waited for: 17 -> 17; matrix products, arithmetic and copies ran while one was open for 0% -> 0% of each run, Pallas kernels for 3% -> 5%
where the time goes in v7:
time: 87.7 us; the launch traced here: 87.6 us
  waiting for transfers between devices  43.3 us (49%)
  starting transfers between devices  33.8 us (39%)
  Pallas kernels  6.62 us (8%)
  local copies, waits for them, and re-layouts  3.03 us (3%)
    ppermute x22, waiting for transfers between devices, _permute(): return lax.ppermute(a, AXES, _perm(move))  43.3 us
    ppermute x22, starting transfers between devices, _permute(): return lax.ppermute(a, AXES, _perm(move))  33.8 us
    unnamed x10, local copies, waits for them, and re-layouts  3.03 us
  transfers between devices with their start and end apart: 22, of which 17 were waited for; matrix products, arithmetic and copies ran while one was open for 0% of the time, Pallas kernels for 5%

profile of v7, /device:TPU:1, one launch (start us, length us, event | category | flops | bytes accessed | tf_op | source)
XLA Modules:
  0.0 87.6 jit_solution(18029882137913734577)
XLA Ops:
  0.0 0.0 copy-start
  0.0 3.2 %collective-permute-start = (bf16[2,256,1152]{2,1,0:T(8,128)(2,1)}, bf16[2,256,1152]{2,1,0:T(8,128)(2,1)S(1)}, u32[]{:S(2)}, u32[]{:S(2)}) collective-permute-start(bf16[2,256,1152]{2,1,0:T(8,128)(2,1)} %tokens.1), channel_id=1, source_target_pairs={{0,1},{1,0},{2,3},{3,2},{4,5},{5,4},{6,7},{7,6},{8,9},{9,8},{10,11... | collective-permute-start | bytes 3538952 | tf_op jit(solution)/shard_map/ppermute | solution.py:27
  3.2 0.0 copy-start.4
  3.2 1.3 %copy-done.4 = bf16[2,256,1152]{2,1,0:T(8,128)(2,1)S(1)} copy-done((bf16[2,256,1152]{2,1,0:T(8,128)(2,1)S(1)}, bf16[2,256,1152]{2,1,0:T(8,128)(2,1)}, u32[]{:S(2)}) %copy-start.4) | copy-done | bytes 1179672
  4.5 0.1 order_own.1.mine
  4.6 1.4 %collective-permute-done.swapped = bf16[2,256,1152]{2,1,0:T(8,128)(2,1)S(1)} collective-permute-done((bf16[2,256,1152]{2,1,0:T(8,128)(2,1)}, bf16[2,256,1152]{2,1,0:T(8,128)(2,1)S(1)}, u32[]{:S(2)}, u32[]{:S(2)}) %collective-permute-start) | collective-permute-done | bytes 1179680 | tf_op jit(solution)/shard_map/ppermute | solution.py:27
  5.9 0.1 order_other.1
  6.0 0.0 copy-done
  6.1 0.5 collective-permute-start.4
  6.5 0.1 collective-permute-start.5
  6.7 0.4 collective-permute-start.6
  7.0 3.8 %collective-permute-start.1 = (bf16[2,64,1152]{2,1,0:T(8,128)(2,1)S(1)}, bf16[2,64,1152]{2,1,0:T(8,128)(2,1)S(1)}, u32[]{:S(2)}, u32[]{:S(2)}) collective-permute-start(bf16[2,64,1152]{2,1,0:T(8,128)(2,1)S(1)} %get-tuple-element.36), channel_id=1, source_target_pairs={{0,2},{1,15},{2,4},{3,1},{4,6},{5,3},{6,8},{7,5},{8,10},{9,7},{10,... | collective-permute-start | bytes 884744 | tf_op jit(solution)/shard_map/ppermute | solution.py:27
  10.9 0.0 collective-permute-start.2
  10.9 10.0 %collective-permute-done.1.near = bf16[2,64,1152]{2,1,0:T(8,128)(2,1)S(1)} collective-permute-done((bf16[2,64,1152]{2,1,0:T(8,128)(2,1)S(1)}, bf16[2,64,1152]{2,1,0:T(8,128)(2,1)S(1)}, u32[]{:S(2)}, u32[]{:S(2)}) %collective-permute-start.1) | collective-permute-done | bytes 294944 | tf_op jit(solution)/shard_map/ppermute | solution.py:27
  20.9 1.2 %collective-permute-done.2.two = bf16[2,64,1152]{2,1,0:T(8,128)(2,1)S(1)} collective-permute-done((bf16[2,64,1152]{2,1,0:T(8,128)(2,1)S(1)}, bf16[2,64,1152]{2,1,0:T(8,128)(2,1)S(1)}, u32[]{:S(2)}, u32[]{:S(2)}) %collective-permute-start.2) | collective-permute-done | bytes 294944 | tf_op jit(solution)/shard_map/ppermute | solution.py:27
  22.1 0.0 collective-permute-start.3
  22.1 0.1 pack_quarters.1
  22.2 0.0 collective-permute-done.4.g1
  22.2 0.0 collective-permute-done.5.u1
  22.2 0.0 collective-permute-done.6.d1
  22.2 1.3 %collective-permute-start.10 = (bf16[4,48,1152]{2,1,0:T(8,128)(2,1)S(1)}, bf16[4,48,1152]{2,1,0:T(8,128)(2,1)S(1)}, u32[]{:S(2)}, u32[]{:S(2)}) collective-permute-start(bf16[4,48,1152]{2,1,0:T(8,128)(2,1)S(1)} %get-tuple-element.50), channel_id=1, source_target_pairs={{0,16},{1,65},{2,18},{3,67},{4,20},{5,69},{6,22},{7,71},{8,24},{9,... | collective-permute-start | bytes 1327112 | tf_op jit(solution)/shard_map/ppermute | solution.py:27
  23.5 2.7 %collective-permute-start.7 = (bf16[4,48,1152]{2,1,0:T(8,128)(2,1)S(1)}, bf16[4,48,1152]{2,1,0:T(8,128)(2,1)S(1)}, u32[]{:S(2)}, u32[]{:S(2)}) collective-permute-start(bf16[4,48,1152]{2,1,0:T(8,128)(2,1)S(1)} %get-tuple-element.47), channel_id=1, source_target_pairs={{0,192},{1,49},{2,194},{3,51},{4,196},{5,53},{6,198},{7,55},{8,200... | collective-permute-start | bytes 1327112 | tf_op jit(solution)/shard_map/ppermute | solution.py:27
  26.3 0.0 collective-permute-start.8
  26.3 1.5 %collective-permute-start.9 = (bf16[4,48,1152]{2,1,0:T(8,128)(2,1)S(1)}, bf16[4,48,1152]{2,1,0:T(8,128)(2,1)S(1)}, u32[]{:S(2)}, u32[]{:S(2)}) collective-permute-start(bf16[4,48,1152]{2,1,0:T(8,128)(2,1)S(1)} %get-tuple-element.49), channel_id=1, source_target_pairs={{0,48},{1,193},{2,50},{3,195},{4,52},{5,197},{6,54},{7,199},{8,56}... | collective-permute-start | bytes 1327112 | tf_op jit(solution)/shard_map/ppermute | solution.py:27
  27.7 0.0 copy-start.1
  27.7 1.7 %copy-done.1 = bf16[144,9216]{1,0:T(8,128)(2,1)S(1)} copy-done((bf16[144,9216]{1,0:T(8,128)(2,1)S(1)}, bf16[144,9216]{1,0:T(8,128)(2,1)}, u32[]{:S(2)}) %copy-start.1) | copy-done | bytes 2654232
  29.5 0.0 copy-start.2
  29.5 0.9 %own_features.1.start = f32[576,256]{1,0:T(8,128)S(1)} custom-call(bf16[2,256,1152]{2,1,0:T(8,128)(2,1)S(1)} %get-tuple-element.51.whole, bf16[144,9216]{1,0:T(8,128)(2,1)S(1)} %copy-done, bf16[144,9216]{1,0:T(8,128)(2,1)S(1)} %collective-permute-done.4.g1, bf16[144,9216]{1,0:T(8,128)(2,1)S(1)} %copy-done.1, bf16[144,9216]{1,0:T(8,128)(2,1)S(1)} %collective-permute-done.5.u1), custom_call_target="tpu_custom_call" | custom-call | flops 679477248 | bytes 3317760 | tf_op jit(solution)/shard_map/own_features/pallas_call | solution.py:150
  30.4 0.5 collective-permute-done.10.m2
  31.0 1.3 %collective-permute-done.7.p1 = bf16[4,48,1152]{2,1,0:T(8,128)(2,1)S(1)} collective-permute-done((bf16[4,48,1152]{2,1,0:T(8,128)(2,1)S(1)}, bf16[4,48,1152]{2,1,0:T(8,128)(2,1)S(1)}, u32[]{:S(2)}, u32[]{:S(2)}) %collective-permute-start.7) | collective-permute-done | bytes 442400 | tf_op jit(solution)/shard_map/ppermute | solution.py:27
  32.3 5.3 %collective-permute-done.8.m1 = bf16[4,48,1152]{2,1,0:T(8,128)(2,1)S(1)} collective-permute-done((bf16[4,48,1152]{2,1,0:T(8,128)(2,1)S(1)}, bf16[4,48,1152]{2,1,0:T(8,128)(2,1)S(1)}, u32[]{:S(2)}, u32[]{:S(2)}) %collective-permute-start.8) | collective-permute-done | bytes 442400 | tf_op jit(solution)/shard_map/ppermute | solution.py:27
  37.6 0.7 collective-permute-done.9.p2
  38.2 0.0 copy-done.2
  38.2 1.7 %gate_up_around.1.start = f32[576,256]{1,0:T(8,128)S(1)} custom-call(bf16[2,64,1152]{2,1,0:T(8,128)(2,1)S(1)} %collective-permute-done.1.near, bf16[2,64,1152]{2,1,0:T(8,128)(2,1)S(1)} %collective-permute-done.2.two, bf16[4,48,1152]{2,1,0:T(8,128)(2,1)S(1)} %collective-permute-done.7.p1, bf16[4,48,1152]{2,1,0:T(8,128)(2,1)S(1)} %collective-permute-done.8.m1, ...), custom_call_target="tpu_custom_call" | custom-call | flops 1358954496 | bytes 5308416 | tf_op jit(solution)/shard_map/gate_up_around/pallas_call | solution.py:219
  40.0 0.0 copy-start.3
  40.0 0.0 collective-permute-done.3.direct
  40.0 1.0 %gate_up_silu.1.h0 = bf16[288,256]{1,0:T(8,128)(2,1)S(1)} custom-call(bf16[2,256,1152]{2,1,0:T(8,128)(2,1)S(1)} %collective-permute-done.3.direct, f32[576,256]{1,0:T(8,128)S(1)} %gate_up_around.1.start, bf16[144,9216]{1,0:T(8,128)(2,1)S(1)} %copy-done, bf16[144,9216]{1,0:T(8,128)(2,1)S(1)} %collective-permute-done.4.g1, bf16[144,9216]{1,0:T(8,128)(2,1)S(1)} %copy-done.2, ...), custom_call_target="tpu_custom_call" | custom-call | flops 679477248 | bytes 2654208 | tf_op jit(solution)/shard_map/gate_up_silu/pallas_call | solution.py:258
  41.0 1.4 %collective-permute-start.13 = (bf16[288,256]{1,0:T(8,128)(2,1)S(1)}, bf16[288,256]{1,0:T(8,128)(2,1)S(1)}, u32[]{:S(2)}, u32[]{:S(2)}) collective-permute-start(bf16[288,256]{1,0:T(8,128)(2,1)S(1)} %gate_up_silu.1.h0), channel_id=1, source_target_pairs={{0,6},{1,7},{2,0},{3,1},{4,2},{5,3},{6,4},{7,5},{8,14},{9,15},{10,... | collective-permute-start | bytes 442376 | tf_op jit(solution)/shard_map/ppermute | solution.py:27
  42.4 0.0 collective-permute-start.11
  42.4 0.4 collective-permute-start.12
  42.8 3.8 %collective-permute-done.13.h1 = bf16[288,256]{1,0:T(8,128)(2,1)S(1)} collective-permute-done((bf16[288,256]{1,0:T(8,128)(2,1)S(1)}, bf16[288,256]{1,0:T(8,128)(2,1)S(1)}, u32[]{:S(2)}, u32[]{:S(2)}) %collective-permute-start.13) | collective-permute-done | bytes 147488 | tf_op jit(solution)/shard_map/ppermute | solution.py:27
  46.5 0.0 copy-done.3
  46.5 1.2 %down_near.1.near = f32[2,256,1152]{2,1,0:T(8,128)S(1)} custom-call(bf16[288,256]{1,0:T(8,128)(2,1)S(1)} %gate_up_silu.1.h0, bf16[288,256]{1,0:T(8,128)(2,1)S(1)} %collective-permute-done.13.h1, bf16[1152,1152]{1,0:T(8,128)(2,1)S(1)} %copy-done.3, bf16[1152,1152]{1,0:T(8,128)(2,1)S(1)} %collective-permute-done.6.d1), custom_call_target="tpu_custom_call" | custom-call | flops 679477248 | bytes 2654208 | tf_op jit(solution)/shard_map/down_near/pallas_call | solution.py:316
  47.8 7.6 %collective-permute-done.11.h2 = bf16[288,256]{1,0:T(8,128)(2,1)S(1)} collective-permute-done((bf16[288,256]{1,0:T(8,128)(2,1)S(1)}, bf16[288,256]{1,0:T(8,128)(2,1)S(1)}, u32[]{:S(2)}, u32[]{:S(2)}) %collective-permute-start.11) | collective-permute-done | bytes 147488 | tf_op jit(solution)/shard_map/ppermute | solution.py:27
  55.4 0.0 collective-permute-done.12.h3
  55.4 1.2 %down_far.1 = (f32[2,64,1152]{2,1,0:T(8,128)S(1)}, bf16[2,64,1152]{2,1,0:T(8,128)(2,1)S(1)}, bf16[2,64,1152]{2,1,0:T(8,128)(2,1)S(1)}, bf16[2,64,1152]{2,1,0:T(8,128)(2,1)S(1)}) custom-call(bf16[288,256]{1,0:T(8,128)(2,1)S(1)} %collective-permute-done.11.h2, bf16[288,256]{1,0:T(8,128)(2,1)S(1)} %collective-permute-done.12.h3, ...), custom_call_target="tpu_custom_call" | custom-call | flops 679477248 | bytes 2654208 | tf_op jit(solution)/shard_map/down_far/pallas_call | solution.py:324
  56.6 2.1 %collective-permute-start.14 = (bf16[2,64,1152]{2,1,0:T(8,128)(2,1)S(1)}, bf16[2,64,1152]{2,1,0:T(8,128)(2,1)S(1)}, u32[]{:S(2)}, u32[]{:S(2)}) collective-permute-start(bf16[2,64,1152]{2,1,0:T(8,128)(2,1)S(1)} %get-tuple-element.54), channel_id=1, source_target_pairs={{0,128},{1,33},{2,130},{3,35},{4,132},{5,37},{6,134},{7,39},{8,136... | collective-permute-start | bytes 884744 | tf_op jit(solution)/shard_map/ppermute | solution.py:27
  58.7 1.1 %collective-permute-start.15 = (bf16[2,64,1152]{2,1,0:T(8,128)(2,1)S(1)}, bf16[2,64,1152]{2,1,0:T(8,128)(2,1)S(1)}, u32[]{:S(2)}, u32[]{:S(2)}) collective-permute-start(bf16[2,64,1152]{2,1,0:T(8,128)(2,1)S(1)} %get-tuple-element.55), channel_id=1, source_target_pairs={{0,64},{1,17},{2,66},{3,19},{4,68},{5,21},{6,70},{7,23},{8,72},{9,... | collective-permute-start | bytes 884744 | tf_op jit(solution)/shard_map/ppermute | solution.py:27
  59.7 1.6 %collective-permute-start.16 = (bf16[2,64,1152]{2,1,0:T(8,128)(2,1)S(1)}, bf16[2,64,1152]{2,1,0:T(8,128)(2,1)S(1)}, u32[]{:S(2)}, u32[]{:S(2)}) collective-permute-start(bf16[2,64,1152]{2,1,0:T(8,128)(2,1)S(1)} %get-tuple-element.56), channel_id=1, source_target_pairs={{0,192},{1,49},{2,194},{3,51},{4,196},{5,53},{6,198},{7,55},{8,200... | collective-permute-start | bytes 884744 | tf_op jit(solution)/shard_map/ppermute | solution.py:27
  61.4 2.7 %collective-permute-done.14.g1 = bf16[2,64,1152]{2,1,0:T(8,128)(2,1)S(1)} collective-permute-done((bf16[2,64,1152]{2,1,0:T(8,128)(2,1)S(1)}, bf16[2,64,1152]{2,1,0:T(8,128)(2,1)S(1)}, u32[]{:S(2)}, u32[]{:S(2)}) %collective-permute-start.14) | collective-permute-done | bytes 294944 | tf_op jit(solution)/shard_map/ppermute | solution.py:27
  64.1 3.2 %collective-permute-done.15.g2 = bf16[2,64,1152]{2,1,0:T(8,128)(2,1)S(1)} collective-permute-done((bf16[2,64,1152]{2,1,0:T(8,128)(2,1)S(1)}, bf16[2,64,1152]{2,1,0:T(8,128)(2,1)S(1)}, u32[]{:S(2)}, u32[]{:S(2)}) %collective-permute-start.15) | collective-permute-done | bytes 294944 | tf_op jit(solution)/shard_map/ppermute | solution.py:27
  67.2 0.1 collective-permute-done.16.g3
  67.3 0.1 sum_first.1
  67.5 2.0 %collective-permute-start.17 = (bf16[2,16,1152]{2,1,0:T(8,128)(2,1)S(1)}, bf16[2,16,1152]{2,1,0:T(8,128)(2,1)S(1)}, u32[]{:S(2)}, u32[]{:S(2)}) collective-permute-start(bf16[2,16,1152]{2,1,0:T(8,128)(2,1)S(1)} %get-tuple-element.58), channel_id=1, source_target_pairs={{0,32},{1,129},{2,34},{3,131},{4,36},{5,133},{6,38},{7,135},{8,40}... | collective-permute-start | bytes 221192 | tf_op jit(solution)/shard_map/ppermute | solution.py:27
  69.5 1.5 %collective-permute-start.18 = (bf16[2,16,1152]{2,1,0:T(8,128)(2,1)S(1)}, bf16[2,16,1152]{2,1,0:T(8,128)(2,1)S(1)}, u32[]{:S(2)}, u32[]{:S(2)}) collective-permute-start(bf16[2,16,1152]{2,1,0:T(8,128)(2,1)S(1)} %get-tuple-element.59), channel_id=1, source_target_pairs={{0,16},{1,65},{2,18},{3,67},{4,20},{5,69},{6,22},{7,71},{8,24},{9,... | collective-permute-start | bytes 221192 | tf_op jit(solution)/shard_map/ppermute | solution.py:27
  70.9 1.2 %collective-permute-start.19 = (bf16[2,16,1152]{2,1,0:T(8,128)(2,1)S(1)}, bf16[2,16,1152]{2,1,0:T(8,128)(2,1)S(1)}, u32[]{:S(2)}, u32[]{:S(2)}) collective-permute-start(bf16[2,16,1152]{2,1,0:T(8,128)(2,1)S(1)} %get-tuple-element.60), channel_id=1, source_target_pairs={{0,48},{1,193},{2,50},{3,195},{4,52},{5,197},{6,54},{7,199},{8,56}... | collective-permute-start | bytes 221192 | tf_op jit(solution)/shard_map/ppermute | solution.py:27
  72.2 0.1 collective-permute-done.17.g1
  72.2 1.6 %collective-permute-done.18.g2 = bf16[2,16,1152]{2,1,0:T(8,128)(2,1)S(1)} collective-permute-done((bf16[2,16,1152]{2,1,0:T(8,128)(2,1)S(1)}, bf16[2,16,1152]{2,1,0:T(8,128)(2,1)S(1)}, u32[]{:S(2)}, u32[]{:S(2)}) %collective-permute-start.18) | collective-permute-done | bytes 73760 | tf_op jit(solution)/shard_map/ppermute | solution.py:27
  73.9 0.5 collective-permute-done.19.g3
  74.5 4.3 %collective-permute-start.20 = (bf16[16,1152]{1,0:T(8,128)(2,1)S(1)}, bf16[16,1152]{1,0:T(8,128)(2,1)S(1)}, u32[]{:S(2)}, u32[]{:S(2)}) collective-permute-start(bf16[16,1152]{1,0:T(8,128)(2,1)S(1)} %get-tuple-element.62), channel_id=1, source_target_pairs={{0,8},{1,9},{2,10},{3,11},{4,12},{5,13},{6,14},{7,15},{8,0},{9,1},... | collective-permute-start | bytes 110600 | tf_op jit(solution)/shard_map/ppermute | solution.py:27
  78.8 2.5 %collective-permute-done.20.got = bf16[16,1152]{1,0:T(8,128)(2,1)S(1)} collective-permute-done((bf16[16,1152]{1,0:T(8,128)(2,1)S(1)}, bf16[16,1152]{1,0:T(8,128)(2,1)S(1)}, u32[]{:S(2)}, u32[]{:S(2)}) %collective-permute-start.20) | collective-permute-done | bytes 36896 | tf_op jit(solution)/shard_map/ppermute | solution.py:27
  81.3 4.7 %collective-permute-start.21 = (bf16[8,1152]{1,0:T(8,128)(2,1)S(1)}, bf16[8,1152]{1,0:T(8,128)(2,1)S(1)}, u32[]{:S(2)}, u32[]{:S(2)}) collective-permute-start(bf16[8,1152]{1,0:T(8,128)(2,1)S(1)} %convert), channel_id=1, source_target_pairs={{0,1},{1,0},{2,3},{3,2},{4,5},{5,4},{6,7},{7,6},{8,9},{9,8},{10,11... | collective-permute-start | bytes 55304 | tf_op jit(solution)/shard_map/ppermute | solution.py:27
  86.1 0.8 collective-permute-done.21
  86.9 0.7 select_convert_fusion
  (4 shorter events, 0.1 us)
Async XLA Ops:
  0.0 6.0 %copy-start = (bf16[144,9216]{1,0:T(8,128)(2,1)S(1)}, bf16[144,9216]{1,0:T(8,128)(2,1)}, u32[]{:S(2)}) copy-start(bf16[144,9216]{1,0:T(8,128)(2,1)} %g0.5) | copy-start | bytes 7962628
  0.0 5.9 %collective-permute-start = (bf16[2,256,1152]{2,1,0:T(8,128)(2,1)}, bf16[2,256,1152]{2,1,0:T(8,128)(2,1)S(1)}, u32[]{:S(2)}, u32[]{:S(2)}) collective-permute-start(bf16[2,256,1152]{2,1,0:T(8,128)(2,1)} %tokens.1), channel_id=1, source_target_pairs={{0,1},{1,0},{2,3},{3,2},{4,5},{5,4},{6,7},{7,6},{8,9},{9,8},{10,11... | collective-permute-start | bytes 3538952 | tf_op jit(solution)/shard_map/ppermute | solution.py:27
  3.2 1.3 %copy-start.4 = (bf16[2,256,1152]{2,1,0:T(8,128)(2,1)S(1)}, bf16[2,256,1152]{2,1,0:T(8,128)(2,1)}, u32[]{:S(2)}) copy-start(bf16[2,256,1152]{2,1,0:T(8,128)(2,1)} %tokens.1) | copy-start | bytes 3538948
  6.1 16.2 %collective-permute-start.4 = (bf16[144,9216]{1,0:T(8,128)(2,1)S(1)}, bf16[144,9216]{1,0:T(8,128)(2,1)S(1)}, u32[]{:S(2)}, u32[]{:S(2)}) collective-permute-start(bf16[144,9216]{1,0:T(8,128)(2,1)S(1)} %copy-done), channel_id=1, source_target_pairs={{0,1},{1,0},{2,3},{3,2},{4,5},{5,4},{6,7},{7,6},{8,9},{9,8},{10,11... | collective-permute-start | bytes 7962632 | tf_op jit(solution)/shard_map/ppermute | solution.py:27
  6.5 15.7 %collective-permute-start.5 = (bf16[144,9216]{1,0:T(8,128)(2,1)}, bf16[144,9216]{1,0:T(8,128)(2,1)S(1)}, u32[]{:S(2)}, u32[]{:S(2)}) collective-permute-start(bf16[144,9216]{1,0:T(8,128)(2,1)} %u0.5), channel_id=1, source_target_pairs={{0,1},{1,0},{2,3},{3,2},{4,5},{5,4},{6,7},{7,6},{8,9},{9,8},{10,11... | collective-permute-start | bytes 7962632 | tf_op jit(solution)/shard_map/ppermute | solution.py:27
  6.7 15.6 %collective-permute-start.6 = (bf16[1152,1152]{1,0:T(8,128)(2,1)}, bf16[1152,1152]{1,0:T(8,128)(2,1)S(1)}, u32[]{:S(2)}, u32[]{:S(2)}) collective-permute-start(bf16[1152,1152]{1,0:T(8,128)(2,1)} %d0.3), channel_id=1, source_target_pairs={{0,1},{1,0},{2,3},{3,2},{4,5},{5,4},{6,7},{7,6},{8,9},{9,8},{10,11... | collective-permute-start | bytes 7962632 | tf_op jit(solution)/shard_map/ppermute | solution.py:27
  7.0 13.8 %collective-permute-start.1 = (bf16[2,64,1152]{2,1,0:T(8,128)(2,1)S(1)}, bf16[2,64,1152]{2,1,0:T(8,128)(2,1)S(1)}, u32[]{:S(2)}, u32[]{:S(2)}) collective-permute-start(bf16[2,64,1152]{2,1,0:T(8,128)(2,1)S(1)} %get-tuple-element.36), channel_id=1, source_target_pairs={{0,2},{1,15},{2,4},{3,1},{4,6},{5,3},{6,8},{7,5},{8,10},{9,7},{10,... | collective-permute-start | bytes 884744 | tf_op jit(solution)/shard_map/ppermute | solution.py:27
  10.9 11.2 %collective-permute-start.2 = (bf16[2,64,1152]{2,1,0:T(8,128)(2,1)S(1)}, bf16[2,64,1152]{2,1,0:T(8,128)(2,1)S(1)}, u32[]{:S(2)}, u32[]{:S(2)}) collective-permute-start(bf16[2,64,1152]{2,1,0:T(8,128)(2,1)S(1)} %get-tuple-element.36), channel_id=1, source_target_pairs={{0,4},{1,5},{2,14},{3,15},{4,8},{5,9},{6,2},{7,3},{8,12},{9,13},{1... | collective-permute-start | bytes 884744 | tf_op jit(solution)/shard_map/ppermute | solution.py:27
  22.1 17.9 %collective-permute-start.3 = (bf16[2,256,1152]{2,1,0:T(8,128)(2,1)S(1)}, bf16[2,256,1152]{2,1,0:T(8,128)(2,1)S(1)}, u32[]{:S(2)}, u32[]{:S(2)}) collective-permute-start(bf16[2,256,1152]{2,1,0:T(8,128)(2,1)S(1)} %get-tuple-element.51.whole), channel_id=1, source_target_pairs={{0,14},{1,3},{2,0},{3,5},{4,2},{5,7},{6,4},{7,9},{8,6},{9,11},{10,... | collective-permute-start | bytes 3538952 | tf_op jit(solution)/shard_map/ppermute | solution.py:27
  22.2 8.7 %collective-permute-start.10 = (bf16[4,48,1152]{2,1,0:T(8,128)(2,1)S(1)}, bf16[4,48,1152]{2,1,0:T(8,128)(2,1)S(1)}, u32[]{:S(2)}, u32[]{:S(2)}) collective-permute-start(bf16[4,48,1152]{2,1,0:T(8,128)(2,1)S(1)} %get-tuple-element.50), channel_id=1, source_target_pairs={{0,16},{1,65},{2,18},{3,67},{4,20},{5,69},{6,22},{7,71},{8,24},{9,... | collective-permute-start | bytes 1327112 | tf_op jit(solution)/shard_map/ppermute | solution.py:27
  23.5 8.7 %collective-permute-start.7 = (bf16[4,48,1152]{2,1,0:T(8,128)(2,1)S(1)}, bf16[4,48,1152]{2,1,0:T(8,128)(2,1)S(1)}, u32[]{:S(2)}, u32[]{:S(2)}) collective-permute-start(bf16[4,48,1152]{2,1,0:T(8,128)(2,1)S(1)} %get-tuple-element.47), channel_id=1, source_target_pairs={{0,192},{1,49},{2,194},{3,51},{4,196},{5,53},{6,198},{7,55},{8,200... | collective-permute-start | bytes 1327112 | tf_op jit(solution)/shard_map/ppermute | solution.py:27
  26.3 11.3 %collective-permute-start.8 = (bf16[4,48,1152]{2,1,0:T(8,128)(2,1)S(1)}, bf16[4,48,1152]{2,1,0:T(8,128)(2,1)S(1)}, u32[]{:S(2)}, u32[]{:S(2)}) collective-permute-start(bf16[4,48,1152]{2,1,0:T(8,128)(2,1)S(1)} %get-tuple-element.48), channel_id=1, source_target_pairs={{0,64},{1,17},{2,66},{3,19},{4,68},{5,21},{6,70},{7,23},{8,72},{9,... | collective-permute-start | bytes 1327112 | tf_op jit(solution)/shard_map/ppermute | solution.py:27
  26.3 12.0 %collective-permute-start.9 = (bf16[4,48,1152]{2,1,0:T(8,128)(2,1)S(1)}, bf16[4,48,1152]{2,1,0:T(8,128)(2,1)S(1)}, u32[]{:S(2)}, u32[]{:S(2)}) collective-permute-start(bf16[4,48,1152]{2,1,0:T(8,128)(2,1)S(1)} %get-tuple-element.49), channel_id=1, source_target_pairs={{0,48},{1,193},{2,50},{3,195},{4,52},{5,197},{6,54},{7,199},{8,56}... | collective-permute-start | bytes 1327112 | tf_op jit(solution)/shard_map/ppermute | solution.py:27
  27.7 1.7 %copy-start.1 = (bf16[144,9216]{1,0:T(8,128)(2,1)S(1)}, bf16[144,9216]{1,0:T(8,128)(2,1)}, u32[]{:S(2)}) copy-start(bf16[144,9216]{1,0:T(8,128)(2,1)} %u0.5) | copy-start | bytes 7962628
  29.5 8.8 %copy-start.2 = (bf16[144,9216]{1,0:T(8,128)(2,1)S(1)}, bf16[144,9216]{1,0:T(8,128)(2,1)}, u32[]{:S(2)}) copy-start(bf16[144,9216]{1,0:T(8,128)(2,1)} %u0.5) | copy-start | bytes 7962628
  40.0 6.6 %copy-start.3 = (bf16[1152,1152]{1,0:T(8,128)(2,1)S(1)}, bf16[1152,1152]{1,0:T(8,128)(2,1)}, u32[]{:S(2)}) copy-start(bf16[1152,1152]{1,0:T(8,128)(2,1)} %d0.3) | copy-start | bytes 7962628
  41.0 5.5 %collective-permute-start.13 = (bf16[288,256]{1,0:T(8,128)(2,1)S(1)}, bf16[288,256]{1,0:T(8,128)(2,1)S(1)}, u32[]{:S(2)}, u32[]{:S(2)}) collective-permute-start(bf16[288,256]{1,0:T(8,128)(2,1)S(1)} %gate_up_silu.1.h0), channel_id=1, source_target_pairs={{0,6},{1,7},{2,0},{3,1},{4,2},{5,3},{6,4},{7,5},{8,14},{9,15},{10,... | collective-permute-start | bytes 442376 | tf_op jit(solution)/shard_map/ppermute | solution.py:27
  42.4 13.0 %collective-permute-start.11 = (bf16[288,256]{1,0:T(8,128)(2,1)S(1)}, bf16[288,256]{1,0:T(8,128)(2,1)S(1)}, u32[]{:S(2)}, u32[]{:S(2)}) collective-permute-start(bf16[288,256]{1,0:T(8,128)(2,1)S(1)} %gate_up_silu.1.h0), channel_id=1, source_target_pairs={{0,4},{1,5},{2,6},{3,7},{4,0},{5,1},{6,2},{7,3},{8,12},{9,13},{10,... | collective-permute-start | bytes 442376 | tf_op jit(solution)/shard_map/ppermute | solution.py:27
  42.4 13.0 %collective-permute-start.12 = (bf16[288,256]{1,0:T(8,128)(2,1)S(1)}, bf16[288,256]{1,0:T(8,128)(2,1)S(1)}, u32[]{:S(2)}, u32[]{:S(2)}) collective-permute-start(bf16[288,256]{1,0:T(8,128)(2,1)S(1)} %gate_up_silu.1.h0), channel_id=1, source_target_pairs={{0,2},{1,3},{2,4},{3,5},{4,6},{5,7},{6,0},{7,1},{8,10},{9,11},{10,... | collective-permute-start | bytes 442376 | tf_op jit(solution)/shard_map/ppermute | solution.py:27
  56.6 7.5 %collective-permute-start.14 = (bf16[2,64,1152]{2,1,0:T(8,128)(2,1)S(1)}, bf16[2,64,1152]{2,1,0:T(8,128)(2,1)S(1)}, u32[]{:S(2)}, u32[]{:S(2)}) collective-permute-start(bf16[2,64,1152]{2,1,0:T(8,128)(2,1)S(1)} %get-tuple-element.54), channel_id=1, source_target_pairs={{0,128},{1,33},{2,130},{3,35},{4,132},{5,37},{6,134},{7,39},{8,136... | collective-permute-start | bytes 884744 | tf_op jit(solution)/shard_map/ppermute | solution.py:27
  58.7 8.6 %collective-permute-start.15 = (bf16[2,64,1152]{2,1,0:T(8,128)(2,1)S(1)}, bf16[2,64,1152]{2,1,0:T(8,128)(2,1)S(1)}, u32[]{:S(2)}, u32[]{:S(2)}) collective-permute-start(bf16[2,64,1152]{2,1,0:T(8,128)(2,1)S(1)} %get-tuple-element.55), channel_id=1, source_target_pairs={{0,64},{1,17},{2,66},{3,19},{4,68},{5,21},{6,70},{7,23},{8,72},{9,... | collective-permute-start | bytes 884744 | tf_op jit(solution)/shard_map/ppermute | solution.py:27
  59.7 7.6 %collective-permute-start.16 = (bf16[2,64,1152]{2,1,0:T(8,128)(2,1)S(1)}, bf16[2,64,1152]{2,1,0:T(8,128)(2,1)S(1)}, u32[]{:S(2)}, u32[]{:S(2)}) collective-permute-start(bf16[2,64,1152]{2,1,0:T(8,128)(2,1)S(1)} %get-tuple-element.56), channel_id=1, source_target_pairs={{0,192},{1,49},{2,194},{3,51},{4,196},{5,53},{6,198},{7,55},{8,200... | collective-permute-start | bytes 884744 | tf_op jit(solution)/shard_map/ppermute | solution.py:27
  67.5 4.8 %collective-permute-start.17 = (bf16[2,16,1152]{2,1,0:T(8,128)(2,1)S(1)}, bf16[2,16,1152]{2,1,0:T(8,128)(2,1)S(1)}, u32[]{:S(2)}, u32[]{:S(2)}) collective-permute-start(bf16[2,16,1152]{2,1,0:T(8,128)(2,1)S(1)} %get-tuple-element.58), channel_id=1, source_target_pairs={{0,32},{1,129},{2,34},{3,131},{4,36},{5,133},{6,38},{7,135},{8,40}... | collective-permute-start | bytes 221192 | tf_op jit(solution)/shard_map/ppermute | solution.py:27
  69.5 4.4 %collective-permute-start.18 = (bf16[2,16,1152]{2,1,0:T(8,128)(2,1)S(1)}, bf16[2,16,1152]{2,1,0:T(8,128)(2,1)S(1)}, u32[]{:S(2)}, u32[]{:S(2)}) collective-permute-start(bf16[2,16,1152]{2,1,0:T(8,128)(2,1)S(1)} %get-tuple-element.59), channel_id=1, source_target_pairs={{0,16},{1,65},{2,18},{3,67},{4,20},{5,69},{6,22},{7,71},{8,24},{9,... | collective-permute-start | bytes 221192 | tf_op jit(solution)/shard_map/ppermute | solution.py:27
  70.9 3.5 %collective-permute-start.19 = (bf16[2,16,1152]{2,1,0:T(8,128)(2,1)S(1)}, bf16[2,16,1152]{2,1,0:T(8,128)(2,1)S(1)}, u32[]{:S(2)}, u32[]{:S(2)}) collective-permute-start(bf16[2,16,1152]{2,1,0:T(8,128)(2,1)S(1)} %get-tuple-element.60), channel_id=1, source_target_pairs={{0,48},{1,193},{2,50},{3,195},{4,52},{5,197},{6,54},{7,199},{8,56}... | collective-permute-start | bytes 221192 | tf_op jit(solution)/shard_map/ppermute | solution.py:27
  74.5 6.8 %collective-permute-start.20 = (bf16[16,1152]{1,0:T(8,128)(2,1)S(1)}, bf16[16,1152]{1,0:T(8,128)(2,1)S(1)}, u32[]{:S(2)}, u32[]{:S(2)}) collective-permute-start(bf16[16,1152]{1,0:T(8,128)(2,1)S(1)} %get-tuple-element.62), channel_id=1, source_target_pairs={{0,8},{1,9},{2,10},{3,11},{4,12},{5,13},{6,14},{7,15},{8,0},{9,1},... | collective-permute-start | bytes 110600 | tf_op jit(solution)/shard_map/ppermute | solution.py:27
  81.3 5.6 %collective-permute-start.21 = (bf16[8,1152]{1,0:T(8,128)(2,1)S(1)}, bf16[8,1152]{1,0:T(8,128)(2,1)S(1)}, u32[]{:S(2)}, u32[]{:S(2)}) collective-permute-start(bf16[8,1152]{1,0:T(8,128)(2,1)S(1)} %convert), channel_id=1, source_target_pairs={{0,1},{1,0},{2,3},{3,2},{4,5},{5,4},{6,7},{7,6},{8,9},{9,8},{10,11... | collective-permute-start | bytes 55304 | tf_op jit(solution)/shard_map/ppermute | solution.py:27
